TPU v7x, 512 devices: a whole 4x8x8 slice. The times are simulated.
512 devices in a mesh: head: 16 (over y, core), req: 32 (over x, z).
Axes of the slice: x: 4, y: 8, z: 8, core: 2. Of those that a mesh axis runs over, the one named last changes fastest.
Arguments:
- tokens: bfloat16 [4, 96, 8192], P(None, 'head', 'req'), may hold values from -6 to 6
- gate_inner_weight: bfloat16 [8192, 2, 16384], P('req', None, 'head'), may hold values from -0.0625 to 0.0625
- step_weight: bfloat16 [8192, 256], P('req', 'head'), may hold values from -0.0625 to 0.0625
- bc_weight: bfloat16 [8192, 2048], P('req', 'head'), may hold values from -0.0625 to 0.0625
- conv_inner: bfloat16 [96, 3, 16384], P('req', None, 'head'), may hold values from -6 to 6
- conv_groups: bfloat16 [96, 3, 2048], P('req', None, 'head'), may hold values from -6 to 6
- inner_taps: float32 [4, 16384], P(None, 'head'), may hold values from -0.6 to 0.6
- inner_bias: float32 [16384], P('head'), may hold values from -0.5 to 0.5
- group_taps: float32 [4, 2048], P(None, 'head'), may hold values from -0.6 to 0.6
- group_bias: float32 [2048], P('head'), may hold values from -0.5 to 0.5
- step_bias: float32 [256], P('head'), may hold values from -3 to 0
- log_decay: float32 [256], P('head'), may hold values from -2 to 1.5
- skip_gain: float32 [256], P('head'), may hold values from 0.5 to 1.5
- norm_gain: float32 [16384], P('head'), may hold values from 0.5 to 1.5
- out_weight: bfloat16 [16384, 8192], P('head', 'req'), may hold values from -0.046875 to 0.046875
- ssm_state: float32 [96, 256, 64, 128], P('req', 'head'), may hold values from -6 to 6
Outputs:
- mixed: bfloat16 [4, 96, 8192], P(None, 'head', 'req')
- new_state: float32 [96, 256, 64, 128], P('req', 'head')
- new_conv_inner: bfloat16 [96, 3, 16384], P('req', None, 'head')
- new_conv_groups: bfloat16 [96, 3, 2048], P('req', None, 'head')
All inputs are finite; a program needn't handle non-finite values.
Results may differ from a plain program's by a relative error of at most 0.02.
Values may be sent and summed in bfloat16 or wider, within the bound.
No kernel may reach another device: no remote copies, remote signals or barrier semaphores. Data moves between devices by JAX's collectives and lax.ppermute only.
A program may use at most 64 MiB of HBM per device.

v0:
```python
import jax
import jax.numpy as jnp
from jax import lax
from jax.sharding import PartitionSpec as P

H = 256
G = 8


epsilon = 1e-05


def partner_2(block, axis, stride):
    count = lax.axis_size(axis)
    route = []
    for low in range(count):
        high = low | 1 << stride
        if high != low and high < count:
            route += [(low, high), (high, low)]
    return lax.ppermute(block, axis, route)


def conv_run(history, projected, taps, bias):
    step_count = projected.shape[0]
    sequence = jnp.concatenate([jnp.transpose(history, (1, 0, 2)), projected], axis=0)
    wide = sequence.astype(jnp.float32)
    summed = taps[0] * wide[0:step_count]
    for tap_num in range(1, taps.shape[0]):
        summed = summed + taps[tap_num] * wide[tap_num : tap_num + step_count]
    result = jax.nn.silu(summed + bias)
    kept = sequence[step_count:]
    return (result, jnp.transpose(kept, (1, 0, 2)))


def shards(
    tokens,
    gate_inner_weight,
    step_weight,
    bc_weight,
    conv_inner,
    conv_groups,
    inner_taps,
    inner_bias,
    group_taps,
    group_bias,
    step_bias,
    log_decay,
    skip_gain,
    norm_gain,
    out_weight,
    ssm_state,
):
    step_count = tokens.shape[0]
    rows_dev = ssm_state.shape[0]
    heads_dev = ssm_state.shape[1]
    head_size = ssm_state.shape[2]
    state_size = ssm_state.shape[3]
    width_dev = heads_dev * head_size
    feature_rows = gate_inner_weight.shape[0]
    heads_group = H // G
    gate_inner_flat = gate_inner_weight.reshape(feature_rows, 2 * width_dev)

    def project(token_block):
        part_rows = lax.all_gather(token_block, "head", axis=1, tiled=True)
        flat_rows = part_rows.reshape(part_rows.shape[0] * part_rows.shape[1], feature_rows)
        joined = jnp.concatenate(
            [
                jnp.dot(flat_rows, gate_inner_flat, preferred_element_type=jnp.float32),
                jnp.dot(flat_rows, step_weight, preferred_element_type=jnp.float32),
                jnp.dot(flat_rows, bc_weight, preferred_element_type=jnp.float32),
            ],
            axis=1,
        )
        partial_value = joined.reshape(part_rows.shape[0], part_rows.shape[1], joined.shape[1])
        return lax.psum_scatter(partial_value, "req", scatter_dimension=1, tiled=True)

    projected = jnp.concatenate(
        [project(tokens[step_num : step_num + 1]) for step_num in range(step_count)], axis=0
    )
    gate_proj = projected[..., :width_dev].astype(jnp.bfloat16)
    inner_proj = projected[..., width_dev : 2 * width_dev].astype(jnp.bfloat16)
    step_proj = projected[..., 2 * width_dev : 2 * width_dev + heads_dev].astype(jnp.bfloat16)
    bc_proj = projected[..., 2 * width_dev + heads_dev :].astype(jnp.bfloat16)
    x_conv, new_conv_inner = conv_run(conv_inner, inner_proj, inner_taps, inner_bias)
    bc_conv, new_conv_groups = conv_run(conv_groups, bc_proj, group_taps, group_bias)
    head_index = lax.axis_index("head")
    group_cols = bc_conv
    bit_num = 0
    partner = partner_2(group_cols, "head", bit_num)
    is_lower = head_index // 2**bit_num % 2 == 0
    group_cols = jnp.where(
        is_lower,
        jnp.concatenate([group_cols, partner], axis=2),
        jnp.concatenate([partner, group_cols], axis=2),
    )
    groups_dev = group_cols.shape[2] // (2 * state_size)
    group_split = group_cols.reshape(step_count, rows_dev, groups_dev, 2, state_size)
    heads_per = heads_dev // groups_dev
    b_heads = jnp.repeat(group_split[:, :, :, 0], heads_per, axis=2)
    c_heads = jnp.repeat(group_split[:, :, :, 1], heads_per, axis=2)
    step_size = jax.nn.softplus(step_proj.astype(jnp.float32) + step_bias)
    decay_rate = jnp.exp(-step_size * jnp.exp(log_decay))
    current = ssm_state
    emitted = []
    for step_num in range(step_count):
        x_step = x_conv[step_num].reshape(rows_dev, heads_dev, head_size)
        current = (
            decay_rate[step_num][:, :, None, None] * current
            + (step_size[step_num][:, :, None] * x_step)[..., None]
            * b_heads[step_num][:, :, None, :]
        )
        y_heads = (
            jnp.einsum("rhpn,rhn->rhp", current, c_heads[step_num], precision=lax.Precision.HIGHEST)
            + skip_gain[:, None] * x_step
        )
        gated_y = y_heads * jax.nn.silu(
            gate_proj[step_num].reshape(rows_dev, heads_dev, head_size).astype(jnp.float32)
        )
        grouped = gated_y.reshape(rows_dev, groups_dev, heads_per * head_size)
        squares = jnp.sum(grouped * grouped, axis=-1)
        bit_num = 0
        squares = squares + partner_2(squares, "head", bit_num)
        mean_sq = squares / (heads_group * head_size)
        normed = (
            (grouped * lax.rsqrt(mean_sq + epsilon)[..., None]).reshape(rows_dev, width_dev)
            * norm_gain
        ).astype(jnp.bfloat16)
        compute_part_rows = lax.all_gather(normed[None], "req", axis=1, tiled=True)
        compute_flat_rows = compute_part_rows.reshape(
            compute_part_rows.shape[0] * compute_part_rows.shape[1], width_dev
        )
        product = jnp.dot(compute_flat_rows, out_weight, preferred_element_type=jnp.float32)
        out_partial_value = product.reshape(
            compute_part_rows.shape[0], compute_part_rows.shape[1], product.shape[1]
        )
        emitted.append(
            lax.psum_scatter(
                out_partial_value.astype(jnp.bfloat16), "head", scatter_dimension=1, tiled=True
            )
        )
    mixed = jnp.concatenate(emitted, axis=0)
    return (mixed, current, new_conv_inner, new_conv_groups)


def solution(mesh):
    placed = (
        P(None, "head", "req"),
        P("req", None, "head"),
        P("req", "head"),
        P("req", "head"),
        P("req", None, "head"),
        P("req", None, "head"),
        P(None, "head"),
        P("head"),
        P(None, "head"),
        P("head"),
        P("head"),
        P("head"),
        P("head"),
        P("head"),
        P("head", "req"),
        P("req", "head", None, None),
    )
    return jax.shard_map(
        shards,
        mesh=mesh,
        in_specs=placed,
        out_specs=(
            P(None, "head", "req"),
            P("req", "head", None, None),
            P("req", None, "head"),
            P("req", None, "head"),
        ),
        check_vma=False,
    )
```

profile of v0, /device:TPU:1, one launch (start us, length us, event | category | flops | bytes accessed | tf_op | source)
XLA Modules:
  0.0 1013.2 jit_solution(15998328494383866659)
XLA Ops:
  1.5 21.1 %all_gather.24 = bf16[1,96,256]{2,0,1:T(2,128)(2,1)S(1)} all-gather(bf16[1,6,256]{2,0,1:T(2,128)(2,1)S(1)} %get-tuple-element.62), channel_id=1, replica_groups=mesh['head'=16,'req'=32] {'head'}, dimensions={1}, use_global_device_ids=true | all-gather | bytes 52224 | tf_op jit(solution)/shard_map/all_gather | solution.py:64
  24.7 16.4 %all_gather.25 = bf16[1,96,256]{2,0,1:T(2,128)(2,1)S(1)} all-gather(bf16[1,6,256]{2,0,1:T(2,128)(2,1)S(1)} %get-tuple-element.63), channel_id=1, replica_groups=mesh['head'=16,'req'=32] {'head'}, dimensions={1}, use_global_device_ids=true | all-gather | bytes 52224 | tf_op jit(solution)/shard_map/all_gather | solution.py:64
  42.6 14.7 %all_gather.26 = bf16[1,96,256]{2,0,1:T(2,128)(2,1)S(1)} all-gather(bf16[1,6,256]{2,0,1:T(2,128)(2,1)S(1)} %get-tuple-element.65), channel_id=1, replica_groups=mesh['head'=16,'req'=32] {'head'}, dimensions={1}, use_global_device_ids=true | all-gather | bytes 52224 | tf_op jit(solution)/shard_map/all_gather | solution.py:64
  58.8 16.1 %all_gather.27 = bf16[1,96,256]{2,0,1:T(2,128)(2,1)S(1)} all-gather(bf16[1,6,256]{2,0,1:T(2,128)(2,1)S(1)} %get-tuple-element.64), channel_id=1, replica_groups=mesh['head'=16,'req'=32] {'head'}, dimensions={1}, use_global_device_ids=true | all-gather | bytes 52224 | tf_op jit(solution)/shard_map/all_gather | solution.py:64
  85.8 3.0 copy.63
  90.9 616.8 %all-reduce.15 = (bf16[1,96,2192]{2,0,1:T(2,128)(2,1)}, bf16[1,96,2192]{2,0,1:T(2,128)(2,1)}, bf16[1,96,2192]{2,0,1:T(2,128)(2,1)}, bf16[1,96,2192]{2,0,1:T(2,128)(2,1)}) all-reduce(f32[1,96,2192]{2,0,1:T(1,128)} %copy.63, f32[1,96,2192]{2,0,1:T(1,128)S(1)} %copy.61, ...), channel_id=5, replica_groups=mesh['head'=16,'req'=32] {'req'}, use_global_device_ids=true, to_apply=%region_3.0.clone | all-reduce | flops 841728 | bytes 5050368
  709.6 3.7 collective-permute-start
  715.7 2.7 fusion.4
  718.4 3.5 fusion.16
  722.0 4.0 fusion.5
  729.2 2.5 fusion.85
  741.6 35.7 %all_gather.28 = bf16[1,96,1024]{2,0,1:T(2,128)(2,1)S(1)} all-gather(bf16[1,3,1024]{2,0,1:T(2,128)(2,1)S(1)} %copy.64), channel_id=1, replica_groups=mesh['head'=16,'req'=32] {'req'}, dimensions={1}, use_global_device_ids=true | all-gather | bytes 202752 | tf_op jit(solution)/shard_map/all_gather | solution.py:128
  777.3 36.5 %all_gather.29 = bf16[1,96,1024]{2,0,1:T(2,128)(2,1)S(1)} all-gather(bf16[1,3,1024]{2,0,1:T(2,128)(2,1)S(1)} %copy.65), channel_id=1, replica_groups=mesh['head'=16,'req'=32] {'req'}, dimensions={1}, use_global_device_ids=true | all-gather | bytes 202752 | tf_op jit(solution)/shard_map/all_gather | solution.py:128
  814.3 35.0 %all_gather.30 = bf16[1,96,1024]{2,0,1:T(2,128)(2,1)S(1)} all-gather(bf16[1,3,1024]{2,0,1:T(2,128)(2,1)S(1)} %copy.66), channel_id=1, replica_groups=mesh['head'=16,'req'=32] {'req'}, dimensions={1}, use_global_device_ids=true | all-gather | bytes 202752 | tf_op jit(solution)/shard_map/all_gather | solution.py:128
  849.5 36.3 %all_gather.31 = bf16[1,96,1024]{2,0,1:T(2,128)(2,1)S(1)} all-gather(bf16[1,3,1024]{2,0,1:T(2,128)(2,1)S(1)} %copy.67), channel_id=1, replica_groups=mesh['head'=16,'req'=32] {'req'}, dimensions={1}, use_global_device_ids=true | all-gather | bytes 202752 | tf_op jit(solution)/shard_map/all_gather | solution.py:128
  886.1 73.8 %fusion.79 = (bf16[8,256]{1,0:T(8,128)(2,1)S(1)}, bf16[8,256]{1,0:T(8,128)(2,1)S(1)}, bf16[8,256]{1,0:T(8,128)(2,1)S(1)}, bf16[8,256]{1,0:T(8,128)(2,1)S(1)}) fusion(bf16[1,96,256]{2,1,0:T(8,128)(2,1)S(1)} %fusion.9, bf16[1,96,256]{2,1,0:T(8,128)(2,1)S(1)} %fusion.8, bf16[1,96,256]{2,1,0:T(8,128)(2,1)S(1)} %fusion.7, bf16[1,96,256]{2,1,0:T(8,128)(2,1)S(1)} %fusion.6), kind=kCustom, calls=%all-reduce-scatter.4 | all-reduce-scatter fusion | flops 131073 | bytes 215040
  963.1 4.2 collective-permute-start.7
  967.4 4.7 collective-permute-start.8
  976.7 2.5 collective-permute-start.11
  983.3 2.6 collective-permute-start.12
  988.5 6.3 collective-permute-start.15
  996.7 3.1 collective-permute-start.16
  1002.5 6.0 collective-permute-start.19
  1008.5 2.8 collective-permute-start.20
  (172 shorter events, 56.2 us)
Async XLA Ops:
  0.6 813.2 %copy-start = (bf16[1024,256]{1,0:T(8,128)(2,1)S(1)}, bf16[1024,256]{1,0:T(8,128)(2,1)}, u32[]{:S(2)}) copy-start(bf16[1024,256]{1,0:T(8,128)(2,1)} %param.30) | copy-start | bytes 1572868
  90.8 623.3 %copy-start.5 = (bf16[3,3,1024]{2,1,0:T(4,128)(2,1)S(1)}, bf16[3,3,1024]{2,1,0:T(4,128)(2,1)}, u32[]{:S(2)}) copy-start(bf16[3,3,1024]{2,1,0:T(4,128)(2,1)} %param.20) | copy-start | bytes 55300
  90.9 623.3 %copy-start.7 = (f32[1024]{0:T(1024)S(1)}, f32[1024]{0:T(1024)}, u32[]{:S(2)}) copy-start(f32[1024]{0:T(1024)} %param.23) | copy-start | bytes 12292
  709.6 6.0 collective-permute-start
  732.0 9.0 collective-permute-start.4
  733.9 7.1 collective-permute-start.3
  736.3 4.7 collective-permute-start.2
  738.2 3.2 collective-permute-start.1
  959.9 19.2 %collective-permute-start.5 = (bf16[8,256]{1,0:T(8,128)(2,1)S(1)}, bf16[8,256]{1,0:T(8,128)(2,1)S(1)}, u32[]{:S(2)}, u32[]{:S(2)}) collective-permute-start(bf16[8,256]{1,0:T(8,128)(2,1)S(1)} %get-tuple-element.39), channel_id=1, source_target_pairs={{0,32},{32,64},{64,96},{96,128},{128,160},{160,192},{192,224},{224... | collective-permute-start | bytes 12296
  961.8 19.3 %collective-permute-start.6 = (bf16[8,256]{1,0:T(8,128)(2,1)S(1)}, bf16[8,256]{1,0:T(8,128)(2,1)S(1)}, u32[]{:S(2)}, u32[]{:S(2)}) collective-permute-start(bf16[8,256]{1,0:T(8,128)(2,1)S(1)} %get-tuple-element.39), channel_id=1, source_target_pairs={{0,64},{32,96},{64,128},{96,160},{128,192},{160,224},{192,256},{22... | collective-permute-start | bytes 12296
  963.1 20.1 %collective-permute-start.7 = (bf16[8,256]{1,0:T(8,128)(2,1)S(1)}, bf16[8,256]{1,0:T(8,128)(2,1)S(1)}, u32[]{:S(2)}, u32[]{:S(2)}) collective-permute-start(bf16[8,256]{1,0:T(8,128)(2,1)S(1)} %get-tuple-element.39), channel_id=1, source_target_pairs={{0,96},{32,128},{64,160},{96,192},{128,224},{160,256},{192,288},{2... | collective-permute-start | bytes 12296
  967.4 9.3 collective-permute-start.8
  974.7 13.7 %collective-permute-start.10 = (bf16[8,256]{1,0:T(8,128)(2,1)S(1)}, bf16[8,256]{1,0:T(8,128)(2,1)S(1)}, u32[]{:S(2)}, u32[]{:S(2)}) collective-permute-start(bf16[8,256]{1,0:T(8,128)(2,1)S(1)} %get-tuple-element.38), channel_id=1, source_target_pairs={{0,64},{32,96},{64,128},{96,160},{128,192},{160,224},{192,256},{22... | collective-permute-start | bytes 12296
  976.7 18.1 %collective-permute-start.11 = (bf16[8,256]{1,0:T(8,128)(2,1)S(1)}, bf16[8,256]{1,0:T(8,128)(2,1)S(1)}, u32[]{:S(2)}, u32[]{:S(2)}) collective-permute-start(bf16[8,256]{1,0:T(8,128)(2,1)S(1)} %get-tuple-element.38), channel_id=1, source_target_pairs={{0,96},{32,128},{64,160},{96,192},{128,224},{160,256},{192,288},{2... | collective-permute-start | bytes 12296
  979.2 17.6 %collective-permute-start.9 = (bf16[8,256]{1,0:T(8,128)(2,1)S(1)}, bf16[8,256]{1,0:T(8,128)(2,1)S(1)}, u32[]{:S(2)}, u32[]{:S(2)}) collective-permute-start(bf16[8,256]{1,0:T(8,128)(2,1)S(1)} %get-tuple-element.38), channel_id=1, source_target_pairs={{0,32},{32,64},{64,96},{96,128},{128,160},{160,192},{192,224},{224... | collective-permute-start | bytes 12296
  981.1 21.4 %collective-permute-start.13 = (bf16[8,256]{1,0:T(8,128)(2,1)S(1)}, bf16[8,256]{1,0:T(8,128)(2,1)S(1)}, u32[]{:S(2)}, u32[]{:S(2)}) collective-permute-start(bf16[8,256]{1,0:T(8,128)(2,1)S(1)} %get-tuple-element.37), channel_id=1, source_target_pairs={{0,32},{32,64},{64,96},{96,128},{128,160},{160,192},{192,224},{224... | collective-permute-start | bytes 12296
  983.3 3.4 collective-permute-start.12
  986.7 21.8 %collective-permute-start.14 = (bf16[8,256]{1,0:T(8,128)(2,1)S(1)}, bf16[8,256]{1,0:T(8,128)(2,1)S(1)}, u32[]{:S(2)}, u32[]{:S(2)}) collective-permute-start(bf16[8,256]{1,0:T(8,128)(2,1)S(1)} %get-tuple-element.37), channel_id=1, source_target_pairs={{0,64},{32,96},{64,128},{96,160},{128,192},{160,224},{192,256},{22... | collective-permute-start | bytes 12296
  988.5 22.9 %collective-permute-start.15 = (bf16[8,256]{1,0:T(8,128)(2,1)S(1)}, bf16[8,256]{1,0:T(8,128)(2,1)S(1)}, u32[]{:S(2)}, u32[]{:S(2)}) collective-permute-start(bf16[8,256]{1,0:T(8,128)(2,1)S(1)} %get-tuple-element.37), channel_id=1, source_target_pairs={{0,96},{32,128},{64,160},{96,192},{128,224},{160,256},{192,288},{2... | collective-permute-start | bytes 12296
  994.8 17.3 %collective-permute-start.17 = (bf16[8,256]{1,0:T(8,128)(2,1)S(1)}, bf16[8,256]{1,0:T(8,128)(2,1)S(1)}, u32[]{:S(2)}, u32[]{:S(2)}) collective-permute-start(bf16[8,256]{1,0:T(8,128)(2,1)S(1)} %get-tuple-element.36), channel_id=1, source_target_pairs={{0,32},{32,64},{64,96},{96,128},{128,160},{160,192},{192,224},{224... | collective-permute-start | bytes 12296
  996.7 3.9 collective-permute-start.16
  1000.6 11.5 %collective-permute-start.18 = (bf16[8,256]{1,0:T(8,128)(2,1)S(1)}, bf16[8,256]{1,0:T(8,128)(2,1)S(1)}, u32[]{:S(2)}, u32[]{:S(2)}) collective-permute-start(bf16[8,256]{1,0:T(8,128)(2,1)S(1)} %get-tuple-element.36), channel_id=1, source_target_pairs={{0,64},{32,96},{64,128},{96,160},{128,192},{160,224},{192,256},{22... | collective-permute-start | bytes 12296
  1002.5 9.6 collective-permute-start.19
  1008.5 3.6 collective-permute-start.20
  (12 other events, 3158.3 us)
where the time goes:
time: 1010 us
  blocking collectives  902 us (89%)
  starting transfers between devices  59.4 us (6%)
  local copies, waits for them, and re-layouts  24.6 us (2%)
  matrix products  18.6 us (2%)
    unnamed x2, blocking collectives  691 us
    all_gather x4, blocking collectives, shards(): compute_part_rows = lax.all_gather(normed[None], 'req', axis=1, tiled=True)  144 us
    all_gather x4, blocking collectives, project(): part_rows = lax.all_gather(token_block, 'head', axis=1, tiled=True)  68.3 us
    unnamed x16, starting transfers between devices  47.1 us
  transfers between devices with their start and end apart: 21, of which 4 were waited for; matrix products, arithmetic and copies ran while one was open for 1% of the time, Pallas kernels for 0%

commit v1 on v0

v1 whole, which is shorter than its diff:
```python
import functools

import jax
import jax.numpy as jnp
from jax import lax
from jax.experimental import pallas as pl
from jax.experimental.pallas import tpu as pltpu
from jax.sharding import Mesh
from jax.sharding import PartitionSpec as P

EPSILON = 1e-05
F32 = jnp.float32
BF16 = jnp.bfloat16
Y_SIZE, CORE_SIZE, X_SIZE, Z_SIZE = 8, 2, 4, 8
HEAD_AXES = ("y", "core")
REQ_AXES = ("x", "z")
VMEM_LIMIT = 40 * 1024 * 1024


def silu(value):
    return value / (1.0 + jnp.exp(-value))


def call(body, out_shape, scratch=(), cost=None):
    whole = pl.BlockSpec(memory_space=pltpu.VMEM)
    return pl.pallas_call(
        body,
        out_shape=out_shape,
        out_specs=jax.tree.map(lambda _: whole, out_shape),
        scratch_shapes=list(scratch),
        compiler_params=pltpu.CompilerParams(vmem_limit_bytes=VMEM_LIMIT),
        cost_estimate=cost,
    )


def fold_x(in_ref, out_ref, sums):
    parts, rows, width = in_ref.shape
    half = width // 2
    block = rows // Z_SIZE
    total = in_ref[0].astype(F32)
    for part in range(1, parts):
        total = total + in_ref[part].astype(F32)
    for z in range(Z_SIZE):
        for side in range(2):
            at = (2 * z + side) * block
            sums[at : at + block, :] = total[z * block : (z + 1) * block, side * half : (side + 1) * half]
    out_ref[...] = sums[...].astype(BF16)


def conv_steps(seq, taps, bias, steps):
    summed = taps[0:1, :] * seq[0:steps]
    for tap in range(1, taps.shape[0]):
        summed = summed + taps[tap : tap + 1, :] * seq[tap : tap + steps]
    return silu(summed + bias)


def fold_z(in_ref, hist_ref, taps_ref, bias_ref, proj_ref, bc_ref, kept_ref, seq):
    parts = in_ref.shape[0]
    requests, history, width = hist_ref.shape
    rows = in_ref.shape[1] // 2
    steps = rows // requests
    first = in_ref.shape[2] - width
    total = in_ref[0].astype(F32)
    for part in range(1, parts):
        total = total + in_ref[part].astype(F32)
    proj_ref[...] = total.astype(BF16).astype(F32)
    for req in range(requests):
        seq[0:history, :] = hist_ref[req].astype(F32)
        seq[history : history + steps, :] = proj_ref[req * steps : (req + 1) * steps, first:]
        bc_ref[req * steps : (req + 1) * steps, :] = conv_steps(seq, taps_ref[...], bias_ref[...], steps)
        kept_ref[req] = seq[steps : steps + history, :].astype(BF16)


def scan_steps(
    proj_ref,
    pair_ref,
    hist_ref,
    taps_ref,
    bias_ref,
    step_bias_ref,
    log_decay_ref,
    skip_ref,
    state_ref,
    gated_ref,
    squares_ref,
    new_state_ref,
    kept_ref,
    seq,
    spread,
    rank,
    base,
):
    requests, width, state_size = state_ref.shape
    heads = step_bias_ref.shape[1]
    history = hist_ref.shape[1]
    rows = gated_ref.shape[0]
    steps = rows // requests
    step = proj_ref[rows : 2 * rows, width : width + heads] + step_bias_ref[...]
    step_size = jnp.maximum(step, 0.0) + jnp.log1p(jnp.exp(-jnp.abs(step)))
    spread[0:rows, :] = step_size
    spread[rows : 2 * rows, :] = jnp.exp(-step_size * jnp.exp(log_decay_ref[...]))
    spread[2 * rows : 2 * rows + 1, :] = skip_ref[...]
    spread[2 * rows + 1 :, :] = jnp.zeros((spread.shape[0] - 2 * rows - 1, heads), F32)
    per_head = width // heads
    channel = lax.broadcasted_iota(jnp.int32, (heads, width), 1)
    low = lax.broadcasted_iota(jnp.int32, (heads, width), 0) * per_head
    owner = jnp.where((channel >= low) & (channel < low + per_head), 1.0, 0.0).astype(F32)
    wide = jnp.dot(spread[...], owner, precision=lax.Precision.HIGHEST, preferred_element_type=F32)
    skip = wide[2 * rows : 2 * rows + 1]
    for req in range(requests):
        start = req * steps
        seq[0:history, :] = hist_ref[req].astype(F32)
        seq[history : history + steps, :] = proj_ref[rows + start : rows + start + steps, 0:width]
        x_conv = conv_steps(seq, taps_ref[...], bias_ref[...], steps)
        kept_ref[req] = seq[steps : steps + history, :].astype(BF16)
        b_rows = pair_ref[0, start : start + steps, :]
        c_rows = pair_ref[1, start : start + steps, :]
        state = state_ref[req]
        c_high = c_rows.astype(BF16).astype(F32)
        rank[0:steps, 0:state_size] = c_high
        rank[steps : 2 * steps, 0:state_size] = c_rows - c_high
        rank[2 * steps :, 0:state_size] = jnp.zeros((rank.shape[0] - 2 * steps, state_size), F32)
        c_parts = rank[:, 0:state_size].astype(BF16)
        state_high = state.astype(BF16)
        state_low = (state - state_high.astype(F32)).astype(BF16)
        across = (((1,), (1,)), ((), ()))
        by_high = lax.dot_general(c_parts, state_high, across, preferred_element_type=F32)
        by_low = lax.dot_general(c_parts, state_low, across, preferred_element_type=F32)
        base[...] = by_high[0:steps] + by_high[steps : 2 * steps] + by_low[0:steps]
        taken = []
        fade = None
        for step_num in range(steps):
            row = start + step_num
            x_row = x_conv[step_num : step_num + 1]
            decay = wide[rows + row : rows + row + 1]
            fade = decay if fade is None else fade * decay
            taken = [(source, decay * value) for source, value in taken]
            taken.append((step_num, wide[row : row + 1] * x_row))
            y_row = fade * base[step_num : step_num + 1, :] + skip * x_row
            for source, value in taken:
                match = jnp.sum(
                    b_rows[source : source + 1] * c_rows[step_num : step_num + 1], axis=1, keepdims=True
                )
                y_row = y_row + match * value
            gated = y_row * silu(proj_ref[row : row + 1, 0:width])
            gated_ref[row : row + 1, :] = gated
            square = jnp.sum(gated * gated, axis=1, keepdims=True)
            squares_ref[row : row + 1, :] = jnp.broadcast_to(square, (1, squares_ref.shape[1]))
        b_high = b_rows.astype(BF16).astype(F32)
        b_low = b_rows - b_high
        ones = jnp.ones((steps, state_size), F32)
        zeros = jnp.zeros((steps, state_size), F32)
        rank[0:steps, 0:state_size] = b_high
        rank[steps : 2 * steps, 0:state_size] = b_high
        rank[2 * steps : 3 * steps, 0:state_size] = b_low
        rank[3 * steps :, 0:state_size] = zeros
        rank[0:steps, state_size:] = zeros
        rank[steps : 2 * steps, state_size:] = zeros
        rank[2 * steps : 3 * steps, state_size:] = zeros
        rank[3 * steps :, state_size:] = ones
        right = rank[...].astype(BF16)
        for source, value in taken:
            high = value.astype(BF16).astype(F32)
            seq[source : source + 1, :] = high
            seq[steps + source : steps + source + 1, :] = value - high
            seq[2 * steps + source : 2 * steps + source + 1, :] = high
        fade_high = fade.astype(BF16).astype(F32)
        fade_mid = (fade - fade_high).astype(BF16).astype(F32)
        seq[3 * steps : 3 * steps + 1, :] = fade_high
        seq[3 * steps + 1 : 3 * steps + 2, :] = fade_mid
        seq[3 * steps + 2 : 3 * steps + 3, :] = fade - fade_high - fade_mid
        seq[3 * steps + 3 :, :] = jnp.zeros((seq.shape[0] - 3 * steps - 3, width), F32)
        left = seq[...].astype(BF16)
        both = lax.dot_general(left, right, (((0,), (0,)), ((), ())), preferred_element_type=F32)
        new_state_ref[req] = both[:, state_size:] * state + both[:, 0:state_size]


def normalise(group_width, gated_ref, squares_ref, gain_ref, out_ref, rows_two):
    rows, width = gated_ref.shape
    half = width // 2
    mean = (squares_ref[0] + squares_ref[1])[:, 0:1] / group_width
    normed = gated_ref[...] * lax.rsqrt(mean + EPSILON) * gain_ref[...]
    rows_two[0:rows, :] = normed[:, 0:half]
    rows_two[rows : 2 * rows, :] = normed[:, half:]
    block = rows_two[...].astype(BF16)
    for copy in range(out_ref.shape[0]):
        out_ref[copy] = block


def project_out(in_ref, weight_ref, out_ref, first, second, sums):
    blocks, block_rows, half = in_ref.shape
    rows = block_rows // 2
    flat = in_ref[...].reshape(blocks * block_rows, half)
    first[...] = jnp.dot(flat, weight_ref[0:half, :], preferred_element_type=F32)
    second[...] = jnp.dot(flat, weight_ref[half:, :], preferred_element_type=F32)
    for block in range(blocks):
        at = block * block_rows
        sums[block * rows : (block + 1) * rows, :] = (
            first[at : at + rows, :] + second[at + rows : at + block_rows, :]
        )
    out_ref[...] = sums[...].astype(BF16)


def shards(
    tokens,
    gate_inner_weight,
    step_weight,
    bc_weight,
    conv_inner,
    conv_groups,
    inner_taps,
    inner_bias,
    group_taps,
    group_bias,
    step_bias,
    log_decay,
    skip_gain,
    norm_gain,
    out_weight,
    ssm_state,
):
    steps, rows_head, features = tokens.shape
    requests, heads, head_size, state_size = ssm_state.shape
    width = heads * head_size
    head_count = Y_SIZE * CORE_SIZE
    req_count = X_SIZE * Z_SIZE
    rows = steps * requests
    sds = jax.ShapeDtypeStruct

    with jax.named_scope("weights"):
        weights = jnp.concatenate(
            [
                gate_inner_weight[:, 0],
                bc_weight,
                gate_inner_weight[:, 1],
                step_weight,
                jnp.zeros((features, bc_weight.shape[1] - heads), BF16),
            ],
            axis=1,
        )
    columns = weights.shape[1]
    half = columns // 2

    with jax.named_scope("gather_tokens"):
        own = jnp.transpose(tokens, (1, 0, 2)).reshape(rows_head * steps, features)
        own = jnp.broadcast_to(own[None], (head_count,) + own.shape)
        gathered = lax.all_to_all(own, HEAD_AXES, 0, 0, tiled=True)
        gathered = gathered.reshape(req_count * rows, features)

    with jax.named_scope("project"):
        partial_proj = jnp.dot(gathered, weights, preferred_element_type=F32).astype(BF16)
        partial_proj = partial_proj.reshape(X_SIZE, Z_SIZE * rows, columns)
    with jax.named_scope("sum_x"):
        parts = lax.all_to_all(partial_proj, "x", 0, 0, tiled=True)
        folded = call(
            fold_x,
            sds((Z_SIZE * 2 * rows, half), BF16),
            [pltpu.VMEM((Z_SIZE * 2 * rows, half), F32)],
        )(parts)
    with jax.named_scope("sum_z"):
        parts = lax.all_to_all(folded.reshape(Z_SIZE, 2 * rows, half), "z", 0, 0, tiled=True)
        history = conv_groups.shape[1]
        proj, bc_conv, new_conv_groups = call(
            fold_z,
            (
                sds((2 * rows, half), F32),
                sds((rows, bc_weight.shape[1]), F32),
                sds(conv_groups.shape, BF16),
            ),
            [pltpu.VMEM((8, bc_weight.shape[1]), F32)],
        )(parts, conv_groups, group_taps, group_bias[None])
    with jax.named_scope("scan"):
        pair = lax.all_gather(bc_conv, "core", axis=0, tiled=False)
        gated, squares, new_state, new_conv_inner = call(
            scan_steps,
            (
                sds((rows, width), F32),
                sds((rows, 128), F32),
                sds((requests, width, state_size), F32),
                sds(conv_inner.shape, BF16),
            ),
            [
                pltpu.VMEM((4 * steps, width), F32),
                pltpu.VMEM((32, heads), F32),
                pltpu.VMEM((4 * steps, 2 * state_size), F32),
                pltpu.VMEM((steps, width), F32),
            ],
        )(
            proj,
            pair,
            conv_inner,
            inner_taps,
            inner_bias[None],
            step_bias[None],
            log_decay[None],
            skip_gain[None],
            ssm_state.reshape(requests, width, state_size),
        )
    with jax.named_scope("normalise"):
        squares_pair = lax.all_gather(squares, "core", axis=0, tiled=False)
        normed = call(
            functools.partial(normalise, CORE_SIZE * width),
            sds((req_count, 2 * rows, width // 2), BF16),
            [pltpu.VMEM((2 * rows, width // 2), F32)],
        )(gated, squares_pair, norm_gain[None])
    with jax.named_scope("gather_normed"):
        all_rows = lax.all_to_all(normed, REQ_AXES, 0, 0, tiled=True)
    with jax.named_scope("project_out"):
        out_columns = out_weight.shape[1]
        product = call(
            project_out,
            sds((req_count * rows, out_columns), BF16),
            [
                pltpu.VMEM((req_count * 2 * rows, out_columns), F32),
                pltpu.VMEM((req_count * 2 * rows, out_columns), F32),
                pltpu.VMEM((req_count * rows, out_columns), F32),
            ],
        )(all_rows, out_weight)
    with jax.named_scope("sum_head"):
        blocks = product.reshape(head_count, rows_head * steps, out_columns)
        blocks = lax.all_to_all(blocks, HEAD_AXES, 0, 0, tiled=True)
        mixed = jnp.sum(blocks.astype(F32), axis=0).astype(BF16)
        mixed = jnp.transpose(mixed.reshape(rows_head, steps, out_columns), (1, 0, 2))
    return (mixed, new_state.reshape(ssm_state.shape), new_conv_inner, new_conv_groups)


def solution(mesh):
    head, req = HEAD_AXES, REQ_AXES
    split = Mesh(
        mesh.devices.reshape(Y_SIZE, CORE_SIZE, X_SIZE, Z_SIZE), HEAD_AXES + REQ_AXES
    )
    placed = (
        P(None, head, req),
        P(req, None, head),
        P(req, head),
        P(req, head),
        P(req, None, head),
        P(req, None, head),
        P(None, head),
        P(head),
        P(None, head),
        P(head),
        P(head),
        P(head),
        P(head),
        P(head),
        P(head, req),
        P(req, head, None, None),
    )
    return jax.shard_map(
        shards,
        mesh=split,
        in_specs=placed,
        out_specs=(
            P(None, head, req),
            P(req, head, None, None),
            P(req, None, head),
            P(req, None, head),
        ),
        check_vma=False,
    )
```

time: 1010 us -> 123 us (0.12)
  blocking collectives: 902 us -> 94.3 us
  starting transfers between devices: 59.4 us -> 10.2 us
  matrix products: 18.6 us -> 0.63 us
  local copies, waits for them, and re-layouts: 24.6 us -> 7.25 us
    unnamed x2 -> x0, blocking collectives: 691 us -> none
    all_gather x8 -> x2, blocking collectives: 212 us -> 6.06 us  [the longest x1 4.12 us: shards(): pair = lax.all_gather(bc_conv, 'core', axis=0, tiled=False)]
    all_to_all x0 -> x4, blocking collectives: none -> 88.3 us  [the longest x1 25.3 us: shards(): parts = lax.all_to_all(partial_proj, 'x', 0, 0, tiled=True)]
    unnamed x16 -> x0, starting transfers between devices: 47.1 us -> none
    dot_general x20 -> x1, matrix products: 18.6 us -> 0.63 us  [shards(): jnp.dot(gathered, weights, preferred_element_type=F32).astype(BF16)]
    ppermute x5 -> x0, starting transfers between devices: 12.3 us -> none  [partner_2(): return lax.ppermute(block, axis, route)]
    all_to_all x0 -> x1, starting transfers between devices: none -> 10.2 us  [shards(): gathered = lax.all_to_all(own, HEAD_AXES, 0, 0, tiled=True)]
  transfers between devices with their start and end apart: 21 -> 1, of which waited for: 4 -> 1; matrix products, arithmetic and copies ran while one was open for 1% -> 4% of each run, Pallas kernels for 0% -> 0%
where the time goes in v1:
time: 123 us
  blocking collectives  94.3 us (77%)
  starting transfers between devices  10.2 us (8%)
  local copies, waits for them, and re-layouts  7.25 us (6%)
  waiting for transfers between devices  5.16 us (4%)
  Pallas kernels  4.44 us (4%)
    all_to_all x1, blocking collectives, shards(): parts = lax.all_to_all(partial_proj, 'x', 0, 0, tiled=True)  25.3 us
    all_to_all x1, blocking collectives, shards(): lax.all_to_all(folded.reshape(Z_SIZE, 2 * rows, half), 'z', 0, 0, tiled=T...  23.9 us
    all_to_all x1, blocking collectives, shards(): all_rows = lax.all_to_all(normed, REQ_AXES, 0, 0, tiled=True)  23.1 us
    all_to_all x1, blocking collectives, shards(): blocks = lax.all_to_all(blocks, HEAD_AXES, 0, 0, tiled=True)  16 us
    all_to_all x1, starting transfers between devices, shards(): gathered = lax.all_to_all(own, HEAD_AXES, 0, 0, tiled=True)  10.2 us
    all_to_all x1, waiting for transfers between devices, shards(): gathered = lax.all_to_all(own, HEAD_AXES, 0, 0, tiled=True)  5.16 us
    all_gather x1, blocking collectives, shards(): pair = lax.all_gather(bc_conv, 'core', axis=0, tiled=False)  4.12 us
    slice x1, local copies, waits for them, and re-layouts, shards(): gate_inner_weight[:, 1]  3.21 us
  transfers between devices with their start and end apart: 1, of which 1 were waited for; matrix products, arithmetic and copies ran while one was open for 4% of the time, Pallas kernels for 0%

profile of v1, /device:TPU:1, one launch (start us, length us, event | category | flops | bytes accessed | tf_op | source)
XLA Modules:
  0.0 122.9 jit_solution(558476527821427878)
XLA Ops:
  0.6 0.7 broadcast_in_dim.29
  1.3 0.7 broadcast_in_dim.30
  2.0 10.2 %all-to-all-start = ((bf16[16,24,256]{2,1,0:T(8,128)(2,1)}), bf16[16,24,256]{2,1,0:T(8,128)(2,1)S(1)}, u32[]{:S(2)}, u32[]{:S(2)}) async-start(bf16[16,24,256]{2,1,0:T(8,128)(2,1)} %broadcast_in_dim.30), calls=%async_computation | async-start | bytes 393216 | tf_op jit(solution)/shard_map/gather_tokens/all_to_all | solution.py:247
  12.2 3.2 %fusion = (bf16[256,1,1024]{2,1,0:T(2,128)(2,1)S(1)}, bf16[256,1,1024]{2,1,0:T(2,128)(2,1)S(1)}) fusion(bf16[256,2,1024]{2,1,0:T(2,128)(2,1)} %param.17), kind=kLoop, calls=%fused_computation.3 | loop fusion | bytes 2097152 | tf_op jit(solution)/shard_map/weights/slice | solution.py:235
  15.5 0.1 copy.27
  15.6 0.4 copy_bitcast_fusion
  16.0 0.4 copy-done.12
  16.4 1.0 concatenate.3
  17.4 5.2 %all-to-all-done = bf16[16,24,256]{2,1,0:T(8,128)(2,1)S(1)} async-done(((bf16[16,24,256]{2,1,0:T(8,128)(2,1)}), bf16[16,24,256]{2,1,0:T(8,128)(2,1)S(1)}, u32[]{:S(2)}, u32[]{:S(2)}) %all-to-all-start) | async-done | bytes 196640 | tf_op jit(solution)/shard_map/gather_tokens/all_to_all | solution.py:247
  22.6 0.6 convolution_convert_fusion
  23.2 25.3 %all_to_all.25.in_ref = bf16[4,96,2304]{2,1,0:T(8,128)(2,1)S(1)} all-to-all(bf16[4,96,2304]{2,1,0:T(8,128)(2,1)S(1)} %bitcast.35), channel_id=1, replica_groups=mesh['y'=8,'core'=2,'x'=4,'z'=8] {'x'}, dimensions={0} | all-to-all | bytes 3538944 | tf_op jit(solution)/shard_map/sum_x/all_to_all | solution.py:254
  48.6 0.0 copy-start.3
  48.6 0.0 copy-start.4
  48.7 0.4 sum_x.1
  49.1 23.9 %all_to_all.26.in_ref = bf16[8,24,1152]{2,1,0:T(8,128)(2,1)S(1)} all-to-all(bf16[8,24,1152]{2,1,0:T(8,128)(2,1)S(1)} %bitcast.24), channel_id=1, replica_groups=mesh['y'=8,'core'=2,'x'=4,'z'=8] {'z'}, dimensions={0} | all-to-all | bytes 884736 | tf_op jit(solution)/shard_map/sum_z/all_to_all | solution.py:261
  73.0 0.7 sum_z.1
  73.7 4.1 %all-gather.2.pair_ref = f32[2,12,128]{2,1,0:T(8,128)S(1)} all-gather(f32[1,12,128]{2,1,0:T(8,128)S(1)} %bitcast.28), channel_id=2, replica_groups=mesh['y'=8,'core'=2,'x'=4,'z'=8] {'core'}, dimensions={0}, use_global_device_ids=true | all-gather | bytes 18432 | tf_op jit(solution)/shard_map/scan/all_gather | solution.py:273
  77.8 2.5 %scan.1 = (f32[12,1024]{1,0:T(8,128)S(1)}, f32[12,128]{1,0:T(8,128)S(1)}, f32[3,1024,128]{2,1,0:T(8,128)}, bf16[3,3,1024]{2,1,0:T(4,128)(2,1)}) custom-call(f32[24,1152]{1,0:T(8,128)S(1)} %get-tuple-element.11.proj_ref, f32[2,12,128]{2,1,0:T(8,128)S(1)} %all-gather.2.pair_ref, bf16[3,3,1024]{2,1,0:T(4,128)(2,1)S(1)} %copy-done.2, f32[4,1024]{1,0:T(4,128)S(1)} %copy-done.3, ...), custom_call_target="tpu_custom_call" | custom-call | tf_op jit(solution)/shard_map/scan/pallas_call | solution.py:274
  80.4 1.9 %all-gather.3.squares_ref = f32[2,12,128]{2,1,0:T(8,128)S(1)} all-gather(f32[1,12,128]{2,1,0:T(8,128)S(1)} %bitcast.27), channel_id=3, replica_groups=mesh['y'=8,'core'=2,'x'=4,'z'=8] {'core'}, dimensions={0}, use_global_device_ids=true | all-gather | bytes 18432 | tf_op jit(solution)/shard_map/normalise/all_gather | solution.py:300
  82.3 0.1 normalise.1
  82.4 23.1 %all_to_all.27.in_ref = bf16[32,24,512]{2,1,0:T(8,128)(2,1)S(1)} all-to-all(bf16[32,24,512]{2,1,0:T(8,128)(2,1)S(1)} %normalise.1), channel_id=1, replica_groups=mesh['y'=8,'core'=2,'x'=4,'z'=8] {'x','z'}, dimensions={0} | all-to-all | bytes 1572864 | tf_op jit(solution)/shard_map/gather_normed/all_to_all | solution.py:307
  105.5 0.7 project_out.1
  106.2 16.0 %all_to_all.28 = bf16[16,24,256]{2,1,0:T(8,128)(2,1)S(1)} all-to-all(bf16[16,24,256]{2,1,0:T(8,128)(2,1)S(1)} %bitcast.26), channel_id=1, replica_groups=mesh['y'=8,'core'=2,'x'=4,'z'=8] {'y','core'}, dimensions={0} | all-to-all | bytes 393216 | tf_op jit(solution)/shard_map/sum_head/all_to_all | solution.py:321
  122.2 0.6 reshape.36
  (27 shorter events, 0.1 us)
Async XLA Ops:
  2.0 20.6 %all-to-all-start = ((bf16[16,24,256]{2,1,0:T(8,128)(2,1)}), bf16[16,24,256]{2,1,0:T(8,128)(2,1)S(1)}, u32[]{:S(2)}, u32[]{:S(2)}) async-start(bf16[16,24,256]{2,1,0:T(8,128)(2,1)} %broadcast_in_dim.30), calls=%async_computation | async-start | bytes 393216 | tf_op jit(solution)/shard_map/gather_tokens/all_to_all | solution.py:247
  12.2 3.2 %copy-start.13 = (bf16[256,16]{0,1:T(8,128)(2,1)S(1)}, bf16[256,16]{0,1:T(8,128)(2,1)}, u32[]{:S(2)}) copy-start(bf16[256,16]{0,1:T(8,128)(2,1)} %param.18) | copy-start | bytes 24580
  15.6 0.8 copy-start.12
  48.6 24.4 %copy-start.6 = (bf16[3,3,128]{2,1,0:T(4,128)(2,1)S(1)}, bf16[3,3,128]{2,1,0:T(4,128)(2,1)}, u32[]{:S(2)}) copy-start(bf16[3,3,128]{2,1,0:T(4,128)(2,1)} %hist_ref.2) | copy-start | bytes 6916
  48.6 24.4 %copy-start.7 = (f32[4,128]{1,0:T(4,128)S(1)}, f32[4,128]{1,0:T(4,128)}, u32[]{:S(2)}) copy-start(f32[4,128]{1,0:T(4,128)} %taps_ref.2) | copy-start | bytes 6148
  48.6 24.4 %copy-start.11 = (f32[128]{0:T(128)S(1)}, f32[128]{0:T(128)}, u32[]{:S(2)}) copy-start(f32[128]{0:T(128)} %param.25) | copy-start | bytes 1540
  48.6 29.2 %copy-start = (f32[3,16,64,128]{3,2,1,0:T(8,128)S(1)}, f32[3,16,64,128]{3,2,1,0:T(8,128)}, u32[]{:S(2)}) copy-start(f32[3,16,64,128]{3,2,1,0:T(8,128)} %param.31) | copy-start | bytes 4718596
  48.6 29.2 %copy-start.2 = (bf16[3,3,1024]{2,1,0:T(4,128)(2,1)S(1)}, bf16[3,3,1024]{2,1,0:T(4,128)(2,1)}, u32[]{:S(2)}) copy-start(bf16[3,3,1024]{2,1,0:T(4,128)(2,1)} %hist_ref.3) | copy-start | bytes 55300
  48.6 29.2 %copy-start.3 = (f32[4,1024]{1,0:T(4,128)S(1)}, f32[4,1024]{1,0:T(4,128)}, u32[]{:S(2)}) copy-start(f32[4,1024]{1,0:T(4,128)} %taps_ref.3) | copy-start | bytes 49156
  48.6 29.2 %copy-start.4 = (f32[1024]{0:T(1024)S(1)}, f32[1024]{0:T(1024)}, u32[]{:S(2)}) copy-start(f32[1024]{0:T(1024)} %param.23) | copy-start | bytes 12292
  48.6 29.2 %copy-start.8 = (f32[16]{0:T(128)S(1)}, f32[16]{0:T(128)}, u32[]{:S(2)}) copy-start(f32[16]{0:T(128)} %param.26) | copy-start | bytes 196
  48.6 29.2 %copy-start.9 = (f32[16]{0:T(128)S(1)}, f32[16]{0:T(128)}, u32[]{:S(2)}) copy-start(f32[16]{0:T(128)} %param.27) | copy-start | bytes 196
  48.6 29.2 %copy-start.10 = (f32[16]{0:T(128)S(1)}, f32[16]{0:T(128)}, u32[]{:S(2)}) copy-start(f32[16]{0:T(128)} %param.28) | copy-start | bytes 196
  49.1 33.2 %copy-start.5 = (f32[1024]{0:T(1024)S(1)}, f32[1024]{0:T(1024)}, u32[]{:S(2)}) copy-start(f32[1024]{0:T(1024)} %param.29) | copy-start | bytes 12292
  80.4 25.2 %copy-start.1 = (bf16[1024,256]{1,0:T(8,128)(2,1)S(1)}, bf16[1024,256]{1,0:T(8,128)(2,1)}, u32[]{:S(2)}) copy-start(bf16[1024,256]{1,0:T(8,128)(2,1)} %weight_ref.1) | copy-start | bytes 1572868

commit v2 on v1

--- a/solution.py
+++ b/solution.py
@@ -33,18 +33,36 @@
     )
 
 
-def fold_x(in_ref, out_ref, sums):
-    parts, rows, width = in_ref.shape
-    half = width // 2
-    block = rows // Z_SIZE
-    total = in_ref[0].astype(F32)
-    for part in range(1, parts):
-        total = total + in_ref[part].astype(F32)
-    for z in range(Z_SIZE):
-        for side in range(2):
-            at = (2 * z + side) * block
-            sums[at : at + block, :] = total[z * block : (z + 1) * block, side * half : (side + 1) * half]
-    out_ref[...] = sums[...].astype(BF16)
+def project(
+    x_ref, rows_ref, own_ref, first_ref, second_ref, third_ref, extra_ref, out_ref, messages
+):
+    cores, per_core, block_rows, features = rows_ref.shape
+    y_count = per_core // X_SIZE
+    rows = block_rows // 2
+    lanes = out_ref.shape[1]
+    tiles = out_ref.shape[0] // (X_SIZE * Z_SIZE * rows)
+    here = x_ref[0]
+    for core in range(cores):
+        total = None
+        for shift, weight_ref in enumerate((own_ref, first_ref, second_ref, third_ref)):
+            source = lax.rem(here - shift + X_SIZE, X_SIZE)
+            block = rows_ref[core, pl.ds(source * y_count, y_count)]
+            block = block.reshape(y_count * block_rows, features)
+            part = jnp.dot(block, weight_ref[...], preferred_element_type=F32)
+            total = part if total is None else total + part
+            if shift == 0:
+                extra = jnp.dot(block, extra_ref[...], preferred_element_type=F32)
+        for y in range(y_count):
+            for side in range(2):
+                target = 2 * (y * cores + core) + side
+                at = y * block_rows + side * rows
+                for tile in range(tiles):
+                    value, column = total, tile * lanes
+                    if column >= total.shape[1]:
+                        value, column = extra, column - total.shape[1]
+                    to = (target * tiles + tile) * rows
+                    messages[to : to + rows, :] = value[at : at + rows, column : column + lanes]
+    out_ref[...] = messages[...].astype(BF16)
 
 
 def conv_steps(seq, taps, bias, steps):
@@ -54,25 +72,40 @@
     return silu(summed + bias)
 
 
-def fold_z(in_ref, hist_ref, taps_ref, bias_ref, proj_ref, bc_ref, kept_ref, seq):
-    parts = in_ref.shape[0]
-    requests, history, width = hist_ref.shape
-    rows = in_ref.shape[1] // 2
+def fold(
+    in_ref, hist_ref, taps_ref, bias_ref, gate_ref, inner_ref, step_ref, bc_ref, kept_ref, seq
+):
+    requests, history, lanes = hist_ref.shape
+    rows = gate_ref.shape[0]
     steps = rows // requests
-    first = in_ref.shape[2] - width
-    total = in_ref[0].astype(F32)
-    for part in range(1, parts):
-        total = total + in_ref[part].astype(F32)
-    proj_ref[...] = total.astype(BF16).astype(F32)
+    chunk = gate_ref.shape[1] // X_SIZE
+    tiles = chunk // lanes
+    extra = None
+    for x in range(X_SIZE):
+        total = in_ref[x * Z_SIZE].astype(F32)
+        for z in range(1, Z_SIZE):
+            total = total + in_ref[x * Z_SIZE + z].astype(F32)
+        rounded = total.astype(BF16).astype(F32)
+        for tile in range(tiles):
+            column = x * chunk + tile * lanes
+            gate_ref[:, column : column + lanes] = rounded[tile * rows : (tile + 1) * rows]
+            at = (tiles + tile) * rows
+            inner_ref[:, column : column + lanes] = rounded[at : at + rows]
+        part = total[2 * tiles * rows :]
+        extra = part if extra is None else extra + part
+    extra = extra.astype(BF16).astype(F32)
+    step_ref[...] = extra[rows : 2 * rows]
     for req in range(requests):
         seq[0:history, :] = hist_ref[req].astype(F32)
-        seq[history : history + steps, :] = proj_ref[req * steps : (req + 1) * steps, first:]
+        seq[history : history + steps, :] = extra[req * steps : (req + 1) * steps]
         bc_ref[req * steps : (req + 1) * steps, :] = conv_steps(seq, taps_ref[...], bias_ref[...], steps)
         kept_ref[req] = seq[steps : steps + history, :].astype(BF16)
 
 
 def scan_steps(
-    proj_ref,
+    gate_ref,
+    inner_ref,
+    step_ref,
     pair_ref,
     hist_ref,
     taps_ref,
@@ -95,7 +128,7 @@
     history = hist_ref.shape[1]
     rows = gated_ref.shape[0]
     steps = rows // requests
-    step = proj_ref[rows : 2 * rows, width : width + heads] + step_bias_ref[...]
+    step = step_ref[:, 0:heads] + step_bias_ref[...]
     step_size = jnp.maximum(step, 0.0) + jnp.log1p(jnp.exp(-jnp.abs(step)))
     spread[0:rows, :] = step_size
     spread[rows : 2 * rows, :] = jnp.exp(-step_size * jnp.exp(log_decay_ref[...]))
@@ -110,7 +143,7 @@
     for req in range(requests):
         start = req * steps
         seq[0:history, :] = hist_ref[req].astype(F32)
-        seq[history : history + steps, :] = proj_ref[rows + start : rows + start + steps, 0:width]
+        seq[history : history + steps, :] = inner_ref[start : start + steps, :]
         x_conv = conv_steps(seq, taps_ref[...], bias_ref[...], steps)
         kept_ref[req] = seq[steps : steps + history, :].astype(BF16)
         b_rows = pair_ref[0, start : start + steps, :]
@@ -142,7 +175,7 @@
                     b_rows[source : source + 1] * c_rows[step_num : step_num + 1], axis=1, keepdims=True
                 )
                 y_row = y_row + match * value
-            gated = y_row * silu(proj_ref[row : row + 1, 0:width])
+            gated = y_row * silu(gate_ref[row : row + 1, :])
             gated_ref[row : row + 1, :] = gated
             square = jnp.sum(gated * gated, axis=1, keepdims=True)
             squares_ref[row : row + 1, :] = jnp.broadcast_to(square, (1, squares_ref.shape[1]))
@@ -227,47 +260,56 @@
     rows = steps * requests
     sds = jax.ShapeDtypeStruct
 
-    with jax.named_scope("weights"):
-        weights = jnp.concatenate(
-            [
-                gate_inner_weight[:, 0],
-                bc_weight,
-                gate_inner_weight[:, 1],
-                step_weight,
-                jnp.zeros((features, bc_weight.shape[1] - heads), BF16),
-            ],
-            axis=1,
+    lanes = bc_weight.shape[1]
+    chunk = width // X_SIZE
+    with jax.named_scope("move_weights"):
+        here = lax.axis_index("x")
+        chunks = []
+        for shift in range(X_SIZE):
+            target = lax.rem(here + shift, X_SIZE)
+            part = lax.dynamic_slice(
+                gate_inner_weight, (0, 0, target * chunk), (features, 2, chunk)
+            )
+            if shift:
+                route = [(x, (x + shift) % X_SIZE) for x in range(X_SIZE)]
+                part = lax.ppermute(part, "x", route)
+            chunks.append(part.reshape(features, 2 * chunk))
+        extra = jnp.concatenate(
+            [bc_weight, step_weight, jnp.zeros((features, lanes - heads), BF16)], axis=1
         )
-    columns = weights.shape[1]
-    half = columns // 2
 
     with jax.named_scope("gather_tokens"):
         own = jnp.transpose(tokens, (1, 0, 2)).reshape(rows_head * steps, features)
-        own = jnp.broadcast_to(own[None], (head_count,) + own.shape)
-        gathered = lax.all_to_all(own, HEAD_AXES, 0, 0, tiled=True)
-        gathered = gathered.reshape(req_count * rows, features)
+        own = jnp.broadcast_to(own[None], (X_SIZE * Y_SIZE,) + own.shape)
+        gathered = lax.all_to_all(own, ("x", "y"), 0, 0, tiled=True)
+        gathered = lax.all_gather(gathered, "core", axis=0, tiled=False)
 
     with jax.named_scope("project"):
-        partial_proj = jnp.dot(gathered, weights, preferred_element_type=F32).astype(BF16)
-        partial_proj = partial_proj.reshape(X_SIZE, Z_SIZE * rows, columns)
-    with jax.named_scope("sum_x"):
-        parts = lax.all_to_all(partial_proj, "x", 0, 0, tiled=True)
-        folded = call(
-            fold_x,
-            sds((Z_SIZE * 2 * rows, half), BF16),
-            [pltpu.VMEM((Z_SIZE * 2 * rows, half), F32)],
-        )(parts)
-    with jax.named_scope("sum_z"):
-        parts = lax.all_to_all(folded.reshape(Z_SIZE, 2 * rows, half), "z", 0, 0, tiled=True)
-        history = conv_groups.shape[1]
-        proj, bc_conv, new_conv_groups = call(
-            fold_z,
+        tiles = 2 * chunk // lanes + 2
+        message_rows = req_count * tiles * rows
+        whole = pl.BlockSpec(memory_space=pltpu.VMEM)
+        messages = pl.pallas_call(
+            project,
+            out_shape=sds((message_rows, lanes), BF16),
+            in_specs=[pl.BlockSpec(memory_space=pltpu.SMEM)] + [whole] * 6,
+            out_specs=whole,
+            scratch_shapes=[pltpu.VMEM((message_rows, lanes), F32)],
+            compiler_params=pltpu.CompilerParams(vmem_limit_bytes=VMEM_LIMIT),
+        )(here.astype(jnp.int32).reshape(1), gathered, *chunks, extra)
+    with jax.named_scope("sum_req"):
+        parts = lax.all_to_all(
+            messages.reshape(req_count, tiles * rows, lanes), REQ_AXES, 0, 0, tiled=True
+        )
+        gate, inner, step, bc_conv, new_conv_groups = call(
+            fold,
             (
-                sds((2 * rows, half), F32),
-                sds((rows, bc_weight.shape[1]), F32),
+                sds((rows, width), F32),
+                sds((rows, width), F32),
+                sds((rows, lanes), F32),
+                sds((rows, lanes), F32),
                 sds(conv_groups.shape, BF16),
             ),
-            [pltpu.VMEM((8, bc_weight.shape[1]), F32)],
+            [pltpu.VMEM((8, lanes), F32)],
         )(parts, conv_groups, group_taps, group_bias[None])
     with jax.named_scope("scan"):
         pair = lax.all_gather(bc_conv, "core", axis=0, tiled=False)
@@ -286,7 +328,9 @@
                 pltpu.VMEM((steps, width), F32),
             ],
         )(
-            proj,
+            gate,
+            inner,
+            step,
             pair,
             conv_inner,
             inner_taps,

time: 123 us -> 122 us (level)
  blocking collectives: 94.3 us -> 81.3 us
  starting transfers between devices: 10.2 us -> 20.6 us
  waiting for transfers between devices: 5.16 us -> 11 us
  local copies, waits for them, and re-layouts: 7.25 us -> 3.32 us
    all_to_all x2 -> x1, blocking collectives: 49.2 us -> 25.5 us  [shards(): lax.all_to_all(messages.reshape(req_count, tiles * rows, lanes), REQ_AXES...]
    ppermute x0 -> x3, waiting for transfers between devices: none -> 11 us  [shards(): part = lax.ppermute(part, 'x', route)]
    ppermute x0 -> x3, starting transfers between devices: none -> 9.93 us  [shards(): part = lax.ppermute(part, 'x', route)]
    all_to_all x1, waiting for transfers between devices: 5.16 us -> 0.01 us  [shards(): gathered = lax.all_to_all(own, ('x', 'y'), 0, 0, tiled=True)]
    all_to_all x1, blocking collectives: 16 us -> 20.6 us  [shards(): blocks = lax.all_to_all(blocks, HEAD_AXES, 0, 0, tiled=True)]
    all_gather x0 -> x1, blocking collectives: none -> 3.93 us  [shards(): gathered = lax.all_gather(gathered, 'core', axis=0, tiled=False)]
    slice x1 -> x0, local copies, waits for them, and re-layouts: 3.21 us -> none  [shards(): gate_inner_weight[:, 1]]
  transfers between devices with their start and end apart: 1 -> 4, of which waited for: 1 -> 3; matrix products, arithmetic and copies ran while one was open for 4% -> 1% of each run, Pallas kernels for 0% -> 0%
where the time goes in v2:
time: 122 us
  blocking collectives  81.3 us (67%)
  starting transfers between devices  20.6 us (17%)
  waiting for transfers between devices  11 us (9%)
  Pallas kernels  4.75 us (4%)
  local copies, waits for them, and re-layouts  3.32 us (3%)
    all_to_all x1, blocking collectives, shards(): lax.all_to_all(messages.reshape(req_count, tiles * rows, lanes), REQ_AXES...  25.5 us
    all_to_all x1, blocking collectives, shards(): all_rows = lax.all_to_all(normed, REQ_AXES, 0, 0, tiled=True)  24.2 us
    all_to_all x1, blocking collectives, shards(): blocks = lax.all_to_all(blocks, HEAD_AXES, 0, 0, tiled=True)  20.6 us
    ppermute x3, waiting for transfers between devices, shards(): part = lax.ppermute(part, 'x', route)  11 us
    all_to_all x1, starting transfers between devices, shards(): gathered = lax.all_to_all(own, ('x', 'y'), 0, 0, tiled=True)  10.6 us
    ppermute x3, starting transfers between devices, shards(): part = lax.ppermute(part, 'x', route)  9.93 us
    all_gather x1, blocking collectives, shards(): pair = lax.all_gather(bc_conv, 'core', axis=0, tiled=False)  5.21 us
    all_gather x1, blocking collectives, shards(): gathered = lax.all_gather(gathered, 'core', axis=0, tiled=False)  3.93 us
  transfers between devices with their start and end apart: 4, of which 3 were waited for; matrix products, arithmetic and copies ran while one was open for 1% of the time, Pallas kernels for 0%

profile of v2, /device:TPU:1, one launch (start us, length us, event | category | flops | bytes accessed | tf_op | source)
XLA Modules:
  0.0 121.9 jit_solution(1979076678118538329)
XLA Ops:
  0.6 0.8 broadcast_in_dim.28
  1.4 0.8 broadcast_in_dim.29
  2.2 10.6 %all-to-all-start = ((bf16[32,24,256]{2,1,0:T(8,128)(2,1)}), bf16[32,24,256]{2,1,0:T(8,128)(2,1)S(1)}, u32[]{:S(2)}, u32[]{:S(2)}) async-start(bf16[32,24,256]{2,1,0:T(8,128)(2,1)} %broadcast_in_dim.29), calls=%async_computation | async-start | bytes 786432 | tf_op jit(solution)/shard_map/gather_tokens/all_to_all | solution.py:284
  12.9 0.7 constant_dynamic-slice_fusion
  13.6 4.4 %collective-permute-start.2 = (bf16[256,2,256]{2,1,0:T(2,128)(2,1)S(1)}, bf16[256,2,256]{2,1,0:T(2,128)(2,1)S(1)}, u32[]{:S(2)}, u32[]{:S(2)}) collective-permute-start(bf16[256,2,256]{2,1,0:T(2,128)(2,1)S(1)} %get-tuple-element.22), channel_id=1, source_target_pairs={{0,24},{8,0},{16,8},{24,16},{1,25},{9,1},{17,9},{25,17},{2,26},{10... | collective-permute-start | bytes 786440 | tf_op jit(solution)/shard_map/move_weights/ppermute | solution.py:275
  18.0 1.9 %collective-permute-start = (bf16[256,2,256]{2,1,0:T(2,128)(2,1)S(1)}, bf16[256,2,256]{2,1,0:T(2,128)(2,1)S(1)}, u32[]{:S(2)}, u32[]{:S(2)}) collective-permute-start(bf16[256,2,256]{2,1,0:T(2,128)(2,1)S(1)} %get-tuple-element.23), channel_id=1, source_target_pairs={{0,8},{8,16},{16,24},{24,0},{1,9},{9,17},{17,25},{25,1},{2,10},{10... | collective-permute-start | bytes 786440 | tf_op jit(solution)/shard_map/move_weights/ppermute | solution.py:275
  20.0 3.6 %collective-permute-start.1 = (bf16[256,2,256]{2,1,0:T(2,128)(2,1)S(1)}, bf16[256,2,256]{2,1,0:T(2,128)(2,1)S(1)}, u32[]{:S(2)}, u32[]{:S(2)}) collective-permute-start(bf16[256,2,256]{2,1,0:T(2,128)(2,1)S(1)} %get-tuple-element.25), channel_id=1, source_target_pairs={{0,16},{8,24},{16,0},{24,8},{1,17},{9,25},{17,1},{25,9},{2,18},{10... | collective-permute-start | bytes 786440 | tf_op jit(solution)/shard_map/move_weights/ppermute | solution.py:275
  23.6 0.1 copy.21
  23.8 0.1 pad.2.clone
  23.9 1.9 %collective-permute-done.2 = bf16[256,2,256]{2,1,0:T(2,128)(2,1)S(1)} collective-permute-done((bf16[256,2,256]{2,1,0:T(2,128)(2,1)S(1)}, bf16[256,2,256]{2,1,0:T(2,128)(2,1)S(1)}, u32[]{:S(2)}, u32[]{:S(2)}) %collective-permute-start.2) | collective-permute-done | bytes 262176 | tf_op jit(solution)/shard_map/move_weights/ppermute | solution.py:275
  25.9 3.9 %collective-permute-done = bf16[256,2,256]{2,1,0:T(2,128)(2,1)S(1)} collective-permute-done((bf16[256,2,256]{2,1,0:T(2,128)(2,1)S(1)}, bf16[256,2,256]{2,1,0:T(2,128)(2,1)S(1)}, u32[]{:S(2)}, u32[]{:S(2)}) %collective-permute-start) | collective-permute-done | bytes 262176 | tf_op jit(solution)/shard_map/move_weights/ppermute | solution.py:275
  29.8 5.2 %collective-permute-done.1 = bf16[256,2,256]{2,1,0:T(2,128)(2,1)S(1)} collective-permute-done((bf16[256,2,256]{2,1,0:T(2,128)(2,1)S(1)}, bf16[256,2,256]{2,1,0:T(2,128)(2,1)S(1)}, u32[]{:S(2)}, u32[]{:S(2)}) %collective-permute-start.1) | collective-permute-done | bytes 262176 | tf_op jit(solution)/shard_map/move_weights/ppermute | solution.py:275
  35.0 3.9 %all-gather = bf16[64,24,256]{2,1,0:T(8,128)(2,1)S(1)} all-gather(bf16[32,24,256]{2,1,0:T(8,128)(2,1)S(1)} %all-to-all-done), channel_id=2, replica_groups=mesh['y'=8,'core'=2,'x'=4,'z'=8] {'core'}, dimensions={0}, use_global_device_ids=true | all-gather | bytes 1179648 | tf_op jit(solution)/shard_map/gather_tokens/all_gather | solution.py:285
  39.0 0.7 project.1
  39.8 25.5 %all_to_all.20.in_ref = bf16[32,72,128]{2,1,0:T(8,128)(2,1)S(1)} all-to-all(bf16[32,72,128]{2,1,0:T(8,128)(2,1)S(1)} %bitcast.25), channel_id=1, replica_groups=mesh['y'=8,'core'=2,'x'=4,'z'=8] {'x','z'}, dimensions={0} | all-to-all | bytes 1179648 | tf_op jit(solution)/shard_map/sum_req/all_to_all | solution.py:300
  65.3 0.7 sum_req.1
  66.0 5.2 %all-gather.3.pair_ref = f32[2,12,128]{2,1,0:T(8,128)S(1)} all-gather(f32[1,12,128]{2,1,0:T(8,128)S(1)} %bitcast.33), channel_id=3, replica_groups=mesh['y'=8,'core'=2,'x'=4,'z'=8] {'core'}, dimensions={0}, use_global_device_ids=true | all-gather | bytes 18432 | tf_op jit(solution)/shard_map/scan/all_gather | solution.py:315
  71.2 2.6 %scan.1 = (f32[12,1024]{1,0:T(8,128)S(1)}, f32[12,128]{1,0:T(8,128)S(1)}, f32[3,1024,128]{2,1,0:T(8,128)}, bf16[3,3,1024]{2,1,0:T(4,128)(2,1)}) custom-call(f32[12,1024]{1,0:T(8,128)S(1)} %get-tuple-element.13.gate_ref, f32[12,1024]{1,0:T(8,128)S(1)} %get-tuple-element.14.inner_ref, f32[12,128]{1,0:T(8,128)S(1)} %get-tuple-element.15.step_ref, ...), custom_call_target="tpu_custom_call" | custom-call | tf_op jit(solution)/shard_map/scan/pallas_call | solution.py:316
  73.8 1.9 %all-gather.4.squares_ref = f32[2,12,128]{2,1,0:T(8,128)S(1)} all-gather(f32[1,12,128]{2,1,0:T(8,128)S(1)} %bitcast.32), channel_id=4, replica_groups=mesh['y'=8,'core'=2,'x'=4,'z'=8] {'core'}, dimensions={0}, use_global_device_ids=true | all-gather | bytes 18432 | tf_op jit(solution)/shard_map/normalise/all_gather | solution.py:344
  75.7 0.1 normalise.1
  75.9 24.2 %all_to_all.21.in_ref = bf16[32,24,512]{2,1,0:T(8,128)(2,1)S(1)} all-to-all(bf16[32,24,512]{2,1,0:T(8,128)(2,1)S(1)} %normalise.1), channel_id=1, replica_groups=mesh['y'=8,'core'=2,'x'=4,'z'=8] {'x','z'}, dimensions={0} | all-to-all | bytes 1572864 | tf_op jit(solution)/shard_map/gather_normed/all_to_all | solution.py:351
  100.0 0.7 project_out.1
  100.7 20.6 %all_to_all.22 = bf16[16,24,256]{2,1,0:T(8,128)(2,1)S(1)} all-to-all(bf16[16,24,256]{2,1,0:T(8,128)(2,1)S(1)} %bitcast.31), channel_id=1, replica_groups=mesh['y'=8,'core'=2,'x'=4,'z'=8] {'y','core'}, dimensions={0} | all-to-all | bytes 393216 | tf_op jit(solution)/shard_map/sum_head/all_to_all | solution.py:365
  121.3 0.6 reshape.48
  (38 shorter events, 0.3 us)
Async XLA Ops:
  0.6 12.3 %copy-start.12 = (bf16[256,2,1024]{2,1,0:T(2,128)(2,1)S(1)}, bf16[256,2,1024]{2,1,0:T(2,128)(2,1)}, u32[]{:S(2)}) copy-start(bf16[256,2,1024]{2,1,0:T(2,128)(2,1)} %param.17) | copy-start | bytes 3145732
  2.2 21.4 %copy-start.14 = (bf16[256,16]{0,1:T(8,128)(2,1)S(1)}, bf16[256,16]{0,1:T(8,128)(2,1)}, u32[]{:S(2)}) copy-start(bf16[256,16]{0,1:T(8,128)(2,1)} %param.18) | copy-start | bytes 24580
  2.2 32.8 %all-to-all-start = ((bf16[32,24,256]{2,1,0:T(8,128)(2,1)}), bf16[32,24,256]{2,1,0:T(8,128)(2,1)S(1)}, u32[]{:S(2)}, u32[]{:S(2)}) async-start(bf16[32,24,256]{2,1,0:T(8,128)(2,1)} %broadcast_in_dim.29), calls=%async_computation | async-start | bytes 786432 | tf_op jit(solution)/shard_map/gather_tokens/all_to_all | solution.py:284
  12.9 11.0 %copy-start.13 = (bf16[256,128]{1,0:T(8,128)(2,1)S(1)}, bf16[256,128]{1,0:T(8,128)(2,1)}, u32[]{:S(2)}) copy-start(bf16[256,128]{1,0:T(8,128)(2,1)} %param.19) | copy-start | bytes 196612
  13.6 12.2 %collective-permute-start.2 = (bf16[256,2,256]{2,1,0:T(2,128)(2,1)S(1)}, bf16[256,2,256]{2,1,0:T(2,128)(2,1)S(1)}, u32[]{:S(2)}, u32[]{:S(2)}) collective-permute-start(bf16[256,2,256]{2,1,0:T(2,128)(2,1)S(1)} %get-tuple-element.22), channel_id=1, source_target_pairs={{0,24},{8,0},{16,8},{24,16},{1,25},{9,1},{17,9},{25,17},{2,26},{10... | collective-permute-start | bytes 786440 | tf_op jit(solution)/shard_map/move_weights/ppermute | solution.py:275
  18.0 11.7 %collective-permute-start = (bf16[256,2,256]{2,1,0:T(2,128)(2,1)S(1)}, bf16[256,2,256]{2,1,0:T(2,128)(2,1)S(1)}, u32[]{:S(2)}, u32[]{:S(2)}) collective-permute-start(bf16[256,2,256]{2,1,0:T(2,128)(2,1)S(1)} %get-tuple-element.23), channel_id=1, source_target_pairs={{0,8},{8,16},{16,24},{24,0},{1,9},{9,17},{17,25},{25,1},{2,10},{10... | collective-permute-start | bytes 786440 | tf_op jit(solution)/shard_map/move_weights/ppermute | solution.py:275
  20.0 15.0 %collective-permute-start.1 = (bf16[256,2,256]{2,1,0:T(2,128)(2,1)S(1)}, bf16[256,2,256]{2,1,0:T(2,128)(2,1)S(1)}, u32[]{:S(2)}, u32[]{:S(2)}) collective-permute-start(bf16[256,2,256]{2,1,0:T(2,128)(2,1)S(1)} %get-tuple-element.25), channel_id=1, source_target_pairs={{0,16},{8,24},{16,0},{24,8},{1,17},{9,25},{17,1},{25,9},{2,18},{10... | collective-permute-start | bytes 786440 | tf_op jit(solution)/shard_map/move_weights/ppermute | solution.py:275
  39.0 26.3 %copy-start.6 = (bf16[3,3,128]{2,1,0:T(4,128)(2,1)S(1)}, bf16[3,3,128]{2,1,0:T(4,128)(2,1)}, u32[]{:S(2)}) copy-start(bf16[3,3,128]{2,1,0:T(4,128)(2,1)} %hist_ref.2) | copy-start | bytes 6916
  39.0 26.3 %copy-start.7 = (f32[4,128]{1,0:T(4,128)S(1)}, f32[4,128]{1,0:T(4,128)}, u32[]{:S(2)}) copy-start(f32[4,128]{1,0:T(4,128)} %taps_ref.2) | copy-start | bytes 6148
  39.0 26.3 %copy-start.11 = (f32[128]{0:T(128)S(1)}, f32[128]{0:T(128)}, u32[]{:S(2)}) copy-start(f32[128]{0:T(128)} %param.25) | copy-start | bytes 1540
  39.0 32.2 %copy-start = (f32[3,16,64,128]{3,2,1,0:T(8,128)S(1)}, f32[3,16,64,128]{3,2,1,0:T(8,128)}, u32[]{:S(2)}) copy-start(f32[3,16,64,128]{3,2,1,0:T(8,128)} %param.31) | copy-start | bytes 4718596
  39.0 32.2 %copy-start.2 = (bf16[3,3,1024]{2,1,0:T(4,128)(2,1)S(1)}, bf16[3,3,1024]{2,1,0:T(4,128)(2,1)}, u32[]{:S(2)}) copy-start(bf16[3,3,1024]{2,1,0:T(4,128)(2,1)} %hist_ref.3) | copy-start | bytes 55300
  39.0 32.2 %copy-start.3 = (f32[4,1024]{1,0:T(4,128)S(1)}, f32[4,1024]{1,0:T(4,128)}, u32[]{:S(2)}) copy-start(f32[4,1024]{1,0:T(4,128)} %taps_ref.3) | copy-start | bytes 49156
  39.0 32.2 %copy-start.4 = (f32[1024]{0:T(1024)S(1)}, f32[1024]{0:T(1024)}, u32[]{:S(2)}) copy-start(f32[1024]{0:T(1024)} %param.23) | copy-start | bytes 12292
  39.0 32.2 %copy-start.8 = (f32[16]{0:T(128)S(1)}, f32[16]{0:T(128)}, u32[]{:S(2)}) copy-start(f32[16]{0:T(128)} %param.26) | copy-start | bytes 196
  39.0 32.2 %copy-start.9 = (f32[16]{0:T(128)S(1)}, f32[16]{0:T(128)}, u32[]{:S(2)}) copy-start(f32[16]{0:T(128)} %param.27) | copy-start | bytes 196
  39.0 32.2 %copy-start.10 = (f32[16]{0:T(128)S(1)}, f32[16]{0:T(128)}, u32[]{:S(2)}) copy-start(f32[16]{0:T(128)} %param.28) | copy-start | bytes 196
  39.8 36.0 %copy-start.5 = (f32[1024]{0:T(1024)S(1)}, f32[1024]{0:T(1024)}, u32[]{:S(2)}) copy-start(f32[1024]{0:T(1024)} %param.29) | copy-start | bytes 12292
  73.8 26.3 %copy-start.1 = (bf16[1024,256]{1,0:T(8,128)(2,1)S(1)}, bf16[1024,256]{1,0:T(8,128)(2,1)}, u32[]{:S(2)}) copy-start(bf16[1024,256]{1,0:T(8,128)(2,1)} %weight_ref.1) | copy-start | bytes 1572868

commit v3 on v2

--- a/solution.py
+++ b/solution.py
@@ -11,9 +11,17 @@
 EPSILON = 1e-05
 F32 = jnp.float32
 BF16 = jnp.bfloat16
-Y_SIZE, CORE_SIZE, X_SIZE, Z_SIZE = 8, 2, 4, 8
+Y_SIZE, CORE_SIZE = 8, 2
 HEAD_AXES = ("y", "core")
-REQ_AXES = ("x", "z")
+REQ_AXES = ("x1", "x0", "z2", "z1", "z0")
+REQ_COUNT = 32
+SQUARE_AXES = ("x0", "z0")
+SQUARE = 4
+MEMBERS = [
+    [16 * x1 + 8 * x0 + 2 * z_high + z0 for x1 in range(2) for z_high in range(4)]
+    for x0 in range(2)
+    for z0 in range(2)
+]
 VMEM_LIMIT = 40 * 1024 * 1024
 
 
@@ -33,19 +41,38 @@
     )
 
 
+def copy_tokens(in_ref, out_ref, flat):
+    requests, steps, _ = in_ref.shape
+    for req in range(requests):
+        flat[req * steps : (req + 1) * steps, :] = in_ref[req].astype(F32)
+    block = flat[...].astype(BF16)
+    for copy in range(out_ref.shape[0]):
+        out_ref[copy] = block
+
+
+def sum_heads(in_ref, out_ref, flat):
+    requests, steps, _ = out_ref.shape
+    total = in_ref[0].astype(F32)
+    for part in range(1, in_ref.shape[0]):
+        total = total + in_ref[part].astype(F32)
+    flat[...] = total
+    for req in range(requests):
+        out_ref[req] = flat[req * steps : (req + 1) * steps, :].astype(BF16)
+
+
 def project(
-    x_ref, rows_ref, own_ref, first_ref, second_ref, third_ref, extra_ref, out_ref, messages
+    here_ref, rows_ref, own_ref, first_ref, second_ref, third_ref, extra_ref, out_ref, messages
 ):
     cores, per_core, block_rows, features = rows_ref.shape
-    y_count = per_core // X_SIZE
+    y_count = per_core // SQUARE
     rows = block_rows // 2
     lanes = out_ref.shape[1]
-    tiles = out_ref.shape[0] // (X_SIZE * Z_SIZE * rows)
-    here = x_ref[0]
+    tiles = out_ref.shape[0] // (REQ_COUNT * rows)
+    here = here_ref[0]
     for core in range(cores):
         total = None
         for shift, weight_ref in enumerate((own_ref, first_ref, second_ref, third_ref)):
-            source = lax.rem(here - shift + X_SIZE, X_SIZE)
+            source = jnp.bitwise_xor(here, shift)
             block = rows_ref[core, pl.ds(source * y_count, y_count)]
             block = block.reshape(y_count * block_rows, features)
             part = jnp.dot(block, weight_ref[...], preferred_element_type=F32)
@@ -78,16 +105,16 @@
     requests, history, lanes = hist_ref.shape
     rows = gate_ref.shape[0]
     steps = rows // requests
-    chunk = gate_ref.shape[1] // X_SIZE
+    chunk = gate_ref.shape[1] // SQUARE
     tiles = chunk // lanes
     extra = None
-    for x in range(X_SIZE):
-        total = in_ref[x * Z_SIZE].astype(F32)
-        for z in range(1, Z_SIZE):
-            total = total + in_ref[x * Z_SIZE + z].astype(F32)
+    for square, members in enumerate(MEMBERS):
+        total = in_ref[members[0]].astype(F32)
+        for member in members[1:]:
+            total = total + in_ref[member].astype(F32)
         rounded = total.astype(BF16).astype(F32)
         for tile in range(tiles):
-            column = x * chunk + tile * lanes
+            column = square * chunk + tile * lanes
             gate_ref[:, column : column + lanes] = rounded[tile * rows : (tile + 1) * rows]
             at = (tiles + tile) * rows
             inner_ref[:, column : column + lanes] = rounded[at : at + rows]
@@ -256,32 +283,35 @@
     requests, heads, head_size, state_size = ssm_state.shape
     width = heads * head_size
     head_count = Y_SIZE * CORE_SIZE
-    req_count = X_SIZE * Z_SIZE
+    req_count = REQ_COUNT
     rows = steps * requests
     sds = jax.ShapeDtypeStruct
 
     lanes = bc_weight.shape[1]
-    chunk = width // X_SIZE
+    chunk = width // SQUARE
     with jax.named_scope("move_weights"):
-        here = lax.axis_index("x")
+        here = lax.axis_index(SQUARE_AXES)
         chunks = []
-        for shift in range(X_SIZE):
-            target = lax.rem(here + shift, X_SIZE)
+        for flip in range(SQUARE):
+            target = jnp.bitwise_xor(here, flip)
             part = lax.dynamic_slice(
                 gate_inner_weight, (0, 0, target * chunk), (features, 2, chunk)
             )
-            if shift:
-                route = [(x, (x + shift) % X_SIZE) for x in range(X_SIZE)]
-                part = lax.ppermute(part, "x", route)
+            if flip:
+                route = [(at, at ^ flip) for at in range(SQUARE)]
+                part = lax.ppermute(part, SQUARE_AXES, route)
             chunks.append(part.reshape(features, 2 * chunk))
         extra = jnp.concatenate(
             [bc_weight, step_weight, jnp.zeros((features, lanes - heads), BF16)], axis=1
         )
 
     with jax.named_scope("gather_tokens"):
-        own = jnp.transpose(tokens, (1, 0, 2)).reshape(rows_head * steps, features)
-        own = jnp.broadcast_to(own[None], (X_SIZE * Y_SIZE,) + own.shape)
-        gathered = lax.all_to_all(own, ("x", "y"), 0, 0, tiled=True)
+        own = call(
+            copy_tokens,
+            sds((SQUARE * Y_SIZE, rows_head * steps, features), BF16),
+            [pltpu.VMEM((rows_head * steps, features), F32)],
+        )(jnp.transpose(tokens, (1, 0, 2)))
+        gathered = lax.all_to_all(own, SQUARE_AXES + ("y",), 0, 0, tiled=True)
         gathered = lax.all_gather(gathered, "core", axis=0, tiled=False)
 
     with jax.named_scope("project"):
@@ -363,15 +393,19 @@
     with jax.named_scope("sum_head"):
         blocks = product.reshape(head_count, rows_head * steps, out_columns)
         blocks = lax.all_to_all(blocks, HEAD_AXES, 0, 0, tiled=True)
-        mixed = jnp.sum(blocks.astype(F32), axis=0).astype(BF16)
-        mixed = jnp.transpose(mixed.reshape(rows_head, steps, out_columns), (1, 0, 2))
+        mixed = call(
+            sum_heads,
+            sds((rows_head, steps, out_columns), BF16),
+            [pltpu.VMEM((rows_head * steps, out_columns), F32)],
+        )(blocks)
+        mixed = jnp.transpose(mixed, (1, 0, 2))
     return (mixed, new_state.reshape(ssm_state.shape), new_conv_inner, new_conv_groups)
 
 
 def solution(mesh):
     head, req = HEAD_AXES, REQ_AXES
     split = Mesh(
-        mesh.devices.reshape(Y_SIZE, CORE_SIZE, X_SIZE, Z_SIZE), HEAD_AXES + REQ_AXES
+        mesh.devices.reshape((Y_SIZE, CORE_SIZE) + (2,) * len(REQ_AXES)), HEAD_AXES + REQ_AXES
     )
     placed = (
         P(None, head, req),

time: 122 us -> 121 us (level)
  local copies, waits for them, and re-layouts: 3.32 us -> 1.83 us
  Pallas kernels: 4.75 us -> 6.16 us
  starting transfers between devices: 20.6 us -> 19.3 us
    broadcast_in_dim x2 -> x0, local copies, waits for them, and re-layouts: 1.58 us -> none  [shards(): own = jnp.broadcast_to(own[None], (X_SIZE * Y_SIZE,) + own.shape)]
    ppermute x3, starting transfers between devices: 9.93 us -> 8.37 us  [shards(): part = lax.ppermute(part, SQUARE_AXES, route)]
    pallas_call x0 -> x2, Pallas kernels: none -> 1.42 us  [the longest x1 0.78 us: shards(): call(copy_tokens, sds((SQUARE * Y_SIZE, rows_head * steps, features), BF1...]
    all_to_all x1, blocking collectives: 25.5 us -> 26.8 us  [shards(): lax.all_to_all(messages.reshape(req_count, tiles * rows, lanes), REQ_AXES...]
where the time goes in v3:
time: 121 us
  blocking collectives  81.8 us (68%)
  starting transfers between devices  19.3 us (16%)
  waiting for transfers between devices  10.8 us (9%)
  Pallas kernels  6.16 us (5%)
  local copies, waits for them, and re-layouts  1.83 us (2%)
    all_to_all x1, blocking collectives, shards(): lax.all_to_all(messages.reshape(req_count, tiles * rows, lanes), REQ_AXES...  26.8 us
    all_to_all x1, blocking collectives, shards(): all_rows = lax.all_to_all(normed, REQ_AXES, 0, 0, tiled=True)  24.2 us
    all_to_all x1, blocking collectives, shards(): blocks = lax.all_to_all(blocks, HEAD_AXES, 0, 0, tiled=True)  20.9 us
    all_to_all x1, starting transfers between devices, shards(): gathered = lax.all_to_all(own, SQUARE_AXES + ('y',), 0, 0, tiled=True)  10.9 us
    ppermute x3, waiting for transfers between devices, shards(): part = lax.ppermute(part, SQUARE_AXES, route)  10.8 us
    ppermute x3, starting transfers between devices, shards(): part = lax.ppermute(part, SQUARE_AXES, route)  8.37 us
    all_gather x1, blocking collectives, shards(): pair = lax.all_gather(bc_conv, 'core', axis=0, tiled=False)  5.21 us
    all_gather x1, blocking collectives, shards(): gathered = lax.all_gather(gathered, 'core', axis=0, tiled=False)  2.82 us
  transfers between devices with their start and end apart: 4, of which 3 were waited for; matrix products, arithmetic and copies ran while one was open for 1% of the time, Pallas kernels for 0%

profile of v3, /device:TPU:1, one launch (start us, length us, event | category | flops | bytes accessed | tf_op | source)
XLA Modules:
  0.0 120.8 jit_solution(9806299803150946920)
XLA Ops:
  0.6 0.7 copy-done.4
  1.3 0.8 gather_tokens.1
  2.1 10.9 %all-to-all-start = ((bf16[32,24,256]{2,1,0:T(8,128)(2,1)}), bf16[32,24,256]{2,1,0:T(8,128)(2,1)S(1)}, u32[]{:S(2)}, u32[]{:S(2)}) async-start(bf16[32,24,256]{2,1,0:T(8,128)(2,1)} %gather_tokens.1), calls=%async_computation | async-start | bytes 786432 | tf_op jit(solution)/shard_map/gather_tokens/all_to_all | solution.py:314
  13.1 0.7 constant_dynamic-slice_fusion
  13.8 4.1 %collective-permute-start.2 = (bf16[256,2,256]{2,1,0:T(2,128)(2,1)S(1)}, bf16[256,2,256]{2,1,0:T(2,128)(2,1)S(1)}, u32[]{:S(2)}, u32[]{:S(2)}) collective-permute-start(bf16[256,2,256]{2,1,0:T(2,128)(2,1)S(1)} %get-tuple-element.22), channel_id=1, source_target_pairs={{0,9},{1,8},{8,1},{9,0},{2,11},{3,10},{10,3},{11,2},{4,13},{5,12},... | collective-permute-start | bytes 786440 | tf_op jit(solution)/shard_map/move_weights/ppermute | solution.py:302
  17.9 2.2 %collective-permute-start = (bf16[256,2,256]{2,1,0:T(2,128)(2,1)S(1)}, bf16[256,2,256]{2,1,0:T(2,128)(2,1)S(1)}, u32[]{:S(2)}, u32[]{:S(2)}) collective-permute-start(bf16[256,2,256]{2,1,0:T(2,128)(2,1)S(1)} %get-tuple-element.23), channel_id=1, source_target_pairs={{0,1},{1,0},{8,9},{9,8},{2,3},{3,2},{10,11},{11,10},{4,5},{5,4},{1... | collective-permute-start | bytes 786440 | tf_op jit(solution)/shard_map/move_weights/ppermute | solution.py:302
  20.1 2.1 %collective-permute-start.1 = (bf16[256,2,256]{2,1,0:T(2,128)(2,1)S(1)}, bf16[256,2,256]{2,1,0:T(2,128)(2,1)S(1)}, u32[]{:S(2)}, u32[]{:S(2)}) collective-permute-start(bf16[256,2,256]{2,1,0:T(2,128)(2,1)S(1)} %get-tuple-element.25), channel_id=1, source_target_pairs={{0,8},{1,9},{8,0},{9,1},{2,10},{3,11},{10,2},{11,3},{4,12},{5,13},... | collective-permute-start | bytes 786440 | tf_op jit(solution)/shard_map/move_weights/ppermute | solution.py:302
  22.2 0.1 copy.21
  22.4 0.1 pad.2.clone
  22.5 4.0 %collective-permute-done.2 = bf16[256,2,256]{2,1,0:T(2,128)(2,1)S(1)} collective-permute-done((bf16[256,2,256]{2,1,0:T(2,128)(2,1)S(1)}, bf16[256,2,256]{2,1,0:T(2,128)(2,1)S(1)}, u32[]{:S(2)}, u32[]{:S(2)}) %collective-permute-start.2) | collective-permute-done | bytes 262176 | tf_op jit(solution)/shard_map/move_weights/ppermute | solution.py:302
  26.5 6.2 %collective-permute-done = bf16[256,2,256]{2,1,0:T(2,128)(2,1)S(1)} collective-permute-done((bf16[256,2,256]{2,1,0:T(2,128)(2,1)S(1)}, bf16[256,2,256]{2,1,0:T(2,128)(2,1)S(1)}, u32[]{:S(2)}, u32[]{:S(2)}) %collective-permute-start) | collective-permute-done | bytes 262176 | tf_op jit(solution)/shard_map/move_weights/ppermute | solution.py:302
  32.7 0.6 collective-permute-done.1
  33.4 2.8 %all-gather = bf16[64,24,256]{2,1,0:T(8,128)(2,1)S(1)} all-gather(bf16[32,24,256]{2,1,0:T(8,128)(2,1)S(1)} %all-to-all-done), channel_id=2, replica_groups=mesh['y'=8,'core'=2,'x1'=2,'x0'=2,'z2'=2,'z1'=2,'z0'=2] {'core'}, dimensions={0}, use_global_device_ids=true | all-gather | bytes 1179648 | tf_op jit(solution)/shard_map/gather_tokens/all_gather | solution.py:315
  36.3 0.7 project.1
  37.0 26.8 %all_to_all.20.in_ref = bf16[32,72,128]{2,1,0:T(8,128)(2,1)S(1)} all-to-all(bf16[32,72,128]{2,1,0:T(8,128)(2,1)S(1)} %bitcast.25), channel_id=1, replica_groups=mesh['y'=8,'core'=2,'x1'=2,'x0'=2,'z2'=2,'z1'=2,'z0'=2] {'x1','x0','z2',..., dimensions={0} | all-to-all | bytes 1179648 | tf_op jit(solution)/shard_map/sum_req/all_to_all | solution.py:330
  63.8 0.7 sum_req.1
  64.5 5.2 %all-gather.3.pair_ref = f32[2,12,128]{2,1,0:T(8,128)S(1)} all-gather(f32[1,12,128]{2,1,0:T(8,128)S(1)} %bitcast.34), channel_id=3, replica_groups=mesh['y'=8,'core'=2,'x1'=2,'x0'=2,'z2'=2,'z1'=2,'z0'=2] {'core'}, dimensions={0}, use_global_device_ids=true | all-gather | bytes 18432 | tf_op jit(solution)/shard_map/scan/all_gather | solution.py:345
  69.7 2.6 %scan.1 = (f32[12,1024]{1,0:T(8,128)S(1)}, f32[12,128]{1,0:T(8,128)S(1)}, f32[3,1024,128]{2,1,0:T(8,128)}, bf16[3,3,1024]{2,1,0:T(4,128)(2,1)}) custom-call(f32[12,1024]{1,0:T(8,128)S(1)} %get-tuple-element.13.gate_ref, f32[12,1024]{1,0:T(8,128)S(1)} %get-tuple-element.14.inner_ref, f32[12,128]{1,0:T(8,128)S(1)} %get-tuple-element.15.step_ref, ...), custom_call_target="tpu_custom_call" | custom-call | tf_op jit(solution)/shard_map/scan/pallas_call | solution.py:346
  72.3 1.9 %all-gather.4.squares_ref = f32[2,12,128]{2,1,0:T(8,128)S(1)} all-gather(f32[1,12,128]{2,1,0:T(8,128)S(1)} %bitcast.33), channel_id=4, replica_groups=mesh['y'=8,'core'=2,'x1'=2,'x0'=2,'z2'=2,'z1'=2,'z0'=2] {'core'}, dimensions={0}, use_global_device_ids=true | all-gather | bytes 18432 | tf_op jit(solution)/shard_map/normalise/all_gather | solution.py:374
  74.3 0.1 normalise.1
  74.4 24.2 %all_to_all.21.in_ref = bf16[32,24,512]{2,1,0:T(8,128)(2,1)S(1)} all-to-all(bf16[32,24,512]{2,1,0:T(8,128)(2,1)S(1)} %normalise.1), channel_id=1, replica_groups=mesh['y'=8,'core'=2,'x1'=2,'x0'=2,'z2'=2,'z1'=2,'z0'=2] {'x1','x0','z2',..., dimensions={0} | all-to-all | bytes 1572864 | tf_op jit(solution)/shard_map/gather_normed/all_to_all | solution.py:381
  98.6 0.7 project_out.1
  99.2 20.9 %all_to_all.22.in_ref = bf16[16,24,256]{2,1,0:T(8,128)(2,1)S(1)} all-to-all(bf16[16,24,256]{2,1,0:T(8,128)(2,1)S(1)} %bitcast.31), channel_id=1, replica_groups=mesh['y'=8,'core'=2,'x1'=2,'x0'=2,'z2'=2,'z1'=2,'z0'=2] {'y','core'}, dimensions={0} | all-to-all | bytes 393216 | tf_op jit(solution)/shard_map/sum_head/all_to_all | solution.py:395
  120.1 0.6 sum_head.1
  (38 shorter events, 0.2 us)
Async XLA Ops:
  0.6 0.7 copy-start.4
  1.3 11.7 %copy-start.13 = (bf16[256,2,1024]{2,1,0:T(2,128)(2,1)S(1)}, bf16[256,2,1024]{2,1,0:T(2,128)(2,1)}, u32[]{:S(2)}) copy-start(bf16[256,2,1024]{2,1,0:T(2,128)(2,1)} %param.17) | copy-start | bytes 3145732
  2.1 20.1 %copy-start.15 = (bf16[256,16]{0,1:T(8,128)(2,1)S(1)}, bf16[256,16]{0,1:T(8,128)(2,1)}, u32[]{:S(2)}) copy-start(bf16[256,16]{0,1:T(8,128)(2,1)} %param.18) | copy-start | bytes 24580
  2.1 31.3 %all-to-all-start = ((bf16[32,24,256]{2,1,0:T(8,128)(2,1)}), bf16[32,24,256]{2,1,0:T(8,128)(2,1)S(1)}, u32[]{:S(2)}, u32[]{:S(2)}) async-start(bf16[32,24,256]{2,1,0:T(8,128)(2,1)} %gather_tokens.1), calls=%async_computation | async-start | bytes 786432 | tf_op jit(solution)/shard_map/gather_tokens/all_to_all | solution.py:314
  13.0 9.4 %copy-start.14 = (bf16[256,128]{1,0:T(8,128)(2,1)S(1)}, bf16[256,128]{1,0:T(8,128)(2,1)}, u32[]{:S(2)}) copy-start(bf16[256,128]{1,0:T(8,128)(2,1)} %param.19) | copy-start | bytes 196612
  13.8 12.6 %collective-permute-start.2 = (bf16[256,2,256]{2,1,0:T(2,128)(2,1)S(1)}, bf16[256,2,256]{2,1,0:T(2,128)(2,1)S(1)}, u32[]{:S(2)}, u32[]{:S(2)}) collective-permute-start(bf16[256,2,256]{2,1,0:T(2,128)(2,1)S(1)} %get-tuple-element.22), channel_id=1, source_target_pairs={{0,9},{1,8},{8,1},{9,0},{2,11},{3,10},{10,3},{11,2},{4,13},{5,12},... | collective-permute-start | bytes 786440 | tf_op jit(solution)/shard_map/move_weights/ppermute | solution.py:302
  17.9 14.8 %collective-permute-start = (bf16[256,2,256]{2,1,0:T(2,128)(2,1)S(1)}, bf16[256,2,256]{2,1,0:T(2,128)(2,1)S(1)}, u32[]{:S(2)}, u32[]{:S(2)}) collective-permute-start(bf16[256,2,256]{2,1,0:T(2,128)(2,1)S(1)} %get-tuple-element.23), channel_id=1, source_target_pairs={{0,1},{1,0},{8,9},{9,8},{2,3},{3,2},{10,11},{11,10},{4,5},{5,4},{1... | collective-permute-start | bytes 786440 | tf_op jit(solution)/shard_map/move_weights/ppermute | solution.py:302
  20.1 13.3 %collective-permute-start.1 = (bf16[256,2,256]{2,1,0:T(2,128)(2,1)S(1)}, bf16[256,2,256]{2,1,0:T(2,128)(2,1)S(1)}, u32[]{:S(2)}, u32[]{:S(2)}) collective-permute-start(bf16[256,2,256]{2,1,0:T(2,128)(2,1)S(1)} %get-tuple-element.25), channel_id=1, source_target_pairs={{0,8},{1,9},{8,0},{9,1},{2,10},{3,11},{10,2},{11,3},{4,12},{5,13},... | collective-permute-start | bytes 786440 | tf_op jit(solution)/shard_map/move_weights/ppermute | solution.py:302
  36.2 27.6 %copy-start.7 = (bf16[3,3,128]{2,1,0:T(4,128)(2,1)S(1)}, bf16[3,3,128]{2,1,0:T(4,128)(2,1)}, u32[]{:S(2)}) copy-start(bf16[3,3,128]{2,1,0:T(4,128)(2,1)} %hist_ref.2) | copy-start | bytes 6916
  36.2 27.6 %copy-start.8 = (f32[4,128]{1,0:T(4,128)S(1)}, f32[4,128]{1,0:T(4,128)}, u32[]{:S(2)}) copy-start(f32[4,128]{1,0:T(4,128)} %taps_ref.2) | copy-start | bytes 6148
  36.2 27.6 %copy-start.12 = (f32[128]{0:T(128)S(1)}, f32[128]{0:T(128)}, u32[]{:S(2)}) copy-start(f32[128]{0:T(128)} %param.25) | copy-start | bytes 1540
  36.2 33.5 %copy-start = (f32[3,16,64,128]{3,2,1,0:T(8,128)S(1)}, f32[3,16,64,128]{3,2,1,0:T(8,128)}, u32[]{:S(2)}) copy-start(f32[3,16,64,128]{3,2,1,0:T(8,128)} %param.31) | copy-start | bytes 4718596
  36.2 33.5 %copy-start.2 = (bf16[3,3,1024]{2,1,0:T(4,128)(2,1)S(1)}, bf16[3,3,1024]{2,1,0:T(4,128)(2,1)}, u32[]{:S(2)}) copy-start(bf16[3,3,1024]{2,1,0:T(4,128)(2,1)} %hist_ref.3) | copy-start | bytes 55300
  36.2 33.5 %copy-start.3 = (f32[4,1024]{1,0:T(4,128)S(1)}, f32[4,1024]{1,0:T(4,128)}, u32[]{:S(2)}) copy-start(f32[4,1024]{1,0:T(4,128)} %taps_ref.3) | copy-start | bytes 49156
  36.3 33.4 %copy-start.5 = (f32[1024]{0:T(1024)S(1)}, f32[1024]{0:T(1024)}, u32[]{:S(2)}) copy-start(f32[1024]{0:T(1024)} %param.23) | copy-start | bytes 12292
  36.3 33.4 %copy-start.9 = (f32[16]{0:T(128)S(1)}, f32[16]{0:T(128)}, u32[]{:S(2)}) copy-start(f32[16]{0:T(128)} %param.26) | copy-start | bytes 196
  36.3 33.4 %copy-start.10 = (f32[16]{0:T(128)S(1)}, f32[16]{0:T(128)}, u32[]{:S(2)}) copy-start(f32[16]{0:T(128)} %param.27) | copy-start | bytes 196
  36.3 33.4 %copy-start.11 = (f32[16]{0:T(128)S(1)}, f32[16]{0:T(128)}, u32[]{:S(2)}) copy-start(f32[16]{0:T(128)} %param.28) | copy-start | bytes 196
  37.0 37.2 %copy-start.6 = (f32[1024]{0:T(1024)S(1)}, f32[1024]{0:T(1024)}, u32[]{:S(2)}) copy-start(f32[1024]{0:T(1024)} %param.29) | copy-start | bytes 12292
  72.3 26.3 %copy-start.1 = (bf16[1024,256]{1,0:T(8,128)(2,1)S(1)}, bf16[1024,256]{1,0:T(8,128)(2,1)}, u32[]{:S(2)}) copy-start(bf16[1024,256]{1,0:T(8,128)(2,1)} %weight_ref.1) | copy-start | bytes 1572868

commit v4 on v3

--- a/solution.py
+++ b/solution.py
@@ -17,6 +17,9 @@
 REQ_COUNT = 32
 SQUARE_AXES = ("x0", "z0")
 SQUARE = 4
+PAIR_AXIS = "z0"
+REST_AXES = ("x1", "x0", "z2", "z1")
+REST = 16
 MEMBERS = [
     [16 * x1 + 8 * x0 + 2 * z_high + z0 for x1 in range(2) for z_high in range(4)]
     for x0 in range(2)
@@ -29,15 +32,19 @@
     return value / (1.0 + jnp.exp(-value))
 
 
-def call(body, out_shape, scratch=(), cost=None):
-    whole = pl.BlockSpec(memory_space=pltpu.VMEM)
+WHOLE = pl.BlockSpec(memory_space=pltpu.VMEM)
+SCALARS = pl.BlockSpec(memory_space=pltpu.SMEM)
+
+
+def call(body, out_shape, scratch=(), in_specs=None):
+    places = {} if in_specs is None else {"in_specs": in_specs}
     return pl.pallas_call(
         body,
         out_shape=out_shape,
-        out_specs=jax.tree.map(lambda _: whole, out_shape),
+        out_specs=jax.tree.map(lambda _: WHOLE, out_shape),
         scratch_shapes=list(scratch),
         compiler_params=pltpu.CompilerParams(vmem_limit_bytes=VMEM_LIMIT),
-        cost_estimate=cost,
+        **places,
     )
 
 
@@ -50,14 +57,18 @@
         out_ref[copy] = block
 
 
-def sum_heads(in_ref, out_ref, flat):
+def sum_heads(in_ref, out_ref):
     requests, steps, _ = out_ref.shape
-    total = in_ref[0].astype(F32)
-    for part in range(1, in_ref.shape[0]):
-        total = total + in_ref[part].astype(F32)
-    flat[...] = total
-    for req in range(requests):
-        out_ref[req] = flat[req * steps : (req + 1) * steps, :].astype(BF16)
+    lanes = in_ref.shape[2]
+    half = requests // 2
+    for side in range(2):
+        total = in_ref[side].astype(F32)
+        for part in range(2 + side, in_ref.shape[0], 2):
+            total = total + in_ref[part].astype(F32)
+        for req in range(half):
+            left, right = req * steps, (half + req) * steps
+            out_ref[side * half + req, :, 0:lanes] = total[left : left + steps].astype(BF16)
+            out_ref[side * half + req, :, lanes:] = total[right : right + steps].astype(BF16)
 
 
 def project(
@@ -247,17 +258,19 @@
         out_ref[copy] = block
 
 
-def project_out(in_ref, weight_ref, out_ref, first, second, sums):
+def project_out(in_ref, weights_ref, out_ref, first, second, sums):
     blocks, block_rows, half = in_ref.shape
     rows = block_rows // 2
+    lanes = out_ref.shape[-1]
     flat = in_ref[...].reshape(blocks * block_rows, half)
-    first[...] = jnp.dot(flat, weight_ref[0:half, :], preferred_element_type=F32)
-    second[...] = jnp.dot(flat, weight_ref[half:, :], preferred_element_type=F32)
-    for block in range(blocks):
-        at = block * block_rows
-        sums[block * rows : (block + 1) * rows, :] = (
-            first[at : at + rows, :] + second[at + rows : at + block_rows, :]
-        )
+    for side in range(weights_ref.shape[0]):
+        first[...] = jnp.dot(flat, weights_ref[side, 0:half, :], preferred_element_type=F32)
+        second[...] = jnp.dot(flat, weights_ref[side, half:, :], preferred_element_type=F32)
+        for block in range(blocks):
+            at = block * block_rows
+            total = first[at : at + rows, :] + second[at + rows : at + block_rows, :]
+            sums[block, side, 0:rows, :] = total[:, 0:lanes]
+            sums[block, side, rows : 2 * rows, :] = total[:, lanes : 2 * lanes]
     out_ref[...] = sums[...].astype(BF16)
 
 
@@ -282,7 +295,6 @@
     steps, rows_head, features = tokens.shape
     requests, heads, head_size, state_size = ssm_state.shape
     width = heads * head_size
-    head_count = Y_SIZE * CORE_SIZE
     req_count = REQ_COUNT
     rows = steps * requests
     sds = jax.ShapeDtypeStruct
@@ -305,6 +317,9 @@
             [bc_weight, step_weight, jnp.zeros((features, lanes - heads), BF16)], axis=1
         )
 
+    with jax.named_scope("move_out_weight"):
+        pair_weights = lax.all_gather(out_weight, PAIR_AXIS, axis=0, tiled=False)
+
     with jax.named_scope("gather_tokens"):
         own = call(
             copy_tokens,
@@ -317,14 +332,11 @@
     with jax.named_scope("project"):
         tiles = 2 * chunk // lanes + 2
         message_rows = req_count * tiles * rows
-        whole = pl.BlockSpec(memory_space=pltpu.VMEM)
-        messages = pl.pallas_call(
+        messages = call(
             project,
-            out_shape=sds((message_rows, lanes), BF16),
-            in_specs=[pl.BlockSpec(memory_space=pltpu.SMEM)] + [whole] * 6,
-            out_specs=whole,
-            scratch_shapes=[pltpu.VMEM((message_rows, lanes), F32)],
-            compiler_params=pltpu.CompilerParams(vmem_limit_bytes=VMEM_LIMIT),
+            sds((message_rows, lanes), BF16),
+            [pltpu.VMEM((message_rows, lanes), F32)],
+            [SCALARS] + [WHOLE] * 6,
         )(here.astype(jnp.int32).reshape(1), gathered, *chunks, extra)
     with jax.named_scope("sum_req"):
         parts = lax.all_to_all(
@@ -374,30 +386,27 @@
         squares_pair = lax.all_gather(squares, "core", axis=0, tiled=False)
         normed = call(
             functools.partial(normalise, CORE_SIZE * width),
-            sds((req_count, 2 * rows, width // 2), BF16),
+            sds((REST, 2 * rows, width // 2), BF16),
             [pltpu.VMEM((2 * rows, width // 2), F32)],
         )(gated, squares_pair, norm_gain[None])
     with jax.named_scope("gather_normed"):
-        all_rows = lax.all_to_all(normed, REQ_AXES, 0, 0, tiled=True)
+        some_rows = lax.all_to_all(normed, REST_AXES, 0, 0, tiled=True)
     with jax.named_scope("project_out"):
         out_columns = out_weight.shape[1]
+        block = (REST, 2, 2 * rows, out_columns // 2)
         product = call(
             project_out,
-            sds((req_count * rows, out_columns), BF16),
+            sds(block, BF16),
             [
-                pltpu.VMEM((req_count * 2 * rows, out_columns), F32),
-                pltpu.VMEM((req_count * 2 * rows, out_columns), F32),
-                pltpu.VMEM((req_count * rows, out_columns), F32),
+                pltpu.VMEM((REST * 2 * rows, out_columns), F32),
+                pltpu.VMEM((REST * 2 * rows, out_columns), F32),
+                pltpu.VMEM(block, F32),
             ],
-        )(all_rows, out_weight)
+        )(some_rows, pair_weights)
     with jax.named_scope("sum_head"):
-        blocks = product.reshape(head_count, rows_head * steps, out_columns)
-        blocks = lax.all_to_all(blocks, HEAD_AXES, 0, 0, tiled=True)
-        mixed = call(
-            sum_heads,
-            sds((rows_head, steps, out_columns), BF16),
-            [pltpu.VMEM((rows_head * steps, out_columns), F32)],
-        )(blocks)
+        blocks = product.reshape((2 * REST,) + block[2:])
+        blocks = lax.all_to_all(blocks, HEAD_AXES + (PAIR_AXIS,), 0, 0, tiled=True)
+        mixed = call(sum_heads, sds((rows_head, steps, out_columns), BF16))(blocks)
         mixed = jnp.transpose(mixed, (1, 0, 2))
     return (mixed, new_state.reshape(ssm_state.shape), new_conv_inner, new_conv_groups)
 

time: 121 us -> 132 us (1.091)
  blocking collectives: 81.8 us -> 29 us
  waiting for transfers between devices: 10.8 us -> 41 us
  starting transfers between devices: 19.3 us -> 36.1 us
  between operations: 0.88 us -> 14.3 us
  Pallas kernels: 6.16 us -> 7.67 us
    all_to_all x3 -> x1, blocking collectives: 71.8 us -> 18.9 us  [shards(): blocks = lax.all_to_all(blocks, HEAD_AXES + (PAIR_AXIS,), 0, 0, tiled=True)]
    all_to_all x0 -> x2, waiting for transfers between devices: none -> 28.2 us  [the longest x1 14.8 us: shards(): lax.all_to_all(messages.reshape(req_count, tiles * rows, lanes), REQ_AXES...]
    all_to_all x0 -> x2, starting transfers between devices: none -> 16.8 us  [the longest x1 11.8 us: shards(): lax.all_to_all(messages.reshape(req_count, tiles * rows, lanes), REQ_AXES...]
    pallas_call x4, Pallas kernels: 2.13 us -> 3.66 us  [the longest x1 1.52 us: shards(): call(project, sds((message_rows, lanes), BF16), [pltpu.VMEM((message_rows...]
  transfers between devices with their start and end apart: 4 -> 7, of which waited for: 3 -> 5; matrix products, arithmetic and copies ran while one was open for 1% -> 1% of each run, Pallas kernels for 0% -> 3%
where the time goes in v4:
time: 132 us; the launch traced here: 131 us
  waiting for transfers between devices  41 us (31%)
  starting transfers between devices  36.1 us (27%)
  blocking collectives  29 us (22%)
  between operations  14.3 us (11%)
  Pallas kernels  7.67 us (6%)
  local copies, waits for them, and re-layouts  3.05 us (2%)
    all_to_all x1, blocking collectives, shards(): blocks = lax.all_to_all(blocks, HEAD_AXES + (PAIR_AXIS,), 0, 0, tiled=True)  18.9 us
    all_to_all x1, waiting for transfers between devices, shards(): lax.all_to_all(messages.reshape(req_count, tiles * rows, lanes), REQ_AXES...  14.8 us
    all_to_all x1, waiting for transfers between devices, shards(): some_rows = lax.all_to_all(normed, REST_AXES, 0, 0, tiled=True)  13.4 us
    all_to_all x1, starting transfers between devices, shards(): lax.all_to_all(messages.reshape(req_count, tiles * rows, lanes), REQ_AXES...  11.8 us
    ppermute x3, waiting for transfers between devices, shards(): part = lax.ppermute(part, SQUARE_AXES, route)  11.4 us
    all_to_all x1, starting transfers between devices, shards(): gathered = lax.all_to_all(own, SQUARE_AXES + ('y',), 0, 0, tiled=True)  10.9 us
    ppermute x3, starting transfers between devices, shards(): part = lax.ppermute(part, SQUARE_AXES, route)  8.37 us
    all_to_all x1, starting transfers between devices, shards(): some_rows = lax.all_to_all(normed, REST_AXES, 0, 0, tiled=True)  4.97 us
  transfers between devices with their start and end apart: 7, of which 5 were waited for; matrix products, arithmetic and copies ran while one was open for 1% of the time, Pallas kernels for 3%

profile of v4, /device:TPU:1, one launch (start us, length us, event | category | flops | bytes accessed | tf_op | source)
XLA Modules:
  0.0 131.1 jit_solution(3152739252053290005)
XLA Ops:
  7.2 0.7 copy-done.4
  7.9 0.8 gather_tokens.1
  8.7 10.9 %all-to-all-start = ((bf16[32,24,256]{2,1,0:T(8,128)(2,1)}), bf16[32,24,256]{2,1,0:T(8,128)(2,1)S(1)}, u32[]{:S(2)}, u32[]{:S(2)}) async-start(bf16[32,24,256]{2,1,0:T(8,128)(2,1)} %gather_tokens.1), calls=%async_computation | async-start | bytes 786432 | tf_op jit(solution)/shard_map/gather_tokens/all_to_all | solution.py:329
  19.6 0.7 constant_dynamic-slice_fusion
  20.4 3.1 %collective-permute-start = (bf16[256,2,256]{2,1,0:T(2,128)(2,1)S(1)}, bf16[256,2,256]{2,1,0:T(2,128)(2,1)S(1)}, u32[]{:S(2)}, u32[]{:S(2)}) collective-permute-start(bf16[256,2,256]{2,1,0:T(2,128)(2,1)S(1)} %get-tuple-element.23), channel_id=1, source_target_pairs={{0,1},{1,0},{8,9},{9,8},{2,3},{3,2},{10,11},{11,10},{4,5},{5,4},{1... | collective-permute-start | bytes 786440 | tf_op jit(solution)/shard_map/move_weights/ppermute | solution.py:314
  23.5 3.1 %collective-permute-start.1 = (bf16[256,2,256]{2,1,0:T(2,128)(2,1)S(1)}, bf16[256,2,256]{2,1,0:T(2,128)(2,1)S(1)}, u32[]{:S(2)}, u32[]{:S(2)}) collective-permute-start(bf16[256,2,256]{2,1,0:T(2,128)(2,1)S(1)} %get-tuple-element.25), channel_id=1, source_target_pairs={{0,8},{1,9},{8,0},{9,1},{2,10},{3,11},{10,2},{11,3},{4,12},{5,13},... | collective-permute-start | bytes 786440 | tf_op jit(solution)/shard_map/move_weights/ppermute | solution.py:314
  26.6 2.1 %collective-permute-start.2 = (bf16[256,2,256]{2,1,0:T(2,128)(2,1)S(1)}, bf16[256,2,256]{2,1,0:T(2,128)(2,1)S(1)}, u32[]{:S(2)}, u32[]{:S(2)}) collective-permute-start(bf16[256,2,256]{2,1,0:T(2,128)(2,1)S(1)} %get-tuple-element.22), channel_id=1, source_target_pairs={{0,9},{1,8},{8,1},{9,0},{2,11},{3,10},{10,3},{11,2},{4,13},{5,12},... | collective-permute-start | bytes 786440 | tf_op jit(solution)/shard_map/move_weights/ppermute | solution.py:314
  29.0 2.7 %collective-permute-done = bf16[256,2,256]{2,1,0:T(2,128)(2,1)S(1)} collective-permute-done((bf16[256,2,256]{2,1,0:T(2,128)(2,1)S(1)}, bf16[256,2,256]{2,1,0:T(2,128)(2,1)S(1)}, u32[]{:S(2)}, u32[]{:S(2)}) %collective-permute-start) | collective-permute-done | bytes 262176 | tf_op jit(solution)/shard_map/move_weights/ppermute | solution.py:314
  31.8 8.7 %collective-permute-done.1 = bf16[256,2,256]{2,1,0:T(2,128)(2,1)S(1)} collective-permute-done((bf16[256,2,256]{2,1,0:T(2,128)(2,1)S(1)}, bf16[256,2,256]{2,1,0:T(2,128)(2,1)S(1)}, u32[]{:S(2)}, u32[]{:S(2)}) %collective-permute-start.1) | collective-permute-done | bytes 262176 | tf_op jit(solution)/shard_map/move_weights/ppermute | solution.py:314
  40.6 3.4 %all-gather = bf16[64,24,256]{2,1,0:T(8,128)(2,1)S(1)} all-gather(bf16[32,24,256]{2,1,0:T(8,128)(2,1)S(1)} %all-to-all-done), channel_id=2, replica_groups=mesh['y'=8,'core'=2,'x1'=2,'x0'=2,'z2'=2,'z1'=2,'z0'=2] {'core'}, dimensions={0}, use_global_device_ids=true | all-gather | bytes 1179648 | tf_op jit(solution)/shard_map/gather_tokens/all_gather | solution.py:330
  44.0 1.5 %project.1 = bf16[2304,128]{1,0:T(8,128)(2,1)} custom-call(s32[1]{0:T(128)} %bitcast.here_ref, bf16[2,32,24,256]{3,2,1,0:T(8,128)(2,1)S(1)} %bitcast.25, bf16[256,512]{1,0:T(8,128)(2,1)S(1)} %bitcast.28, bf16[256,512]{1,0:T(8,128)(2,1)S(1)} %bitcast.29, bf16[256,512]{1,0:T(8,128)(2,1)S(1)} %bitcast.30, bf16[256,512]{1,0:T(8,128)(2,1)S(1)} %bitcast.31, ...), custom_call_target="tpu_custom_call" | custom-call | tf_op jit(solution)/shard_map/project/pallas_call | solution.py:335
  45.6 11.8 %all-to-all-start.1 = ((bf16[32,72,128]{2,1,0:T(8,128)(2,1)}), bf16[32,72,128]{2,1,0:T(8,128)(2,1)S(1)}, u32[]{:S(2)}, u32[]{:S(2)}) async-start(bf16[32,72,128]{2,1,0:T(8,128)(2,1)} %bitcast.3), calls=%async_computation.1 | async-start | bytes 1179648 | tf_op jit(solution)/shard_map/sum_req/all_to_all | solution.py:342
  57.5 0.7 all-gather.8.cloned.1.call-update
  58.2 14.8 %all-to-all-done.1.in_ref = bf16[32,72,128]{2,1,0:T(8,128)(2,1)S(1)} async-done(((bf16[32,72,128]{2,1,0:T(8,128)(2,1)}), bf16[32,72,128]{2,1,0:T(8,128)(2,1)S(1)}, u32[]{:S(2)}, u32[]{:S(2)}) %all-to-all-start.1) | async-done | bytes 589856 | tf_op jit(solution)/shard_map/sum_req/all_to_all | solution.py:342
  73.0 0.7 sum_req.1
  73.7 4.9 %all-gather.4.pair_ref = f32[2,12,128]{2,1,0:T(8,128)S(1)} all-gather(f32[1,12,128]{2,1,0:T(8,128)S(1)} %bitcast.35), channel_id=3, replica_groups=mesh['y'=8,'core'=2,'x1'=2,'x0'=2,'z2'=2,'z1'=2,'z0'=2] {'core'}, dimensions={0}, use_global_device_ids=true | all-gather | bytes 18432 | tf_op jit(solution)/shard_map/scan/all_gather | solution.py:357
  78.6 2.5 %scan.1 = (f32[12,1024]{1,0:T(8,128)S(1)}, f32[12,128]{1,0:T(8,128)S(1)}, f32[3,1024,128]{2,1,0:T(8,128)}, bf16[3,3,1024]{2,1,0:T(4,128)(2,1)}) custom-call(f32[12,1024]{1,0:T(8,128)S(1)} %get-tuple-element.13.gate_ref, f32[12,1024]{1,0:T(8,128)S(1)} %get-tuple-element.14.inner_ref, f32[12,128]{1,0:T(8,128)S(1)} %get-tuple-element.15.step_ref, ...), custom_call_target="tpu_custom_call" | custom-call | tf_op jit(solution)/shard_map/scan/pallas_call | solution.py:358
  81.2 1.8 %all-gather.5.squares_ref = f32[2,12,128]{2,1,0:T(8,128)S(1)} all-gather(f32[1,12,128]{2,1,0:T(8,128)S(1)} %bitcast.34), channel_id=4, replica_groups=mesh['y'=8,'core'=2,'x1'=2,'x0'=2,'z2'=2,'z1'=2,'z0'=2] {'core'}, dimensions={0}, use_global_device_ids=true | all-gather | bytes 18432 | tf_op jit(solution)/shard_map/normalise/all_gather | solution.py:386
  83.0 0.8 normalise.1
  83.8 5.0 %all-to-all-start.2 = ((bf16[16,24,512]{2,1,0:T(8,128)(2,1)}), bf16[16,24,512]{2,1,0:T(8,128)(2,1)S(1)}, u32[]{:S(2)}, u32[]{:S(2)}) async-start(bf16[16,24,512]{2,1,0:T(8,128)(2,1)} %normalise.1), calls=%async_computation.2 | async-start | bytes 786432 | tf_op jit(solution)/shard_map/gather_normed/all_to_all | solution.py:393
  88.8 0.7 all-gather.8.cloned.1.call-done
  89.5 13.4 %all-to-all-done.2.in_ref = bf16[16,24,512]{2,1,0:T(8,128)(2,1)S(1)} async-done(((bf16[16,24,512]{2,1,0:T(8,128)(2,1)}), bf16[16,24,512]{2,1,0:T(8,128)(2,1)S(1)}, u32[]{:S(2)}, u32[]{:S(2)}) %all-to-all-start.2) | async-done | bytes 393248 | tf_op jit(solution)/shard_map/gather_normed/all_to_all | solution.py:393
  102.9 1.2 copy-done.1
  104.8 18.9 %all_to_all.20.in_ref = bf16[32,24,128]{2,1,0:T(8,128)(2,1)S(1)} all-to-all(bf16[32,24,128]{2,1,0:T(8,128)(2,1)S(1)} %bitcast.32), channel_id=1, replica_groups=mesh['y'=8,'core'=2,'x1'=2,'x0'=2,'z2'=2,'z1'=2,'z0'=2] {'y','core','z0'}, dimensions={0} | all-to-all | bytes 393216 | tf_op jit(solution)/shard_map/sum_head/all_to_all | solution.py:408
  (43 shorter events, 1.8 us)
Async XLA Ops:
  7.2 0.7 copy-start.4
  7.9 11.7 %copy-start.13 = (bf16[256,2,1024]{2,1,0:T(2,128)(2,1)S(1)}, bf16[256,2,1024]{2,1,0:T(2,128)(2,1)}, u32[]{:S(2)}) copy-start(bf16[256,2,1024]{2,1,0:T(2,128)(2,1)} %param.17) | copy-start | bytes 3145732
  8.7 20.1 %copy-start.15 = (bf16[256,16]{0,1:T(8,128)(2,1)S(1)}, bf16[256,16]{0,1:T(8,128)(2,1)}, u32[]{:S(2)}) copy-start(bf16[256,16]{0,1:T(8,128)(2,1)} %param.18) | copy-start | bytes 24580
  8.7 31.9 %all-to-all-start = ((bf16[32,24,256]{2,1,0:T(8,128)(2,1)}), bf16[32,24,256]{2,1,0:T(8,128)(2,1)S(1)}, u32[]{:S(2)}, u32[]{:S(2)}) async-start(bf16[32,24,256]{2,1,0:T(8,128)(2,1)} %gather_tokens.1), calls=%async_computation | async-start | bytes 786432 | tf_op jit(solution)/shard_map/gather_tokens/all_to_all | solution.py:329
  19.6 9.4 %copy-start.14 = (bf16[256,128]{1,0:T(8,128)(2,1)S(1)}, bf16[256,128]{1,0:T(8,128)(2,1)}, u32[]{:S(2)}) copy-start(bf16[256,128]{1,0:T(8,128)(2,1)} %param.19) | copy-start | bytes 196612
  20.4 11.4 %collective-permute-start = (bf16[256,2,256]{2,1,0:T(2,128)(2,1)S(1)}, bf16[256,2,256]{2,1,0:T(2,128)(2,1)S(1)}, u32[]{:S(2)}, u32[]{:S(2)}) collective-permute-start(bf16[256,2,256]{2,1,0:T(2,128)(2,1)S(1)} %get-tuple-element.23), channel_id=1, source_target_pairs={{0,1},{1,0},{8,9},{9,8},{2,3},{3,2},{10,11},{11,10},{4,5},{5,4},{1... | collective-permute-start | bytes 786440 | tf_op jit(solution)/shard_map/move_weights/ppermute | solution.py:314
  23.5 17.0 %collective-permute-start.1 = (bf16[256,2,256]{2,1,0:T(2,128)(2,1)S(1)}, bf16[256,2,256]{2,1,0:T(2,128)(2,1)S(1)}, u32[]{:S(2)}, u32[]{:S(2)}) collective-permute-start(bf16[256,2,256]{2,1,0:T(2,128)(2,1)S(1)} %get-tuple-element.25), channel_id=1, source_target_pairs={{0,8},{1,9},{8,0},{9,1},{2,10},{3,11},{10,2},{11,3},{4,12},{5,13},... | collective-permute-start | bytes 786440 | tf_op jit(solution)/shard_map/move_weights/ppermute | solution.py:314
  26.6 13.9 %collective-permute-start.2 = (bf16[256,2,256]{2,1,0:T(2,128)(2,1)S(1)}, bf16[256,2,256]{2,1,0:T(2,128)(2,1)S(1)}, u32[]{:S(2)}, u32[]{:S(2)}) collective-permute-start(bf16[256,2,256]{2,1,0:T(2,128)(2,1)S(1)} %get-tuple-element.22), channel_id=1, source_target_pairs={{0,9},{1,8},{8,1},{9,0},{2,11},{3,10},{10,3},{11,2},{4,13},{5,12},... | collective-permute-start | bytes 786440 | tf_op jit(solution)/shard_map/move_weights/ppermute | solution.py:314
  44.0 29.0 %copy-start.7 = (bf16[3,3,128]{2,1,0:T(4,128)(2,1)S(1)}, bf16[3,3,128]{2,1,0:T(4,128)(2,1)}, u32[]{:S(2)}) copy-start(bf16[3,3,128]{2,1,0:T(4,128)(2,1)} %hist_ref.2) | copy-start | bytes 6916
  44.0 29.0 %copy-start.8 = (f32[4,128]{1,0:T(4,128)S(1)}, f32[4,128]{1,0:T(4,128)}, u32[]{:S(2)}) copy-start(f32[4,128]{1,0:T(4,128)} %taps_ref.2) | copy-start | bytes 6148
  44.0 29.0 %copy-start.12 = (f32[128]{0:T(128)S(1)}, f32[128]{0:T(128)}, u32[]{:S(2)}) copy-start(f32[128]{0:T(128)} %param.25) | copy-start | bytes 1540
  45.6 33.0 %copy-start = (f32[3,16,64,128]{3,2,1,0:T(8,128)S(1)}, f32[3,16,64,128]{3,2,1,0:T(8,128)}, u32[]{:S(2)}) copy-start(f32[3,16,64,128]{3,2,1,0:T(8,128)} %param.31) | copy-start | bytes 4718596
  45.6 33.0 %copy-start.2 = (bf16[3,3,1024]{2,1,0:T(4,128)(2,1)S(1)}, bf16[3,3,1024]{2,1,0:T(4,128)(2,1)}, u32[]{:S(2)}) copy-start(bf16[3,3,1024]{2,1,0:T(4,128)(2,1)} %hist_ref.3) | copy-start | bytes 55300
  45.6 33.0 %copy-start.3 = (f32[4,1024]{1,0:T(4,128)S(1)}, f32[4,1024]{1,0:T(4,128)}, u32[]{:S(2)}) copy-start(f32[4,1024]{1,0:T(4,128)} %taps_ref.3) | copy-start | bytes 49156
  45.6 33.0 %copy-start.5 = (f32[1024]{0:T(1024)S(1)}, f32[1024]{0:T(1024)}, u32[]{:S(2)}) copy-start(f32[1024]{0:T(1024)} %param.23) | copy-start | bytes 12292
  45.6 33.0 %copy-start.9 = (f32[16]{0:T(128)S(1)}, f32[16]{0:T(128)}, u32[]{:S(2)}) copy-start(f32[16]{0:T(128)} %param.26) | copy-start | bytes 196
  45.6 33.0 %copy-start.10 = (f32[16]{0:T(128)S(1)}, f32[16]{0:T(128)}, u32[]{:S(2)}) copy-start(f32[16]{0:T(128)} %param.27) | copy-start | bytes 196
  45.6 33.0 %copy-start.11 = (f32[16]{0:T(128)S(1)}, f32[16]{0:T(128)}, u32[]{:S(2)}) copy-start(f32[16]{0:T(128)} %param.28) | copy-start | bytes 196
  45.6 27.4 %all-to-all-start.1 = ((bf16[32,72,128]{2,1,0:T(8,128)(2,1)}), bf16[32,72,128]{2,1,0:T(8,128)(2,1)S(1)}, u32[]{:S(2)}, u32[]{:S(2)}) async-start(bf16[32,72,128]{2,1,0:T(8,128)(2,1)} %bitcast.3), calls=%async_computation.1 | async-start | bytes 1179648 | tf_op jit(solution)/shard_map/sum_req/all_to_all | solution.py:342
  57.4 25.5 %copy-start.6 = (f32[1024]{0:T(1024)S(1)}, f32[1024]{0:T(1024)}, u32[]{:S(2)}) copy-start(f32[1024]{0:T(1024)} %param.29) | copy-start | bytes 12292
  57.4 32.1 %all-gather.8.cloned.1.call-start = ((), (), s32[]{:S(2)}) async-start(), calls=%async_computation.4 | async-start | bytes 1572864 | tf_op jit(solution)/shard_map/move_out_weight/all_gather | solution.py:321
  83.8 19.1 %all-to-all-start.2 = ((bf16[16,24,512]{2,1,0:T(8,128)(2,1)}), bf16[16,24,512]{2,1,0:T(8,128)(2,1)S(1)}, u32[]{:S(2)}, u32[]{:S(2)}) async-start(bf16[16,24,512]{2,1,0:T(8,128)(2,1)} %normalise.1), calls=%async_computation.2 | async-start | bytes 786432 | tf_op jit(solution)/shard_map/gather_normed/all_to_all | solution.py:393
  102.9 1.2 copy-start.1
Sparse Core Ops, SparseCore 0:
  60.4 29.1 all-gather.7

commit v5 on v4

--- a/solution.py
+++ b/solution.py
@@ -34,6 +34,7 @@
 
 WHOLE = pl.BlockSpec(memory_space=pltpu.VMEM)
 SCALARS = pl.BlockSpec(memory_space=pltpu.SMEM)
+UNREAD = pl.BlockSpec(memory_space=pl.ANY)
 
 
 def call(body, out_shape, scratch=(), in_specs=None):
@@ -48,7 +49,7 @@
     )
 
 
-def copy_tokens(in_ref, out_ref, flat):
+def copy_tokens(in_ref, _first, _second, out_ref, flat):
     requests, steps, _ = in_ref.shape
     for req in range(requests):
         flat[req * steps : (req + 1) * steps, :] = in_ref[req].astype(F32)
@@ -246,7 +247,7 @@
         new_state_ref[req] = both[:, state_size:] * state + both[:, 0:state_size]
 
 
-def normalise(group_width, gated_ref, squares_ref, gain_ref, out_ref, rows_two):
+def normalise(group_width, gated_ref, squares_ref, gain_ref, _, out_ref, rows_two):
     rows, width = gated_ref.shape
     half = width // 2
     mean = (squares_ref[0] + squares_ref[1])[:, 0:1] / group_width
@@ -258,14 +259,14 @@
         out_ref[copy] = block
 
 
-def project_out(in_ref, weights_ref, out_ref, first, second, sums):
+def project_out(side_ref, in_ref, own_ref, other_ref, out_ref, first, second, sums):
     blocks, block_rows, half = in_ref.shape
     rows = block_rows // 2
     lanes = out_ref.shape[-1]
     flat = in_ref[...].reshape(blocks * block_rows, half)
-    for side in range(weights_ref.shape[0]):
-        first[...] = jnp.dot(flat, weights_ref[side, 0:half, :], preferred_element_type=F32)
-        second[...] = jnp.dot(flat, weights_ref[side, half:, :], preferred_element_type=F32)
+    for weight_ref, side in ((own_ref, side_ref[0]), (other_ref, 1 - side_ref[0])):
+        first[...] = jnp.dot(flat, weight_ref[0:half, :], preferred_element_type=F32)
+        second[...] = jnp.dot(flat, weight_ref[half:, :], preferred_element_type=F32)
         for block in range(blocks):
             at = block * block_rows
             total = first[at : at + rows, :] + second[at + rows : at + block_rows, :]
@@ -303,7 +304,7 @@
     chunk = width // SQUARE
     with jax.named_scope("move_weights"):
         here = lax.axis_index(SQUARE_AXES)
-        chunks = []
+        chunks, moved = [], []
         for flip in range(SQUARE):
             target = jnp.bitwise_xor(here, flip)
             part = lax.dynamic_slice(
@@ -312,20 +313,23 @@
             if flip:
                 route = [(at, at ^ flip) for at in range(SQUARE)]
                 part = lax.ppermute(part, SQUARE_AXES, route)
+                moved.append(part)
             chunks.append(part.reshape(features, 2 * chunk))
         extra = jnp.concatenate(
             [bc_weight, step_weight, jnp.zeros((features, lanes - heads), BF16)], axis=1
         )
 
     with jax.named_scope("move_out_weight"):
-        pair_weights = lax.all_gather(out_weight, PAIR_AXIS, axis=0, tiled=False)
+        side = lax.axis_index(PAIR_AXIS)
+        other_weight = lax.ppermute(out_weight, PAIR_AXIS, [(0, 1), (1, 0)])
 
     with jax.named_scope("gather_tokens"):
         own = call(
             copy_tokens,
             sds((SQUARE * Y_SIZE, rows_head * steps, features), BF16),
             [pltpu.VMEM((rows_head * steps, features), F32)],
-        )(jnp.transpose(tokens, (1, 0, 2)))
+            [WHOLE, UNREAD, UNREAD],
+        )(jnp.transpose(tokens, (1, 0, 2)), *moved[:2])
         gathered = lax.all_to_all(own, SQUARE_AXES + ("y",), 0, 0, tiled=True)
         gathered = lax.all_gather(gathered, "core", axis=0, tiled=False)
 
@@ -388,7 +392,8 @@
             functools.partial(normalise, CORE_SIZE * width),
             sds((REST, 2 * rows, width // 2), BF16),
             [pltpu.VMEM((2 * rows, width // 2), F32)],
-        )(gated, squares_pair, norm_gain[None])
+            [WHOLE] * 3 + [UNREAD],
+        )(gated, squares_pair, norm_gain[None], other_weight)
     with jax.named_scope("gather_normed"):
         some_rows = lax.all_to_all(normed, REST_AXES, 0, 0, tiled=True)
     with jax.named_scope("project_out"):
@@ -402,7 +407,8 @@
                 pltpu.VMEM((REST * 2 * rows, out_columns), F32),
                 pltpu.VMEM(block, F32),
             ],
-        )(some_rows, pair_weights)
+            [SCALARS] + [WHOLE] * 3,
+        )(side.astype(jnp.int32).reshape(1), some_rows, out_weight, other_weight)
     with jax.named_scope("sum_head"):
         blocks = product.reshape((2 * REST,) + block[2:])
         blocks = lax.all_to_all(blocks, HEAD_AXES + (PAIR_AXIS,), 0, 0, tiled=True)

time: 132 us -> 126 us (0.955)
  blocking collectives: 29 us -> 53.4 us
  waiting for transfers between devices: 41 us -> 25 us
  between operations: 14.3 us -> 0.9 us
    all_to_all x0 -> x1, blocking collectives: none -> 22.5 us  [shards(): some_rows = lax.all_to_all(normed, REST_AXES, 0, 0, tiled=True)]
    all_to_all x1 -> x0, waiting for transfers between devices: 13.4 us -> none  [shards(): some_rows = lax.all_to_all(normed, REST_AXES, 0, 0, tiled=True)]
    all_to_all x1 -> x0, starting transfers between devices: 4.97 us -> none  [shards(): some_rows = lax.all_to_all(normed, REST_AXES, 0, 0, tiled=True)]
    ppermute x3, starting transfers between devices: 8.37 us -> 12.2 us  [shards(): part = lax.ppermute(part, SQUARE_AXES, route)]
    ppermute x0 -> x1, starting transfers between devices: none -> 3.14 us  [shards(): other_weight = lax.ppermute(out_weight, PAIR_AXIS, [(0, 1), (1, 0)])]
    all_to_all x1, waiting for transfers between devices: 14.8 us -> 12.1 us  [shards(): lax.all_to_all(messages.reshape(req_count, tiles * rows, lanes), REQ_AXES...]
    unnamed x37 -> x35, local copies, waits for them, and re-layouts: 2.24 us -> 0.33 us
    ppermute x3, waiting for transfers between devices: 11.4 us -> 12.9 us  [shards(): part = lax.ppermute(part, SQUARE_AXES, route)]
  transfers between devices with their start and end apart: 7 -> 6, of which waited for: 5 -> 4; matrix products, arithmetic and copies ran while one was open for 1% -> 0% of each run, Pallas kernels for 3% -> 3%
where the time goes in v5:
time: 126 us; the launch traced here: 125 us
  blocking collectives  53.4 us (42%)
  starting transfers between devices  36.6 us (29%)
  waiting for transfers between devices  25 us (20%)
  Pallas kernels  6.96 us (6%)
  local copies, waits for them, and re-layouts  2.32 us (2%)
    all_to_all x1, blocking collectives, shards(): some_rows = lax.all_to_all(normed, REST_AXES, 0, 0, tiled=True)  22.5 us
    all_to_all x1, blocking collectives, shards(): blocks = lax.all_to_all(blocks, HEAD_AXES + (PAIR_AXIS,), 0, 0, tiled=True)  19.2 us
    ppermute x3, waiting for transfers between devices, shards(): part = lax.ppermute(part, SQUARE_AXES, route)  12.9 us
    ppermute x3, starting transfers between devices, shards(): part = lax.ppermute(part, SQUARE_AXES, route)  12.2 us
    all_to_all x1, waiting for transfers between devices, shards(): lax.all_to_all(messages.reshape(req_count, tiles * rows, lanes), REQ_AXES...  12.1 us
    all_to_all x1, starting transfers between devices, shards(): lax.all_to_all(messages.reshape(req_count, tiles * rows, lanes), REQ_AXES...  11.8 us
    all_to_all x1, starting transfers between devices, shards(): gathered = lax.all_to_all(own, SQUARE_AXES + ('y',), 0, 0, tiled=True)  9.52 us
    all_gather x1, blocking collectives, shards(): pair = lax.all_gather(bc_conv, 'core', axis=0, tiled=False)  5.62 us
  transfers between devices with their start and end apart: 6, of which 4 were waited for; matrix products, arithmetic and copies ran while one was open for 0% of the time, Pallas kernels for 3%

profile of v5, /device:TPU:1, one launch (start us, length us, event | category | flops | bytes accessed | tf_op | source)
XLA Modules:
  0.0 125.2 jit_solution(17181455817860058858)
XLA Ops:
  0.7 1.9 %constant_dynamic-slice_fusion = (bf16[256,2,256]{2,1,0:T(2,128)(2,1)S(1)}, bf16[256,2,256]{2,1,0:T(2,128)(2,1)S(1)}, bf16[256,2,256]{2,1,0:T(2,128)(2,1)S(1)}, bf16[256,2,256]{2,1,0:T(2,128)(2,1)S(1)}) fusion(bf16[256,2,1024]{2,1,0:T(2,128)(2,1)} %param.17, s32[]{:T(128)S(6)} %select_n.15, s32[]{:T(128)S(6)} %select_n.13, s32[]{:T(128)S(6)} %select_n.12, ...), kind=kLoop, calls=%fused_computation.1 | loop fusion | bytes 2097168 | tf_op jit(solution)/shard_map/move_weights/dynamic_slice | solution.py:310
  2.6 5.0 %collective-permute-start = (bf16[256,2,256]{2,1,0:T(2,128)(2,1)S(1)}, bf16[256,2,256]{2,1,0:T(2,128)(2,1)S(1)}, u32[]{:S(2)}, u32[]{:S(2)}) collective-permute-start(bf16[256,2,256]{2,1,0:T(2,128)(2,1)S(1)} %get-tuple-element.24), channel_id=1, source_target_pairs={{0,1},{1,0},{8,9},{9,8},{2,3},{3,2},{10,11},{11,10},{4,5},{5,4},{1... | collective-permute-start | bytes 786440 | tf_op jit(solution)/shard_map/move_weights/ppermute | solution.py:315
  7.6 3.1 %collective-permute-start.1 = (bf16[256,2,256]{2,1,0:T(2,128)(2,1)S(1)}, bf16[256,2,256]{2,1,0:T(2,128)(2,1)S(1)}, u32[]{:S(2)}, u32[]{:S(2)}) collective-permute-start(bf16[256,2,256]{2,1,0:T(2,128)(2,1)S(1)} %get-tuple-element.23), channel_id=1, source_target_pairs={{0,8},{1,9},{8,0},{9,1},{2,10},{3,11},{10,2},{11,3},{4,12},{5,13},... | collective-permute-start | bytes 786440 | tf_op jit(solution)/shard_map/move_weights/ppermute | solution.py:315
  10.7 0.6 collective-permute-done._first
  11.3 3.7 %collective-permute-done.1._second = bf16[256,2,256]{2,1,0:T(2,128)(2,1)S(1)} collective-permute-done((bf16[256,2,256]{2,1,0:T(2,128)(2,1)S(1)}, bf16[256,2,256]{2,1,0:T(2,128)(2,1)S(1)}, u32[]{:S(2)}, u32[]{:S(2)}) %collective-permute-start.1) | collective-permute-done | bytes 262176 | tf_op jit(solution)/shard_map/move_weights/ppermute | solution.py:315
  15.0 0.8 gather_tokens.1
  15.8 9.5 %all-to-all-start = ((bf16[32,24,256]{2,1,0:T(8,128)(2,1)}), bf16[32,24,256]{2,1,0:T(8,128)(2,1)S(1)}, u32[]{:S(2)}, u32[]{:S(2)}) async-start(bf16[32,24,256]{2,1,0:T(8,128)(2,1)} %gather_tokens.1), calls=%async_computation | async-start | bytes 786432 | tf_op jit(solution)/shard_map/gather_tokens/all_to_all | solution.py:333
  25.3 4.1 %collective-permute-start.2 = (bf16[256,2,256]{2,1,0:T(2,128)(2,1)S(1)}, bf16[256,2,256]{2,1,0:T(2,128)(2,1)S(1)}, u32[]{:S(2)}, u32[]{:S(2)}) collective-permute-start(bf16[256,2,256]{2,1,0:T(2,128)(2,1)S(1)} %get-tuple-element.22), channel_id=1, source_target_pairs={{0,9},{1,8},{8,1},{9,0},{2,11},{3,10},{10,3},{11,2},{4,13},{5,12},... | collective-permute-start | bytes 786440 | tf_op jit(solution)/shard_map/move_weights/ppermute | solution.py:315
  29.4 0.1 copy.21
  29.8 8.6 %collective-permute-done.2 = bf16[256,2,256]{2,1,0:T(2,128)(2,1)S(1)} collective-permute-done((bf16[256,2,256]{2,1,0:T(2,128)(2,1)S(1)}, bf16[256,2,256]{2,1,0:T(2,128)(2,1)S(1)}, u32[]{:S(2)}, u32[]{:S(2)}) %collective-permute-start.2) | collective-permute-done | bytes 262176 | tf_op jit(solution)/shard_map/move_weights/ppermute | solution.py:315
  38.4 4.3 %all-gather = bf16[64,24,256]{2,1,0:T(8,128)(2,1)S(1)} all-gather(bf16[32,24,256]{2,1,0:T(8,128)(2,1)S(1)} %all-to-all-done), channel_id=2, replica_groups=mesh['y'=8,'core'=2,'x1'=2,'x0'=2,'z2'=2,'z1'=2,'z0'=2] {'core'}, dimensions={0}, use_global_device_ids=true | all-gather | bytes 1179648 | tf_op jit(solution)/shard_map/gather_tokens/all_gather | solution.py:334
  42.8 1.5 %project.1 = bf16[2304,128]{1,0:T(8,128)(2,1)} custom-call(s32[1]{0:T(128)} %bitcast.1.here_ref, bf16[2,32,24,256]{3,2,1,0:T(8,128)(2,1)S(1)} %bitcast.25, bf16[256,512]{1,0:T(8,128)(2,1)S(1)} %bitcast.29, bf16[256,512]{1,0:T(8,128)(2,1)S(1)} %bitcast.30, bf16[256,512]{1,0:T(8,128)(2,1)S(1)} %bitcast.31, bf16[256,512]{1,0:T(8,128)(2,1)S(1)} %bitcast.32, ...), custom_call_target="tpu_custom_call" | custom-call | tf_op jit(solution)/shard_map/project/pallas_call | solution.py:339
  44.3 11.8 %all-to-all-start.1 = ((bf16[32,72,128]{2,1,0:T(8,128)(2,1)}), bf16[32,72,128]{2,1,0:T(8,128)(2,1)S(1)}, u32[]{:S(2)}, u32[]{:S(2)}) async-start(bf16[32,72,128]{2,1,0:T(8,128)(2,1)} %bitcast.4), calls=%async_computation.1 | async-start | bytes 1179648 | tf_op jit(solution)/shard_map/sum_req/all_to_all | solution.py:346
  56.1 3.1 %collective-permute-start.3 = (bf16[1024,256]{1,0:T(8,128)(2,1)S(1)}, bf16[1024,256]{1,0:T(8,128)(2,1)S(1)}, u32[]{:S(2)}, u32[]{:S(2)}) collective-permute-start(bf16[1024,256]{1,0:T(8,128)(2,1)S(1)} %copy-done.1), channel_id=1, source_target_pairs={{0,1},{1,0},{2,3},{3,2},{4,5},{5,4},{6,7},{7,6},{8,9},{9,8},{10,11... | collective-permute-start | bytes 1572872 | tf_op jit(solution)/shard_map/move_out_weight/ppermute | solution.py:324
  59.3 12.1 %all-to-all-done.1.in_ref = bf16[32,72,128]{2,1,0:T(8,128)(2,1)S(1)} async-done(((bf16[32,72,128]{2,1,0:T(8,128)(2,1)}), bf16[32,72,128]{2,1,0:T(8,128)(2,1)S(1)}, u32[]{:S(2)}, u32[]{:S(2)}) %all-to-all-start.1) | async-done | bytes 589856 | tf_op jit(solution)/shard_map/sum_req/all_to_all | solution.py:346
  71.4 0.7 sum_req.1
  72.0 5.6 %all-gather.3.pair_ref = f32[2,12,128]{2,1,0:T(8,128)S(1)} all-gather(f32[1,12,128]{2,1,0:T(8,128)S(1)} %bitcast.36), channel_id=3, replica_groups=mesh['y'=8,'core'=2,'x1'=2,'x0'=2,'z2'=2,'z1'=2,'z0'=2] {'core'}, dimensions={0}, use_global_device_ids=true | all-gather | bytes 18432 | tf_op jit(solution)/shard_map/scan/all_gather | solution.py:361
  77.7 2.5 %scan.1 = (f32[12,1024]{1,0:T(8,128)S(1)}, f32[12,128]{1,0:T(8,128)S(1)}, f32[3,1024,128]{2,1,0:T(8,128)}, bf16[3,3,1024]{2,1,0:T(4,128)(2,1)}) custom-call(f32[12,1024]{1,0:T(8,128)S(1)} %get-tuple-element.13.gate_ref, f32[12,1024]{1,0:T(8,128)S(1)} %get-tuple-element.14.inner_ref, f32[12,128]{1,0:T(8,128)S(1)} %get-tuple-element.15.step_ref, ...), custom_call_target="tpu_custom_call" | custom-call | tf_op jit(solution)/shard_map/scan/pallas_call | solution.py:362
  80.3 1.8 %all-gather.4.squares_ref = f32[2,12,128]{2,1,0:T(8,128)S(1)} all-gather(f32[1,12,128]{2,1,0:T(8,128)S(1)} %bitcast.35), channel_id=4, replica_groups=mesh['y'=8,'core'=2,'x1'=2,'x0'=2,'z2'=2,'z1'=2,'z0'=2] {'core'}, dimensions={0}, use_global_device_ids=true | all-gather | bytes 18432 | tf_op jit(solution)/shard_map/normalise/all_gather | solution.py:390
  82.1 0.1 normalise.1
  82.2 22.5 %all_to_all.20.in_ref = bf16[16,24,512]{2,1,0:T(8,128)(2,1)S(1)} all-to-all(bf16[16,24,512]{2,1,0:T(8,128)(2,1)S(1)} %normalise.1), channel_id=1, replica_groups=mesh['y'=8,'core'=2,'x1'=2,'x0'=2,'z2'=2,'z1'=2,'z0'=2] {'x1','x0','z2',..., dimensions={0} | all-to-all | bytes 786432 | tf_op jit(solution)/shard_map/gather_normed/all_to_all | solution.py:398
  104.7 0.7 project_out.1
  105.3 19.2 %all_to_all.21.in_ref = bf16[32,24,128]{2,1,0:T(8,128)(2,1)S(1)} all-to-all(bf16[32,24,128]{2,1,0:T(8,128)(2,1)S(1)} %bitcast.33), channel_id=1, replica_groups=mesh['y'=8,'core'=2,'x1'=2,'x0'=2,'z2'=2,'z1'=2,'z0'=2] {'y','core','z0'}, dimensions={0} | all-to-all | bytes 393216 | tf_op jit(solution)/shard_map/sum_head/all_to_all | solution.py:414
  124.5 0.6 sum_head.1
  (39 shorter events, 0.3 us)
Async XLA Ops:
  0.6 14.4 %copy-start.4 = (bf16[4,6,256]{2,0,1:T(4,128)(2,1)S(1)}, bf16[4,6,256]{2,0,1:T(4,128)(2,1)}, u32[]{:S(2)}) copy-start(bf16[4,6,256]{2,0,1:T(4,128)(2,1)} %param.16) | copy-start | bytes 36868
  2.6 26.9 %copy-start.14 = (bf16[256,16]{0,1:T(8,128)(2,1)S(1)}, bf16[256,16]{0,1:T(8,128)(2,1)}, u32[]{:S(2)}) copy-start(bf16[256,16]{0,1:T(8,128)(2,1)} %param.18) | copy-start | bytes 24580
  2.6 27.1 %copy-start.13 = (bf16[256,128]{1,0:T(8,128)(2,1)S(1)}, bf16[256,128]{1,0:T(8,128)(2,1)}, u32[]{:S(2)}) copy-start(bf16[256,128]{1,0:T(8,128)(2,1)} %param.19) | copy-start | bytes 196612
  2.6 8.7 %collective-permute-start = (bf16[256,2,256]{2,1,0:T(2,128)(2,1)S(1)}, bf16[256,2,256]{2,1,0:T(2,128)(2,1)S(1)}, u32[]{:S(2)}, u32[]{:S(2)}) collective-permute-start(bf16[256,2,256]{2,1,0:T(2,128)(2,1)S(1)} %get-tuple-element.24), channel_id=1, source_target_pairs={{0,1},{1,0},{8,9},{9,8},{2,3},{3,2},{10,11},{11,10},{4,5},{5,4},{1... | collective-permute-start | bytes 786440 | tf_op jit(solution)/shard_map/move_weights/ppermute | solution.py:315
  7.6 7.4 %collective-permute-start.1 = (bf16[256,2,256]{2,1,0:T(2,128)(2,1)S(1)}, bf16[256,2,256]{2,1,0:T(2,128)(2,1)S(1)}, u32[]{:S(2)}, u32[]{:S(2)}) collective-permute-start(bf16[256,2,256]{2,1,0:T(2,128)(2,1)S(1)} %get-tuple-element.23), channel_id=1, source_target_pairs={{0,8},{1,9},{8,0},{9,1},{2,10},{3,11},{10,2},{11,3},{4,12},{5,13},... | collective-permute-start | bytes 786440 | tf_op jit(solution)/shard_map/move_weights/ppermute | solution.py:315
  15.8 22.6 %all-to-all-start = ((bf16[32,24,256]{2,1,0:T(8,128)(2,1)}), bf16[32,24,256]{2,1,0:T(8,128)(2,1)S(1)}, u32[]{:S(2)}, u32[]{:S(2)}) async-start(bf16[32,24,256]{2,1,0:T(8,128)(2,1)} %gather_tokens.1), calls=%async_computation | async-start | bytes 786432 | tf_op jit(solution)/shard_map/gather_tokens/all_to_all | solution.py:333
  25.3 13.1 %collective-permute-start.2 = (bf16[256,2,256]{2,1,0:T(2,128)(2,1)S(1)}, bf16[256,2,256]{2,1,0:T(2,128)(2,1)S(1)}, u32[]{:S(2)}, u32[]{:S(2)}) collective-permute-start(bf16[256,2,256]{2,1,0:T(2,128)(2,1)S(1)} %get-tuple-element.22), channel_id=1, source_target_pairs={{0,9},{1,8},{8,1},{9,0},{2,11},{3,10},{10,3},{11,2},{4,13},{5,12},... | collective-permute-start | bytes 786440 | tf_op jit(solution)/shard_map/move_weights/ppermute | solution.py:315
  42.7 13.4 %copy-start.1 = (bf16[1024,256]{1,0:T(8,128)(2,1)S(1)}, bf16[1024,256]{1,0:T(8,128)(2,1)}, u32[]{:S(2)}) copy-start(bf16[1024,256]{1,0:T(8,128)(2,1)} %own_ref.1) | copy-start | bytes 1572868
  42.7 28.6 %copy-start.7 = (bf16[3,3,128]{2,1,0:T(4,128)(2,1)S(1)}, bf16[3,3,128]{2,1,0:T(4,128)(2,1)}, u32[]{:S(2)}) copy-start(bf16[3,3,128]{2,1,0:T(4,128)(2,1)} %hist_ref.2) | copy-start | bytes 6916
  42.7 28.6 %copy-start.8 = (f32[4,128]{1,0:T(4,128)S(1)}, f32[4,128]{1,0:T(4,128)}, u32[]{:S(2)}) copy-start(f32[4,128]{1,0:T(4,128)} %taps_ref.2) | copy-start | bytes 6148
  42.7 28.6 %copy-start.12 = (f32[128]{0:T(128)S(1)}, f32[128]{0:T(128)}, u32[]{:S(2)}) copy-start(f32[128]{0:T(128)} %param.25) | copy-start | bytes 1540
  42.7 34.9 %copy-start = (f32[3,16,64,128]{3,2,1,0:T(8,128)S(1)}, f32[3,16,64,128]{3,2,1,0:T(8,128)}, u32[]{:S(2)}) copy-start(f32[3,16,64,128]{3,2,1,0:T(8,128)} %param.31) | copy-start | bytes 4718596
  42.7 34.9 %copy-start.2 = (bf16[3,3,1024]{2,1,0:T(4,128)(2,1)S(1)}, bf16[3,3,1024]{2,1,0:T(4,128)(2,1)}, u32[]{:S(2)}) copy-start(bf16[3,3,1024]{2,1,0:T(4,128)(2,1)} %hist_ref.3) | copy-start | bytes 55300
  42.8 34.9 %copy-start.3 = (f32[4,1024]{1,0:T(4,128)S(1)}, f32[4,1024]{1,0:T(4,128)}, u32[]{:S(2)}) copy-start(f32[4,1024]{1,0:T(4,128)} %taps_ref.3) | copy-start | bytes 49156
  42.8 34.9 %copy-start.5 = (f32[1024]{0:T(1024)S(1)}, f32[1024]{0:T(1024)}, u32[]{:S(2)}) copy-start(f32[1024]{0:T(1024)} %param.23) | copy-start | bytes 12292
  42.8 34.9 %copy-start.9 = (f32[16]{0:T(128)S(1)}, f32[16]{0:T(128)}, u32[]{:S(2)}) copy-start(f32[16]{0:T(128)} %param.26) | copy-start | bytes 196
  42.8 34.9 %copy-start.10 = (f32[16]{0:T(128)S(1)}, f32[16]{0:T(128)}, u32[]{:S(2)}) copy-start(f32[16]{0:T(128)} %param.27) | copy-start | bytes 196
  42.8 34.9 %copy-start.11 = (f32[16]{0:T(128)S(1)}, f32[16]{0:T(128)}, u32[]{:S(2)}) copy-start(f32[16]{0:T(128)} %param.28) | copy-start | bytes 196
  44.3 37.7 %copy-start.6 = (f32[1024]{0:T(1024)S(1)}, f32[1024]{0:T(1024)}, u32[]{:S(2)}) copy-start(f32[1024]{0:T(1024)} %param.29) | copy-start | bytes 12292
  44.3 27.0 %all-to-all-start.1 = ((bf16[32,72,128]{2,1,0:T(8,128)(2,1)}), bf16[32,72,128]{2,1,0:T(8,128)(2,1)S(1)}, u32[]{:S(2)}, u32[]{:S(2)}) async-start(bf16[32,72,128]{2,1,0:T(8,128)(2,1)} %bitcast.4), calls=%async_computation.1 | async-start | bytes 1179648 | tf_op jit(solution)/shard_map/sum_req/all_to_all | solution.py:346
  56.1 25.9 %collective-permute-start.3 = (bf16[1024,256]{1,0:T(8,128)(2,1)S(1)}, bf16[1024,256]{1,0:T(8,128)(2,1)S(1)}, u32[]{:S(2)}, u32[]{:S(2)}) collective-permute-start(bf16[1024,256]{1,0:T(8,128)(2,1)S(1)} %copy-done.1), channel_id=1, source_target_pairs={{0,1},{1,0},{2,3},{3,2},{4,5},{5,4},{6,7},{7,6},{8,9},{9,8},{10,11... | collective-permute-start | bytes 1572872 | tf_op jit(solution)/shard_map/move_out_weight/ppermute | solution.py:324

commit v6 on v5

--- a/solution.py
+++ b/solution.py
@@ -15,16 +15,12 @@
 HEAD_AXES = ("y", "core")
 REQ_AXES = ("x1", "x0", "z2", "z1", "z0")
 REQ_COUNT = 32
-SQUARE_AXES = ("x0", "z0")
-SQUARE = 4
+SHARE_AXIS = "x0"
+SHARE = 2
+MEMBERS = [[16 * x1 + 8 * x0 + z for x1 in range(2) for z in range(8)] for x0 in range(SHARE)]
 PAIR_AXIS = "z0"
 REST_AXES = ("x1", "x0", "z2", "z1")
 REST = 16
-MEMBERS = [
-    [16 * x1 + 8 * x0 + 2 * z_high + z0 for x1 in range(2) for z_high in range(4)]
-    for x0 in range(2)
-    for z0 in range(2)
-]
 VMEM_LIMIT = 40 * 1024 * 1024
 
 
@@ -49,7 +45,7 @@
     )
 
 
-def copy_tokens(in_ref, _first, _second, out_ref, flat):
+def copy_tokens(in_ref, out_ref, flat):
     requests, steps, _ = in_ref.shape
     for req in range(requests):
         flat[req * steps : (req + 1) * steps, :] = in_ref[req].astype(F32)
@@ -73,18 +69,18 @@
 
 
 def project(
-    here_ref, rows_ref, own_ref, first_ref, second_ref, third_ref, extra_ref, out_ref, messages
+    here_ref, rows_ref, own_ref, other_ref, extra_ref, _, out_ref, messages
 ):
     cores, per_core, block_rows, features = rows_ref.shape
-    y_count = per_core // SQUARE
+    y_count = per_core // SHARE
     rows = block_rows // 2
     lanes = out_ref.shape[1]
     tiles = out_ref.shape[0] // (REQ_COUNT * rows)
     here = here_ref[0]
     for core in range(cores):
         total = None
-        for shift, weight_ref in enumerate((own_ref, first_ref, second_ref, third_ref)):
-            source = jnp.bitwise_xor(here, shift)
+        for shift, weight_ref in enumerate((own_ref, other_ref)):
+            source = 1 - here if shift else here
             block = rows_ref[core, pl.ds(source * y_count, y_count)]
             block = block.reshape(y_count * block_rows, features)
             part = jnp.dot(block, weight_ref[...], preferred_element_type=F32)
@@ -117,16 +113,16 @@
     requests, history, lanes = hist_ref.shape
     rows = gate_ref.shape[0]
     steps = rows // requests
-    chunk = gate_ref.shape[1] // SQUARE
+    chunk = gate_ref.shape[1] // SHARE
     tiles = chunk // lanes
     extra = None
-    for square, members in enumerate(MEMBERS):
+    for share, members in enumerate(MEMBERS):
         total = in_ref[members[0]].astype(F32)
         for member in members[1:]:
             total = total + in_ref[member].astype(F32)
         rounded = total.astype(BF16).astype(F32)
         for tile in range(tiles):
-            column = square * chunk + tile * lanes
+            column = share * chunk + tile * lanes
             gate_ref[:, column : column + lanes] = rounded[tile * rows : (tile + 1) * rows]
             at = (tiles + tile) * rows
             inner_ref[:, column : column + lanes] = rounded[at : at + rows]
@@ -247,7 +243,7 @@
         new_state_ref[req] = both[:, state_size:] * state + both[:, 0:state_size]
 
 
-def normalise(group_width, gated_ref, squares_ref, gain_ref, _, out_ref, rows_two):
+def normalise(group_width, gated_ref, squares_ref, gain_ref, out_ref, rows_two):
     rows, width = gated_ref.shape
     half = width // 2
     mean = (squares_ref[0] + squares_ref[1])[:, 0:1] / group_width
@@ -301,20 +297,15 @@
     sds = jax.ShapeDtypeStruct
 
     lanes = bc_weight.shape[1]
-    chunk = width // SQUARE
+    chunk = width // SHARE
     with jax.named_scope("move_weights"):
-        here = lax.axis_index(SQUARE_AXES)
-        chunks, moved = [], []
-        for flip in range(SQUARE):
-            target = jnp.bitwise_xor(here, flip)
-            part = lax.dynamic_slice(
-                gate_inner_weight, (0, 0, target * chunk), (features, 2, chunk)
-            )
-            if flip:
-                route = [(at, at ^ flip) for at in range(SQUARE)]
-                part = lax.ppermute(part, SQUARE_AXES, route)
-                moved.append(part)
-            chunks.append(part.reshape(features, 2 * chunk))
+        here = lax.axis_index(SHARE_AXIS)
+        own_part, other_part = (
+            lax.dynamic_slice(gate_inner_weight, (0, 0, side * chunk), (features, 2, chunk))
+            for side in (here, 1 - here)
+        )
+        other_part = lax.ppermute(other_part, SHARE_AXIS, [(0, 1), (1, 0)])
+        chunks = [part.reshape(features, 2 * chunk) for part in (own_part, other_part)]
         extra = jnp.concatenate(
             [bc_weight, step_weight, jnp.zeros((features, lanes - heads), BF16)], axis=1
         )
@@ -326,11 +317,10 @@
     with jax.named_scope("gather_tokens"):
         own = call(
             copy_tokens,
-            sds((SQUARE * Y_SIZE, rows_head * steps, features), BF16),
+            sds((SHARE * Y_SIZE, rows_head * steps, features), BF16),
             [pltpu.VMEM((rows_head * steps, features), F32)],
-            [WHOLE, UNREAD, UNREAD],
-        )(jnp.transpose(tokens, (1, 0, 2)), *moved[:2])
-        gathered = lax.all_to_all(own, SQUARE_AXES + ("y",), 0, 0, tiled=True)
+        )(jnp.transpose(tokens, (1, 0, 2)))
+        gathered = lax.all_to_all(own, (SHARE_AXIS, "y"), 0, 0, tiled=True)
         gathered = lax.all_gather(gathered, "core", axis=0, tiled=False)
 
     with jax.named_scope("project"):
@@ -340,8 +330,8 @@
             project,
             sds((message_rows, lanes), BF16),
             [pltpu.VMEM((message_rows, lanes), F32)],
-            [SCALARS] + [WHOLE] * 6,
-        )(here.astype(jnp.int32).reshape(1), gathered, *chunks, extra)
+            [SCALARS] + [WHOLE] * 4 + [UNREAD],
+        )(here.astype(jnp.int32).reshape(1), gathered, *chunks, extra, other_weight)
     with jax.named_scope("sum_req"):
         parts = lax.all_to_all(
             messages.reshape(req_count, tiles * rows, lanes), REQ_AXES, 0, 0, tiled=True
@@ -392,8 +382,7 @@
             functools.partial(normalise, CORE_SIZE * width),
             sds((REST, 2 * rows, width // 2), BF16),
             [pltpu.VMEM((2 * rows, width // 2), F32)],
-            [WHOLE] * 3 + [UNREAD],
-        )(gated, squares_pair, norm_gain[None], other_weight)
+        )(gated, squares_pair, norm_gain[None])
     with jax.named_scope("gather_normed"):
         some_rows = lax.all_to_all(normed, REST_AXES, 0, 0, tiled=True)
     with jax.named_scope("project_out"):

time: 126 us -> 116 us (0.921)
  starting transfers between devices: 36.6 us -> 18.7 us
  blocking collectives: 53.4 us -> 65.6 us
  waiting for transfers between devices: 25 us -> 20.9 us
    all_to_all x1, blocking collectives: 22.5 us -> 35.8 us  [shards(): lax.all_to_all(messages.reshape(req_count, tiles * rows, lanes), REQ_AXES...]
    ppermute x3 -> x1, waiting for transfers between devices: 12.9 us -> 0.01 us  [shards(): other_part = lax.ppermute(other_part, SHARE_AXIS, [(0, 1), (1, 0)])]
    all_to_all x2, starting transfers between devices: 21.3 us -> 10.7 us  [the longest x1 6.93 us: shards(): gathered = lax.all_to_all(own, (SHARE_AXIS, 'y'), 0, 0, tiled=True)]
    all_to_all x2, waiting for transfers between devices: 12.1 us -> 20.9 us  [the longest x1 13.8 us: shards(): some_rows = lax.all_to_all(normed, REST_AXES, 0, 0, tiled=True)]
    ppermute x3 -> x1, starting transfers between devices: 12.2 us -> 3.95 us  [shards(): other_part = lax.ppermute(other_part, SHARE_AXIS, [(0, 1), (1, 0)])]
    all_to_all x1, blocking collectives: 19.2 us -> 17.6 us  [shards(): blocks = lax.all_to_all(blocks, HEAD_AXES + (PAIR_AXIS,), 0, 0, tiled=True)]
  transfers between devices with their start and end apart: 6 -> 4, of which waited for: 4 -> 2; matrix products, arithmetic and copies ran while one was open for 0% -> 0% of each run, Pallas kernels for 3% -> 1%
where the time goes in v6:
time: 116 us
  blocking collectives  65.6 us (57%)
  waiting for transfers between devices  20.9 us (18%)
  starting transfers between devices  18.7 us (16%)
  Pallas kernels  6.92 us (6%)
  local copies, waits for them, and re-layouts  2.39 us (2%)
    all_to_all x1, blocking collectives, shards(): lax.all_to_all(messages.reshape(req_count, tiles * rows, lanes), REQ_AXES...  35.8 us
    all_to_all x1, blocking collectives, shards(): blocks = lax.all_to_all(blocks, HEAD_AXES + (PAIR_AXIS,), 0, 0, tiled=True)  17.6 us
    all_to_all x1, waiting for transfers between devices, shards(): some_rows = lax.all_to_all(normed, REST_AXES, 0, 0, tiled=True)  13.8 us
    all_to_all x1, waiting for transfers between devices, shards(): gathered = lax.all_to_all(own, (SHARE_AXIS, 'y'), 0, 0, tiled=True)  7.15 us
    all_to_all x1, starting transfers between devices, shards(): gathered = lax.all_to_all(own, (SHARE_AXIS, 'y'), 0, 0, tiled=True)  6.93 us
    all_gather x1, blocking collectives, shards(): pair = lax.all_gather(bc_conv, 'core', axis=0, tiled=False)  5.75 us
    all_gather x1, blocking collectives, shards(): gathered = lax.all_gather(gathered, 'core', axis=0, tiled=False)  4.66 us
    ppermute x1, starting transfers between devices, shards(): other_weight = lax.ppermute(out_weight, PAIR_AXIS, [(0, 1), (1, 0)])  4 us
  transfers between devices with their start and end apart: 4, of which 2 were waited for; matrix products, arithmetic and copies ran while one was open for 0% of the time, Pallas kernels for 1%

profile of v6, /device:TPU:1, one launch (start us, length us, event | category | flops | bytes accessed | tf_op | source)
XLA Modules:
  0.0 115.5 jit_solution(9528122048047716288)
XLA Ops:
  0.7 2.0 %constant_dynamic-slice_fusion = (bf16[256,2,512]{2,1,0:T(2,128)(2,1)S(1)}, bf16[256,2,512]{2,1,0:T(2,128)(2,1)S(1)}) fusion(bf16[256,2,1024]{2,1,0:T(2,128)(2,1)} %param.17, s32[]{:T(128)S(6)} %select_n.7, s32[]{:T(128)S(6)} %select_n.6), kind=kLoop, calls=%fused_computation.1 | loop fusion | bytes 2097160 | tf_op jit(solution)/shard_map/move_weights/dynamic_slice | solution.py:304
  2.7 3.9 %collective-permute-start = (bf16[256,2,512]{2,1,0:T(2,128)(2,1)S(1)}, bf16[256,2,512]{2,1,0:T(2,128)(2,1)S(1)}, u32[]{:S(2)}, u32[]{:S(2)}) collective-permute-start(bf16[256,2,512]{2,1,0:T(2,128)(2,1)S(1)} %get-tuple-element.22), channel_id=1, source_target_pairs={{0,8},{8,0},{1,9},{9,1},{2,10},{10,2},{3,11},{11,3},{4,12},{12,4},... | collective-permute-start | bytes 1572872 | tf_op jit(solution)/shard_map/move_weights/ppermute | solution.py:307
  6.6 4.0 %collective-permute-start.1 = (bf16[1024,256]{1,0:T(8,128)(2,1)S(1)}, bf16[1024,256]{1,0:T(8,128)(2,1)S(1)}, u32[]{:S(2)}, u32[]{:S(2)}) collective-permute-start(bf16[1024,256]{1,0:T(8,128)(2,1)S(1)} %copy-done.1), channel_id=1, source_target_pairs={{0,1},{1,0},{2,3},{3,2},{4,5},{5,4},{6,7},{7,6},{8,9},{9,8},{10,11... | collective-permute-start | bytes 1572872 | tf_op jit(solution)/shard_map/move_out_weight/ppermute | solution.py:315
  10.6 0.7 gather_tokens.1
  11.3 6.9 %all-to-all-start = ((bf16[16,24,256]{2,1,0:T(8,128)(2,1)}), bf16[16,24,256]{2,1,0:T(8,128)(2,1)S(1)}, u32[]{:S(2)}, u32[]{:S(2)}) async-start(bf16[16,24,256]{2,1,0:T(8,128)(2,1)} %gather_tokens.1), calls=%async_computation | async-start | bytes 393216 | tf_op jit(solution)/shard_map/gather_tokens/all_to_all | solution.py:323
  18.3 0.1 copy.21
  18.4 0.1 copy.22
  18.5 0.1 pad.2.clone
  18.6 7.1 %all-to-all-done = bf16[16,24,256]{2,1,0:T(8,128)(2,1)S(1)} async-done(((bf16[16,24,256]{2,1,0:T(8,128)(2,1)}), bf16[16,24,256]{2,1,0:T(8,128)(2,1)S(1)}, u32[]{:S(2)}, u32[]{:S(2)}) %all-to-all-start) | async-done | bytes 196640 | tf_op jit(solution)/shard_map/gather_tokens/all_to_all | solution.py:323
  25.8 4.7 %all-gather = bf16[32,24,256]{2,1,0:T(8,128)(2,1)S(1)} all-gather(bf16[16,24,256]{2,1,0:T(8,128)(2,1)S(1)} %all-to-all-done), channel_id=2, replica_groups=mesh['y'=8,'core'=2,'x1'=2,'x0'=2,'z2'=2,'z1'=2,'z0'=2] {'core'}, dimensions={0}, use_global_device_ids=true | all-gather | bytes 589824 | tf_op jit(solution)/shard_map/gather_tokens/all_gather | solution.py:324
  30.4 0.1 copy.23
  30.5 0.8 project.1
  31.3 0.0 copy-start.7
  31.4 35.8 %all_to_all.20.in_ref = bf16[32,120,128]{2,1,0:T(8,128)(2,1)S(1)} all-to-all(bf16[32,120,128]{2,1,0:T(8,128)(2,1)S(1)} %bitcast.21), channel_id=1, replica_groups=mesh['y'=8,'core'=2,'x1'=2,'x0'=2,'z2'=2,'z1'=2,'z0'=2] {'x1','x0','z2',..., dimensions={0} | all-to-all | bytes 1966080 | tf_op jit(solution)/shard_map/sum_req/all_to_all | solution.py:336
  67.2 0.7 sum_req.1
  68.0 5.8 %all-gather.3.pair_ref = f32[2,12,128]{2,1,0:T(8,128)S(1)} all-gather(f32[1,12,128]{2,1,0:T(8,128)S(1)} %bitcast.29), channel_id=3, replica_groups=mesh['y'=8,'core'=2,'x1'=2,'x0'=2,'z2'=2,'z1'=2,'z0'=2] {'core'}, dimensions={0}, use_global_device_ids=true | all-gather | bytes 18432 | tf_op jit(solution)/shard_map/scan/all_gather | solution.py:351
  73.8 2.6 %scan.1 = (f32[12,1024]{1,0:T(8,128)S(1)}, f32[12,128]{1,0:T(8,128)S(1)}, f32[3,1024,128]{2,1,0:T(8,128)}, bf16[3,3,1024]{2,1,0:T(4,128)(2,1)}) custom-call(f32[12,1024]{1,0:T(8,128)S(1)} %get-tuple-element.13.gate_ref, f32[12,1024]{1,0:T(8,128)S(1)} %get-tuple-element.14.inner_ref, f32[12,128]{1,0:T(8,128)S(1)} %get-tuple-element.15.step_ref, ...), custom_call_target="tpu_custom_call" | custom-call | tf_op jit(solution)/shard_map/scan/pallas_call | solution.py:352
  76.3 1.8 %all-gather.4.squares_ref = f32[2,12,128]{2,1,0:T(8,128)S(1)} all-gather(f32[1,12,128]{2,1,0:T(8,128)S(1)} %bitcast.28), channel_id=4, replica_groups=mesh['y'=8,'core'=2,'x1'=2,'x0'=2,'z2'=2,'z1'=2,'z0'=2] {'core'}, dimensions={0}, use_global_device_ids=true | all-gather | bytes 18432 | tf_op jit(solution)/shard_map/normalise/all_gather | solution.py:380
  78.2 0.9 normalise.1
  79.0 3.8 %all-to-all-start.2 = ((bf16[16,24,512]{2,1,0:T(8,128)(2,1)}), bf16[16,24,512]{2,1,0:T(8,128)(2,1)S(1)}, u32[]{:S(2)}, u32[]{:S(2)}) async-start(bf16[16,24,512]{2,1,0:T(8,128)(2,1)} %normalise.1), calls=%async_computation.2 | async-start | bytes 786432 | tf_op jit(solution)/shard_map/gather_normed/all_to_all | solution.py:387
  82.8 13.8 %all-to-all-done.2.in_ref = bf16[16,24,512]{2,1,0:T(8,128)(2,1)S(1)} async-done(((bf16[16,24,512]{2,1,0:T(8,128)(2,1)}), bf16[16,24,512]{2,1,0:T(8,128)(2,1)S(1)}, u32[]{:S(2)}, u32[]{:S(2)}) %all-to-all-start.2) | async-done | bytes 393248 | tf_op jit(solution)/shard_map/gather_normed/all_to_all | solution.py:387
  96.6 0.7 project_out.1
  97.3 17.6 %all_to_all.21.in_ref = bf16[32,24,128]{2,1,0:T(8,128)(2,1)S(1)} all-to-all(bf16[32,24,128]{2,1,0:T(8,128)(2,1)S(1)} %bitcast.26), channel_id=1, replica_groups=mesh['y'=8,'core'=2,'x1'=2,'x0'=2,'z2'=2,'z1'=2,'z0'=2] {'y','core','z0'}, dimensions={0} | all-to-all | bytes 393216 | tf_op jit(solution)/shard_map/sum_head/all_to_all | solution.py:403
  114.9 0.6 sum_head.1
  (33 shorter events, 0.1 us)
Async XLA Ops:
  0.6 6.0 %copy-start.1 = (bf16[1024,256]{1,0:T(8,128)(2,1)S(1)}, bf16[1024,256]{1,0:T(8,128)(2,1)}, u32[]{:S(2)}) copy-start(bf16[1024,256]{1,0:T(8,128)(2,1)} %own_ref.1) | copy-start | bytes 1572868
  0.6 10.0 %copy-start.4 = (bf16[4,6,256]{2,0,1:T(4,128)(2,1)S(1)}, bf16[4,6,256]{2,0,1:T(4,128)(2,1)}, u32[]{:S(2)}) copy-start(bf16[4,6,256]{2,0,1:T(4,128)(2,1)} %param.16) | copy-start | bytes 36868
  0.7 17.6 %copy-start.14 = (bf16[256,16]{0,1:T(8,128)(2,1)S(1)}, bf16[256,16]{0,1:T(8,128)(2,1)}, u32[]{:S(2)}) copy-start(bf16[256,16]{0,1:T(8,128)(2,1)} %param.18) | copy-start | bytes 24580
  0.7 17.9 %copy-start.13 = (bf16[256,128]{1,0:T(8,128)(2,1)S(1)}, bf16[256,128]{1,0:T(8,128)(2,1)}, u32[]{:S(2)}) copy-start(bf16[256,128]{1,0:T(8,128)(2,1)} %param.19) | copy-start | bytes 196612
  2.7 27.8 %collective-permute-start = (bf16[256,2,512]{2,1,0:T(2,128)(2,1)S(1)}, bf16[256,2,512]{2,1,0:T(2,128)(2,1)S(1)}, u32[]{:S(2)}, u32[]{:S(2)}) collective-permute-start(bf16[256,2,512]{2,1,0:T(2,128)(2,1)S(1)} %get-tuple-element.22), channel_id=1, source_target_pairs={{0,8},{8,0},{1,9},{9,1},{2,10},{10,2},{3,11},{11,3},{4,12},{12,4},... | collective-permute-start | bytes 1572872 | tf_op jit(solution)/shard_map/move_weights/ppermute | solution.py:307
  6.6 23.9 %collective-permute-start.1 = (bf16[1024,256]{1,0:T(8,128)(2,1)S(1)}, bf16[1024,256]{1,0:T(8,128)(2,1)S(1)}, u32[]{:S(2)}, u32[]{:S(2)}) collective-permute-start(bf16[1024,256]{1,0:T(8,128)(2,1)S(1)} %copy-done.1), channel_id=1, source_target_pairs={{0,1},{1,0},{2,3},{3,2},{4,5},{5,4},{6,7},{7,6},{8,9},{9,8},{10,11... | collective-permute-start | bytes 1572872 | tf_op jit(solution)/shard_map/move_out_weight/ppermute | solution.py:315
  11.3 14.4 %all-to-all-start = ((bf16[16,24,256]{2,1,0:T(8,128)(2,1)}), bf16[16,24,256]{2,1,0:T(8,128)(2,1)S(1)}, u32[]{:S(2)}, u32[]{:S(2)}) async-start(bf16[16,24,256]{2,1,0:T(8,128)(2,1)} %gather_tokens.1), calls=%async_computation | async-start | bytes 393216 | tf_op jit(solution)/shard_map/gather_tokens/all_to_all | solution.py:323
  31.3 36.0 %copy-start.7 = (bf16[3,3,128]{2,1,0:T(4,128)(2,1)S(1)}, bf16[3,3,128]{2,1,0:T(4,128)(2,1)}, u32[]{:S(2)}) copy-start(bf16[3,3,128]{2,1,0:T(4,128)(2,1)} %hist_ref.2) | copy-start | bytes 6916
  31.3 36.0 %copy-start.8 = (f32[4,128]{1,0:T(4,128)S(1)}, f32[4,128]{1,0:T(4,128)}, u32[]{:S(2)}) copy-start(f32[4,128]{1,0:T(4,128)} %taps_ref.2) | copy-start | bytes 6148
  31.3 35.9 %copy-start.9 = (f32[128]{0:T(128)S(1)}, f32[128]{0:T(128)}, u32[]{:S(2)}) copy-start(f32[128]{0:T(128)} %param.25) | copy-start | bytes 1540
  31.3 42.4 %copy-start = (f32[3,16,64,128]{3,2,1,0:T(8,128)S(1)}, f32[3,16,64,128]{3,2,1,0:T(8,128)}, u32[]{:S(2)}) copy-start(f32[3,16,64,128]{3,2,1,0:T(8,128)} %param.31) | copy-start | bytes 4718596
  31.3 42.4 %copy-start.2 = (bf16[3,3,1024]{2,1,0:T(4,128)(2,1)S(1)}, bf16[3,3,1024]{2,1,0:T(4,128)(2,1)}, u32[]{:S(2)}) copy-start(bf16[3,3,1024]{2,1,0:T(4,128)(2,1)} %hist_ref.3) | copy-start | bytes 55300
  31.3 42.4 %copy-start.3 = (f32[4,1024]{1,0:T(4,128)S(1)}, f32[4,1024]{1,0:T(4,128)}, u32[]{:S(2)}) copy-start(f32[4,1024]{1,0:T(4,128)} %taps_ref.3) | copy-start | bytes 49156
  31.3 42.4 %copy-start.5 = (f32[1024]{0:T(1024)S(1)}, f32[1024]{0:T(1024)}, u32[]{:S(2)}) copy-start(f32[1024]{0:T(1024)} %param.23) | copy-start | bytes 12292
  31.3 42.4 %copy-start.10 = (f32[16]{0:T(128)S(1)}, f32[16]{0:T(128)}, u32[]{:S(2)}) copy-start(f32[16]{0:T(128)} %param.26) | copy-start | bytes 196
  31.4 42.4 %copy-start.11 = (f32[16]{0:T(128)S(1)}, f32[16]{0:T(128)}, u32[]{:S(2)}) copy-start(f32[16]{0:T(128)} %param.27) | copy-start | bytes 196
  31.4 42.4 %copy-start.12 = (f32[16]{0:T(128)S(1)}, f32[16]{0:T(128)}, u32[]{:S(2)}) copy-start(f32[16]{0:T(128)} %param.28) | copy-start | bytes 196
  67.2 10.9 %copy-start.6 = (f32[1024]{0:T(1024)S(1)}, f32[1024]{0:T(1024)}, u32[]{:S(2)}) copy-start(f32[1024]{0:T(1024)} %param.29) | copy-start | bytes 12292
  79.0 17.6 %all-to-all-start.2 = ((bf16[16,24,512]{2,1,0:T(8,128)(2,1)}), bf16[16,24,512]{2,1,0:T(8,128)(2,1)S(1)}, u32[]{:S(2)}, u32[]{:S(2)}) async-start(bf16[16,24,512]{2,1,0:T(8,128)(2,1)} %normalise.1), calls=%async_computation.2 | async-start | bytes 786432 | tf_op jit(solution)/shard_map/gather_normed/all_to_all | solution.py:387

commit v7 on v6

--- a/solution.py
+++ b/solution.py
@@ -21,6 +21,7 @@
 PAIR_AXIS = "z0"
 REST_AXES = ("x1", "x0", "z2", "z1")
 REST = 16
+STEP_LANES, PACKED = 16, 6
 VMEM_LIMIT = 40 * 1024 * 1024
 
 
@@ -69,14 +70,22 @@
 
 
 def project(
-    here_ref, rows_ref, own_ref, other_ref, extra_ref, _, out_ref, messages
+    here_ref, _side, rows_ref, own_ref, other_ref, extra_ref, _low, _high, out_ref, messages
 ):
     cores, per_core, block_rows, features = rows_ref.shape
     y_count = per_core // SHARE
     rows = block_rows // 2
     lanes = out_ref.shape[1]
-    tiles = out_ref.shape[0] // (REQ_COUNT * rows)
+    lines = out_ref.shape[0] // REQ_COUNT
+    tiles = lines // rows
     here = here_ref[0]
+    count = y_count * block_rows
+    row = lax.broadcasted_iota(jnp.int32, (count, lanes), 0)
+    slot = lax.broadcasted_iota(jnp.int32, (count, lanes), 1) // STEP_LANES
+    kept = lax.rem(row, PACKED) == slot
+    line = lax.broadcasted_iota(jnp.int32, (count // PACKED, count), 0) * PACKED
+    row = lax.broadcasted_iota(jnp.int32, (count // PACKED, count), 1)
+    adder = jnp.where((row >= line) & (row < line + PACKED), 1.0, 0.0).astype(BF16)
     for core in range(cores):
         total = None
         for shift, weight_ref in enumerate((own_ref, other_ref)):
@@ -87,6 +96,8 @@
             total = part if total is None else total + part
             if shift == 0:
                 extra = jnp.dot(block, extra_ref[...], preferred_element_type=F32)
+        step = jnp.where(kept, extra[:, lanes:], 0.0).astype(BF16)
+        step = jnp.dot(adder, step, preferred_element_type=F32)
         for y in range(y_count):
             for side in range(2):
                 target = 2 * (y * cores + core) + side
@@ -95,8 +106,14 @@
                     value, column = total, tile * lanes
                     if column >= total.shape[1]:
                         value, column = extra, column - total.shape[1]
-                    to = (target * tiles + tile) * rows
+                    to = target * lines + tile * rows
                     messages[to : to + rows, :] = value[at : at + rows, column : column + lanes]
+                to, packed = target * lines + tiles * rows, rows // PACKED
+                at = (2 * y + side) * packed
+                messages[to : to + packed, :] = step[at : at + packed, :]
+                messages[to + packed : (target + 1) * lines, :] = jnp.zeros(
+                    (lines - tiles * rows - packed, lanes), F32
+                )
     out_ref[...] = messages[...].astype(BF16)
 
 
@@ -129,7 +146,9 @@
         part = total[2 * tiles * rows :]
         extra = part if extra is None else extra + part
     extra = extra.astype(BF16).astype(F32)
-    step_ref[...] = extra[rows : 2 * rows]
+    for at in range(rows):
+        line, lane = rows + at // PACKED, at % PACKED * STEP_LANES
+        step_ref[at : at + 1, :] = extra[line : line + 1, lane : lane + STEP_LANES]
     for req in range(requests):
         seq[0:history, :] = hist_ref[req].astype(F32)
         seq[history : history + steps, :] = extra[req * steps : (req + 1) * steps]
@@ -163,7 +182,7 @@
     history = hist_ref.shape[1]
     rows = gated_ref.shape[0]
     steps = rows // requests
-    step = step_ref[:, 0:heads] + step_bias_ref[...]
+    step = step_ref[...] + step_bias_ref[...]
     step_size = jnp.maximum(step, 0.0) + jnp.log1p(jnp.exp(-jnp.abs(step)))
     spread[0:rows, :] = step_size
     spread[rows : 2 * rows, :] = jnp.exp(-step_size * jnp.exp(log_decay_ref[...]))
@@ -255,14 +274,18 @@
         out_ref[copy] = block
 
 
-def project_out(side_ref, in_ref, own_ref, other_ref, out_ref, first, second, sums):
+def project_out(side_ref, in_ref, own_ref, low_ref, high_ref, out_ref, first, second, sums):
     blocks, block_rows, half = in_ref.shape
     rows = block_rows // 2
     lanes = out_ref.shape[-1]
     flat = in_ref[...].reshape(blocks * block_rows, half)
-    for weight_ref, side in ((own_ref, side_ref[0]), (other_ref, 1 - side_ref[0])):
-        first[...] = jnp.dot(flat, weight_ref[0:half, :], preferred_element_type=F32)
-        second[...] = jnp.dot(flat, weight_ref[half:, :], preferred_element_type=F32)
+    here = side_ref[0]
+    for low, high, side in (
+        (own_ref[0:half, :], own_ref[half:, :], here),
+        (low_ref[...], high_ref[...], 1 - here),
+    ):
+        first[...] = jnp.dot(flat, low, preferred_element_type=F32)
+        second[...] = jnp.dot(flat, high, preferred_element_type=F32)
         for block in range(blocks):
             at = block * block_rows
             total = first[at : at + rows, :] + second[at + rows : at + block_rows, :]
@@ -300,19 +323,27 @@
     chunk = width // SHARE
     with jax.named_scope("move_weights"):
         here = lax.axis_index(SHARE_AXIS)
-        own_part, other_part = (
-            lax.dynamic_slice(gate_inner_weight, (0, 0, side * chunk), (features, 2, chunk))
-            for side in (here, 1 - here)
+        own_part = lax.dynamic_slice(
+            lax.optimization_barrier(gate_inner_weight),
+            (0, 0, here * chunk),
+            (features, 2, chunk),
+        )
+        other_part = lax.dynamic_slice(
+            gate_inner_weight, (0, 0, (1 - here) * chunk), (features, 2, chunk)
         )
         other_part = lax.ppermute(other_part, SHARE_AXIS, [(0, 1), (1, 0)])
         chunks = [part.reshape(features, 2 * chunk) for part in (own_part, other_part)]
         extra = jnp.concatenate(
-            [bc_weight, step_weight, jnp.zeros((features, lanes - heads), BF16)], axis=1
+            [bc_weight] + [step_weight] * (lanes // heads), axis=1
         )
 
     with jax.named_scope("move_out_weight"):
-        side = lax.axis_index(PAIR_AXIS)
-        other_weight = lax.ppermute(out_weight, PAIR_AXIS, [(0, 1), (1, 0)])
+        side = lax.axis_index(PAIR_AXIS).astype(jnp.int32).reshape(1)
+        middle = out_weight.shape[0] // 2
+        other_weights = [
+            lax.ppermute(part, PAIR_AXIS, [(0, 1), (1, 0)])
+            for part in (out_weight[:middle], out_weight[middle:])
+        ]
 
     with jax.named_scope("gather_tokens"):
         own = call(
@@ -324,24 +355,25 @@
         gathered = lax.all_gather(gathered, "core", axis=0, tiled=False)
 
     with jax.named_scope("project"):
-        tiles = 2 * chunk // lanes + 2
-        message_rows = req_count * tiles * rows
+        lines = (2 * chunk // lanes + 1) * rows + rows // PACKED
+        lines += -lines % 8
+        message_rows = req_count * lines
         messages = call(
             project,
             sds((message_rows, lanes), BF16),
             [pltpu.VMEM((message_rows, lanes), F32)],
-            [SCALARS] + [WHOLE] * 4 + [UNREAD],
-        )(here.astype(jnp.int32).reshape(1), gathered, *chunks, extra, other_weight)
+            [SCALARS] * 2 + [WHOLE] * 4 + [UNREAD] * 2,
+        )(here.astype(jnp.int32).reshape(1), side, gathered, *chunks, extra, *other_weights)
     with jax.named_scope("sum_req"):
         parts = lax.all_to_all(
-            messages.reshape(req_count, tiles * rows, lanes), REQ_AXES, 0, 0, tiled=True
+            messages.reshape(req_count, lines, lanes), REQ_AXES, 0, 0, tiled=True
         )
         gate, inner, step, bc_conv, new_conv_groups = call(
             fold,
             (
                 sds((rows, width), F32),
                 sds((rows, width), F32),
-                sds((rows, lanes), F32),
+                sds((rows, heads), F32),
                 sds((rows, lanes), F32),
                 sds(conv_groups.shape, BF16),
             ),
@@ -396,8 +428,8 @@
                 pltpu.VMEM((REST * 2 * rows, out_columns), F32),
                 pltpu.VMEM(block, F32),
             ],
-            [SCALARS] + [WHOLE] * 3,
-        )(side.astype(jnp.int32).reshape(1), some_rows, out_weight, other_weight)
+            [SCALARS] + [WHOLE] * 4,
+        )(side, some_rows, out_weight, *other_weights)
     with jax.named_scope("sum_head"):
         blocks = product.reshape((2 * REST,) + block[2:])
         blocks = lax.all_to_all(blocks, HEAD_AXES + (PAIR_AXIS,), 0, 0, tiled=True)

time: 116 us -> 118 us (1.017)
  blocking collectives: 65.6 us -> 83.9 us
  waiting for transfers between devices: 20.9 us -> 3.89 us
  local copies, waits for them, and re-layouts: 2.39 us -> 5.64 us
  starting transfers between devices: 18.7 us -> 16.8 us
    all_to_all x1 -> x2, blocking collectives: 35.8 us -> 51.1 us  [the longest x1 32.4 us: shards(): lax.all_to_all(messages.reshape(req_count, lines, lanes), REQ_AXES, 0, 0,...]
    all_to_all x1 -> x0, waiting for transfers between devices: 13.8 us -> none  [shards(): some_rows = lax.all_to_all(normed, REST_AXES, 0, 0, tiled=True)]
    all_to_all x1, waiting for transfers between devices: 7.15 us -> 0.01 us  [shards(): gathered = lax.all_to_all(own, (SHARE_AXIS, 'y'), 0, 0, tiled=True)]
    ppermute x1 -> x2, waiting for transfers between devices: 0.01 us -> 3.89 us  [shards(): lax.ppermute(part, PAIR_AXIS, [(0, 1), (1, 0)])]
    all_to_all x1 -> x0, starting transfers between devices: 3.81 us -> none  [shards(): some_rows = lax.all_to_all(normed, REST_AXES, 0, 0, tiled=True)]
    all_to_all x1, blocking collectives: 17.6 us -> 19.6 us  [shards(): blocks = lax.all_to_all(blocks, HEAD_AXES + (PAIR_AXIS,), 0, 0, tiled=True)]
    ppermute x1 -> x2, starting transfers between devices: 4 us -> 5.91 us  [shards(): lax.ppermute(part, PAIR_AXIS, [(0, 1), (1, 0)])]
    all_gather x1, blocking collectives: 5.75 us -> 7.66 us  [shards(): pair = lax.all_gather(bc_conv, 'core', axis=0, tiled=False)]
  transfers between devices with their start and end apart: 4 -> 4, of which waited for: 2 -> 1; matrix products, arithmetic and copies ran while one was open for 0% -> 2% of each run, Pallas kernels for 1% -> 1%
where the time goes in v7:
time: 118 us; the launch traced here: 117 us
  blocking collectives  83.9 us (71%)
  starting transfers between devices  16.8 us (14%)
  Pallas kernels  6.19 us (5%)
  local copies, waits for them, and re-layouts  5.64 us (5%)
  waiting for transfers between devices  3.89 us (3%)
    all_to_all x1, blocking collectives, shards(): lax.all_to_all(messages.reshape(req_count, lines, lanes), REQ_AXES, 0, 0,...  32.4 us
    all_to_all x1, blocking collectives, shards(): blocks = lax.all_to_all(blocks, HEAD_AXES + (PAIR_AXIS,), 0, 0, tiled=True)  19.6 us
    all_to_all x1, blocking collectives, shards(): some_rows = lax.all_to_all(normed, REST_AXES, 0, 0, tiled=True)  18.8 us
    all_gather x1, blocking collectives, shards(): pair = lax.all_gather(bc_conv, 'core', axis=0, tiled=False)  7.66 us
    all_to_all x1, starting transfers between devices, shards(): gathered = lax.all_to_all(own, (SHARE_AXIS, 'y'), 0, 0, tiled=True)  6.93 us
    ppermute x2, starting transfers between devices, shards(): lax.ppermute(part, PAIR_AXIS, [(0, 1), (1, 0)])  5.91 us
    ppermute x1, starting transfers between devices, shards(): other_part = lax.ppermute(other_part, SHARE_AXIS, [(0, 1), (1, 0)])  3.94 us
    ppermute x2, waiting for transfers between devices, shards(): lax.ppermute(part, PAIR_AXIS, [(0, 1), (1, 0)])  3.89 us
  transfers between devices with their start and end apart: 4, of which 1 were waited for; matrix products, arithmetic and copies ran while one was open for 2% of the time, Pallas kernels for 1%

profile of v7, /device:TPU:1, one launch (start us, length us, event | category | flops | bytes accessed | tf_op | source)
XLA Modules:
  0.0 117.3 jit_solution(8700468924774028296)
XLA Ops:
  0.7 1.2 %copy-done = bf16[256,2,1024]{2,1,0:T(2,128)(2,1)S(1)} copy-done((bf16[256,2,1024]{2,1,0:T(2,128)(2,1)S(1)}, bf16[256,2,1024]{2,1,0:T(2,128)(2,1)}, u32[]{:S(2)}) %copy-start) | copy-done | bytes 1048600
  1.9 1.2 constant_dynamic-slice_fusion
  3.0 3.9 %collective-permute-start = (bf16[256,2,512]{2,1,0:T(2,128)(2,1)}, bf16[256,2,512]{2,1,0:T(2,128)(2,1)S(1)}, u32[]{:S(2)}, u32[]{:S(2)}) collective-permute-start(bf16[256,2,512]{2,1,0:T(2,128)(2,1)} %constant_dynamic-slice_fusion), channel_id=1, source_target_pairs={{0,8},{8,0},{1,9},{9,1},{2,10},{10,2},{3,11},{11,3},{4,12},{12,4},... | collective-permute-start | bytes 1572872 | tf_op jit(solution)/shard_map/move_weights/ppermute | solution.py:334
  7.0 0.7 copy-done.5
  7.7 0.7 gather_tokens.1
  8.4 6.9 %all-to-all-start = ((bf16[16,24,256]{2,1,0:T(8,128)(2,1)}), bf16[16,24,256]{2,1,0:T(8,128)(2,1)S(1)}, u32[]{:S(2)}, u32[]{:S(2)}) async-start(bf16[16,24,256]{2,1,0:T(8,128)(2,1)} %gather_tokens.1), calls=%async_computation | async-start | bytes 393216 | tf_op jit(solution)/shard_map/gather_tokens/all_to_all | solution.py:354
  15.3 0.8 fusion
  16.2 4.0 %collective-permute-start.2 = (bf16[512,256]{1,0:T(8,128)(2,1)}, bf16[512,256]{1,0:T(8,128)(2,1)S(1)}, u32[]{:S(2)}, u32[]{:S(2)}) collective-permute-start(bf16[512,256]{1,0:T(8,128)(2,1)} %get-tuple-element.22), channel_id=1, source_target_pairs={{0,1},{1,0},{2,3},{3,2},{4,5},{5,4},{6,7},{7,6},{8,9},{9,8},{10,11... | collective-permute-start | bytes 786440 | tf_op jit(solution)/shard_map/move_out_weight/ppermute | solution.py:344
  20.2 1.9 %collective-permute-start.1 = (bf16[512,256]{1,0:T(8,128)(2,1)}, bf16[512,256]{1,0:T(8,128)(2,1)S(1)}, u32[]{:S(2)}, u32[]{:S(2)}) collective-permute-start(bf16[512,256]{1,0:T(8,128)(2,1)} %get-tuple-element.23), channel_id=1, source_target_pairs={{0,1},{1,0},{2,3},{3,2},{4,5},{5,4},{6,7},{7,6},{8,9},{9,8},{10,11... | collective-permute-start | bytes 786440 | tf_op jit(solution)/shard_map/move_out_weight/ppermute | solution.py:344
  22.1 0.1 copy.28
  22.2 0.4 constant_dynamic-slice_fusion.1
  22.7 1.1 concatenate.3.extra_ref
  23.7 3.7 %all-gather = bf16[32,24,256]{2,1,0:T(8,128)(2,1)S(1)} all-gather(bf16[16,24,256]{2,1,0:T(8,128)(2,1)S(1)} %all-to-all-done), channel_id=2, replica_groups=mesh['y'=8,'core'=2,'x1'=2,'x0'=2,'z2'=2,'z1'=2,'z0'=2] {'core'}, dimensions={0}, use_global_device_ids=true | all-gather | bytes 589824 | tf_op jit(solution)/shard_map/gather_tokens/all_gather | solution.py:355
  27.5 3.9 %collective-permute-done.1._low.low_ref = bf16[512,256]{1,0:T(8,128)(2,1)S(1)} collective-permute-done((bf16[512,256]{1,0:T(8,128)(2,1)}, bf16[512,256]{1,0:T(8,128)(2,1)S(1)}, u32[]{:S(2)}, u32[]{:S(2)}) %collective-permute-start.1) | collective-permute-done | bytes 262176 | tf_op jit(solution)/shard_map/move_out_weight/ppermute | solution.py:344
  31.4 0.8 project.1
  32.3 32.4 %all_to_all.20.in_ref = bf16[32,112,128]{2,1,0:T(8,128)(2,1)S(1)} all-to-all(bf16[32,112,128]{2,1,0:T(8,128)(2,1)S(1)} %bitcast.21), channel_id=1, replica_groups=mesh['y'=8,'core'=2,'x1'=2,'x0'=2,'z2'=2,'z1'=2,'z0'=2] {'x1','x0','z2',..., dimensions={0} | all-to-all | bytes 1835008 | tf_op jit(solution)/shard_map/sum_req/all_to_all | solution.py:368
  64.6 0.7 sum_req.1
  65.4 7.7 %all-gather.3.pair_ref = f32[2,12,128]{2,1,0:T(8,128)S(1)} all-gather(f32[1,12,128]{2,1,0:T(8,128)S(1)} %bitcast.29), channel_id=3, replica_groups=mesh['y'=8,'core'=2,'x1'=2,'x0'=2,'z2'=2,'z1'=2,'z0'=2] {'core'}, dimensions={0}, use_global_device_ids=true | all-gather | bytes 18432 | tf_op jit(solution)/shard_map/scan/all_gather | solution.py:383
  73.1 2.6 %scan.1 = (f32[12,1024]{1,0:T(8,128)S(1)}, f32[12,128]{1,0:T(8,128)S(1)}, f32[3,1024,128]{2,1,0:T(8,128)}, bf16[3,3,1024]{2,1,0:T(4,128)(2,1)}) custom-call(f32[12,1024]{1,0:T(8,128)S(1)} %get-tuple-element.13.gate_ref, f32[12,1024]{1,0:T(8,128)S(1)} %get-tuple-element.14.inner_ref, f32[12,16]{1,0:T(8,128)S(1)} %get-tuple-element.15.step_ref, ...), custom_call_target="tpu_custom_call" | custom-call | tf_op jit(solution)/shard_map/scan/pallas_call | solution.py:384
  75.6 1.8 %all-gather.4.squares_ref = f32[2,12,128]{2,1,0:T(8,128)S(1)} all-gather(f32[1,12,128]{2,1,0:T(8,128)S(1)} %bitcast.28), channel_id=4, replica_groups=mesh['y'=8,'core'=2,'x1'=2,'x0'=2,'z2'=2,'z1'=2,'z0'=2] {'core'}, dimensions={0}, use_global_device_ids=true | all-gather | bytes 18432 | tf_op jit(solution)/shard_map/normalise/all_gather | solution.py:412
  77.6 18.8 %all_to_all.21.in_ref = bf16[16,24,512]{2,1,0:T(8,128)(2,1)S(1)} all-to-all(bf16[16,24,512]{2,1,0:T(8,128)(2,1)S(1)} %normalise.1), channel_id=1, replica_groups=mesh['y'=8,'core'=2,'x1'=2,'x0'=2,'z2'=2,'z1'=2,'z0'=2] {'x1','x0','z2',..., dimensions={0} | all-to-all | bytes 786432 | tf_op jit(solution)/shard_map/gather_normed/all_to_all | solution.py:419
  96.3 0.7 project_out.1
  97.0 19.6 %all_to_all.22.in_ref = bf16[32,24,128]{2,1,0:T(8,128)(2,1)S(1)} all-to-all(bf16[32,24,128]{2,1,0:T(8,128)(2,1)S(1)} %bitcast.26), channel_id=1, replica_groups=mesh['y'=8,'core'=2,'x1'=2,'x0'=2,'z2'=2,'z1'=2,'z0'=2] {'y','core','z0'}, dimensions={0} | all-to-all | bytes 393216 | tf_op jit(solution)/shard_map/sum_head/all_to_all | solution.py:435
  116.7 0.6 sum_head.1
  (34 shorter events, 0.3 us)
Async XLA Ops:
  0.6 1.2 %copy-start = (bf16[256,2,1024]{2,1,0:T(2,128)(2,1)S(1)}, bf16[256,2,1024]{2,1,0:T(2,128)(2,1)}, u32[]{:S(2)}) copy-start(bf16[256,2,1024]{2,1,0:T(2,128)(2,1)} %param.17) | copy-start | bytes 3145732
  0.6 14.7 %copy-start.1 = (bf16[1024,256]{1,0:T(8,128)(2,1)S(1)}, bf16[1024,256]{1,0:T(8,128)(2,1)}, u32[]{:S(2)}) copy-start(bf16[1024,256]{1,0:T(8,128)(2,1)} %own_ref.1) | copy-start | bytes 1572868
  0.7 21.4 %copy-start.14 = (bf16[256,16]{0,1:T(8,128)(2,1)S(1)}, bf16[256,16]{0,1:T(8,128)(2,1)}, u32[]{:S(2)}) copy-start(bf16[256,16]{0,1:T(8,128)(2,1)} %param.18) | copy-start | bytes 24580
  3.0 24.4 %collective-permute-start = (bf16[256,2,512]{2,1,0:T(2,128)(2,1)}, bf16[256,2,512]{2,1,0:T(2,128)(2,1)S(1)}, u32[]{:S(2)}, u32[]{:S(2)}) collective-permute-start(bf16[256,2,512]{2,1,0:T(2,128)(2,1)} %constant_dynamic-slice_fusion), channel_id=1, source_target_pairs={{0,8},{8,0},{1,9},{9,1},{2,10},{10,2},{3,11},{11,3},{4,12},{12,4},... | collective-permute-start | bytes 1572872 | tf_op jit(solution)/shard_map/move_weights/ppermute | solution.py:334
  7.0 0.7 copy-start.5
  8.4 15.4 %all-to-all-start = ((bf16[16,24,256]{2,1,0:T(8,128)(2,1)}), bf16[16,24,256]{2,1,0:T(8,128)(2,1)S(1)}, u32[]{:S(2)}, u32[]{:S(2)}) async-start(bf16[16,24,256]{2,1,0:T(8,128)(2,1)} %gather_tokens.1), calls=%async_computation | async-start | bytes 393216 | tf_op jit(solution)/shard_map/gather_tokens/all_to_all | solution.py:354
  16.2 11.3 %collective-permute-start.2 = (bf16[512,256]{1,0:T(8,128)(2,1)}, bf16[512,256]{1,0:T(8,128)(2,1)S(1)}, u32[]{:S(2)}, u32[]{:S(2)}) collective-permute-start(bf16[512,256]{1,0:T(8,128)(2,1)} %get-tuple-element.22), channel_id=1, source_target_pairs={{0,1},{1,0},{2,3},{3,2},{4,5},{5,4},{6,7},{7,6},{8,9},{9,8},{10,11... | collective-permute-start | bytes 786440 | tf_op jit(solution)/shard_map/move_out_weight/ppermute | solution.py:344
  20.2 11.2 %collective-permute-start.1 = (bf16[512,256]{1,0:T(8,128)(2,1)}, bf16[512,256]{1,0:T(8,128)(2,1)S(1)}, u32[]{:S(2)}, u32[]{:S(2)}) collective-permute-start(bf16[512,256]{1,0:T(8,128)(2,1)} %get-tuple-element.23), channel_id=1, source_target_pairs={{0,1},{1,0},{2,3},{3,2},{4,5},{5,4},{6,7},{7,6},{8,9},{9,8},{10,11... | collective-permute-start | bytes 786440 | tf_op jit(solution)/shard_map/move_out_weight/ppermute | solution.py:344
  32.1 32.5 %copy-start.8 = (bf16[3,3,128]{2,1,0:T(4,128)(2,1)S(1)}, bf16[3,3,128]{2,1,0:T(4,128)(2,1)}, u32[]{:S(2)}) copy-start(bf16[3,3,128]{2,1,0:T(4,128)(2,1)} %hist_ref.2) | copy-start | bytes 6916
  32.2 32.5 %copy-start.9 = (f32[4,128]{1,0:T(4,128)S(1)}, f32[4,128]{1,0:T(4,128)}, u32[]{:S(2)}) copy-start(f32[4,128]{1,0:T(4,128)} %taps_ref.2) | copy-start | bytes 6148
  32.2 32.5 %copy-start.10 = (f32[128]{0:T(128)S(1)}, f32[128]{0:T(128)}, u32[]{:S(2)}) copy-start(f32[128]{0:T(128)} %param.25) | copy-start | bytes 1540
  32.2 40.8 %copy-start.2 = (f32[3,16,64,128]{3,2,1,0:T(8,128)S(1)}, f32[3,16,64,128]{3,2,1,0:T(8,128)}, u32[]{:S(2)}) copy-start(f32[3,16,64,128]{3,2,1,0:T(8,128)} %param.31) | copy-start | bytes 4718596
  32.2 40.8 %copy-start.3 = (bf16[3,3,1024]{2,1,0:T(4,128)(2,1)S(1)}, bf16[3,3,1024]{2,1,0:T(4,128)(2,1)}, u32[]{:S(2)}) copy-start(bf16[3,3,1024]{2,1,0:T(4,128)(2,1)} %hist_ref.3) | copy-start | bytes 55300
  32.2 40.8 %copy-start.4 = (f32[4,1024]{1,0:T(4,128)S(1)}, f32[4,1024]{1,0:T(4,128)}, u32[]{:S(2)}) copy-start(f32[4,1024]{1,0:T(4,128)} %taps_ref.3) | copy-start | bytes 49156
  32.2 40.8 %copy-start.6 = (f32[1024]{0:T(1024)S(1)}, f32[1024]{0:T(1024)}, u32[]{:S(2)}) copy-start(f32[1024]{0:T(1024)} %param.23) | copy-start | bytes 12292
  32.2 40.8 %copy-start.11 = (f32[16]{0:T(128)S(1)}, f32[16]{0:T(128)}, u32[]{:S(2)}) copy-start(f32[16]{0:T(128)} %param.26) | copy-start | bytes 196
  32.2 40.8 %copy-start.12 = (f32[16]{0:T(128)S(1)}, f32[16]{0:T(128)}, u32[]{:S(2)}) copy-start(f32[16]{0:T(128)} %param.27) | copy-start | bytes 196
  32.2 40.8 %copy-start.13 = (f32[16]{0:T(128)S(1)}, f32[16]{0:T(128)}, u32[]{:S(2)}) copy-start(f32[16]{0:T(128)} %param.28) | copy-start | bytes 196
  64.6 12.8 %copy-start.7 = (f32[1024]{0:T(1024)S(1)}, f32[1024]{0:T(1024)}, u32[]{:S(2)}) copy-start(f32[1024]{0:T(1024)} %param.29) | copy-start | bytes 12292

commit v8 on v7

--- a/solution.py
+++ b/solution.py
@@ -70,7 +70,7 @@
 
 
 def project(
-    here_ref, _side, rows_ref, own_ref, other_ref, extra_ref, _low, _high, out_ref, messages
+    here_ref, _side, rows_ref, own_ref, other_ref, extra_ref, _later, out_ref, messages
 ):
     cores, per_core, block_rows, features = rows_ref.shape
     y_count = per_core // SHARE
@@ -274,18 +274,14 @@
         out_ref[copy] = block
 
 
-def project_out(side_ref, in_ref, own_ref, low_ref, high_ref, out_ref, first, second, sums):
+def project_out(side_ref, in_ref, own_ref, other_ref, out_ref, first, second, sums):
     blocks, block_rows, half = in_ref.shape
     rows = block_rows // 2
     lanes = out_ref.shape[-1]
     flat = in_ref[...].reshape(blocks * block_rows, half)
-    here = side_ref[0]
-    for low, high, side in (
-        (own_ref[0:half, :], own_ref[half:, :], here),
-        (low_ref[...], high_ref[...], 1 - here),
-    ):
-        first[...] = jnp.dot(flat, low, preferred_element_type=F32)
-        second[...] = jnp.dot(flat, high, preferred_element_type=F32)
+    for weight_ref, side in ((own_ref, side_ref[0]), (other_ref, 1 - side_ref[0])):
+        first[...] = jnp.dot(flat, weight_ref[0:half, :], preferred_element_type=F32)
+        second[...] = jnp.dot(flat, weight_ref[half:, :], preferred_element_type=F32)
         for block in range(blocks):
             at = block * block_rows
             total = first[at : at + rows, :] + second[at + rows : at + block_rows, :]
@@ -339,11 +335,7 @@
 
     with jax.named_scope("move_out_weight"):
         side = lax.axis_index(PAIR_AXIS).astype(jnp.int32).reshape(1)
-        middle = out_weight.shape[0] // 2
-        other_weights = [
-            lax.ppermute(part, PAIR_AXIS, [(0, 1), (1, 0)])
-            for part in (out_weight[:middle], out_weight[middle:])
-        ]
+        other_weight = lax.ppermute(out_weight, PAIR_AXIS, [(0, 1), (1, 0)])
 
     with jax.named_scope("gather_tokens"):
         own = call(
@@ -362,8 +354,8 @@
             project,
             sds((message_rows, lanes), BF16),
             [pltpu.VMEM((message_rows, lanes), F32)],
-            [SCALARS] * 2 + [WHOLE] * 4 + [UNREAD] * 2,
-        )(here.astype(jnp.int32).reshape(1), side, gathered, *chunks, extra, *other_weights)
+            [SCALARS] * 2 + [WHOLE] * 4 + [UNREAD],
+        )(here.astype(jnp.int32).reshape(1), side, gathered, *chunks, extra, other_weight)
     with jax.named_scope("sum_req"):
         parts = lax.all_to_all(
             messages.reshape(req_count, lines, lanes), REQ_AXES, 0, 0, tiled=True
@@ -428,8 +420,8 @@
                 pltpu.VMEM((REST * 2 * rows, out_columns), F32),
                 pltpu.VMEM(block, F32),
             ],
-            [SCALARS] + [WHOLE] * 4,
-        )(side, some_rows, out_weight, *other_weights)
+            [SCALARS] + [WHOLE] * 3,
+        )(side, some_rows, out_weight, other_weight)
     with jax.named_scope("sum_head"):
         blocks = product.reshape((2 * REST,) + block[2:])
         blocks = lax.all_to_all(blocks, HEAD_AXES + (PAIR_AXIS,), 0, 0, tiled=True)

time: 118 us -> 114 us (0.966)
  blocking collectives: 83.9 us -> 81.8 us
  waiting for transfers between devices: 3.89 us -> 5.84 us
  starting transfers between devices: 16.8 us -> 14.9 us
  local copies, waits for them, and re-layouts: 5.64 us -> 4.02 us
    all_to_all x1, waiting for transfers between devices: 0.01 us -> 5.83 us  [shards(): gathered = lax.all_to_all(own, (SHARE_AXIS, 'y'), 0, 0, tiled=True)]
    ppermute x2 -> x1, waiting for transfers between devices: 3.89 us -> 0.01 us  [shards(): other_weight = lax.ppermute(out_weight, PAIR_AXIS, [(0, 1), (1, 0)])]
    all_to_all x1, blocking collectives: 19.6 us -> 17.5 us  [shards(): blocks = lax.all_to_all(blocks, HEAD_AXES + (PAIR_AXIS,), 0, 0, tiled=True)]
    ppermute x2 -> x1, starting transfers between devices: 5.91 us -> 4 us  [shards(): other_weight = lax.ppermute(out_weight, PAIR_AXIS, [(0, 1), (1, 0)])]
    all_to_all x1, blocking collectives: 32.4 us -> 34.1 us  [shards(): lax.all_to_all(messages.reshape(req_count, lines, lanes), REQ_AXES, 0, 0,...]
    all_gather x1, blocking collectives: 7.66 us -> 6.19 us  [shards(): pair = lax.all_gather(bc_conv, 'core', axis=0, tiled=False)]
    all_to_all x1, blocking collectives: 18.8 us -> 17.5 us  [shards(): some_rows = lax.all_to_all(normed, REST_AXES, 0, 0, tiled=True)]
  transfers between devices with their start and end apart: 4 -> 3, of which waited for: 1 -> 1; matrix products, arithmetic and copies ran while one was open for 2% -> 1% of each run, Pallas kernels for 1% -> 1%
where the time goes in v8:
time: 114 us
  blocking collectives  81.8 us (72%)
  starting transfers between devices  14.9 us (13%)
  Pallas kernels  6.19 us (5%)
  waiting for transfers between devices  5.84 us (5%)
  local copies, waits for them, and re-layouts  4.02 us (4%)
    all_to_all x1, blocking collectives, shards(): lax.all_to_all(messages.reshape(req_count, lines, lanes), REQ_AXES, 0, 0,...  34.1 us
    all_to_all x1, blocking collectives, shards(): some_rows = lax.all_to_all(normed, REST_AXES, 0, 0, tiled=True)  17.5 us
    all_to_all x1, blocking collectives, shards(): blocks = lax.all_to_all(blocks, HEAD_AXES + (PAIR_AXIS,), 0, 0, tiled=True)  17.5 us
    all_to_all x1, starting transfers between devices, shards(): gathered = lax.all_to_all(own, (SHARE_AXIS, 'y'), 0, 0, tiled=True)  6.93 us
    all_gather x1, blocking collectives, shards(): pair = lax.all_gather(bc_conv, 'core', axis=0, tiled=False)  6.19 us
    all_to_all x1, waiting for transfers between devices, shards(): gathered = lax.all_to_all(own, (SHARE_AXIS, 'y'), 0, 0, tiled=True)  5.83 us
    all_gather x1, blocking collectives, shards(): gathered = lax.all_gather(gathered, 'core', axis=0, tiled=False)  4.66 us
    ppermute x1, starting transfers between devices, shards(): other_weight = lax.ppermute(out_weight, PAIR_AXIS, [(0, 1), (1, 0)])  4 us
  transfers between devices with their start and end apart: 3, of which 1 were waited for; matrix products, arithmetic and copies ran while one was open for 1% of the time, Pallas kernels for 1%

profile of v8, /device:TPU:1, one launch (start us, length us, event | category | flops | bytes accessed | tf_op | source)
XLA Modules:
  0.0 113.6 jit_solution(6488626187679909521)
XLA Ops:
  0.7 1.2 %copy-done = bf16[256,2,1024]{2,1,0:T(2,128)(2,1)S(1)} copy-done((bf16[256,2,1024]{2,1,0:T(2,128)(2,1)S(1)}, bf16[256,2,1024]{2,1,0:T(2,128)(2,1)}, u32[]{:S(2)}) %copy-start) | copy-done | bytes 1048600
  1.9 0.4 constant_dynamic-slice_fusion
  2.2 3.9 %collective-permute-start = (bf16[256,2,512]{2,1,0:T(2,128)(2,1)S(1)}, bf16[256,2,512]{2,1,0:T(2,128)(2,1)S(1)}, u32[]{:S(2)}, u32[]{:S(2)}) collective-permute-start(bf16[256,2,512]{2,1,0:T(2,128)(2,1)S(1)} %constant_dynamic-slice_fusion), channel_id=1, source_target_pairs={{0,8},{8,0},{1,9},{9,1},{2,10},{10,2},{3,11},{11,3},{4,12},{12,4},... | collective-permute-start | bytes 1572872 | tf_op jit(solution)/shard_map/move_weights/ppermute | solution.py:330
  6.2 4.0 %collective-permute-start.1 = (bf16[1024,256]{1,0:T(8,128)(2,1)}, bf16[1024,256]{1,0:T(8,128)(2,1)S(1)}, u32[]{:S(2)}, u32[]{:S(2)}) collective-permute-start(bf16[1024,256]{1,0:T(8,128)(2,1)} %own_ref.1), channel_id=1, source_target_pairs={{0,1},{1,0},{2,3},{3,2},{4,5},{5,4},{6,7},{7,6},{8,9},{9,8},{10,11... | collective-permute-start | bytes 1572872 | tf_op jit(solution)/shard_map/move_out_weight/ppermute | solution.py:338
  10.2 0.7 copy-done.5
  10.9 0.7 gather_tokens.1
  11.6 6.9 %all-to-all-start = ((bf16[16,24,256]{2,1,0:T(8,128)(2,1)}), bf16[16,24,256]{2,1,0:T(8,128)(2,1)S(1)}, u32[]{:S(2)}, u32[]{:S(2)}) async-start(bf16[16,24,256]{2,1,0:T(8,128)(2,1)} %gather_tokens.1), calls=%async_computation | async-start | bytes 393216 | tf_op jit(solution)/shard_map/gather_tokens/all_to_all | solution.py:346
  18.5 0.1 copy.28
  18.7 0.4 constant_dynamic-slice_fusion.1
  19.0 0.1 copy.36
  19.1 1.1 concatenate.3.extra_ref
  20.2 5.8 %all-to-all-done = bf16[16,24,256]{2,1,0:T(8,128)(2,1)S(1)} async-done(((bf16[16,24,256]{2,1,0:T(8,128)(2,1)}), bf16[16,24,256]{2,1,0:T(8,128)(2,1)S(1)}, u32[]{:S(2)}, u32[]{:S(2)}) %all-to-all-start) | async-done | bytes 196640 | tf_op jit(solution)/shard_map/gather_tokens/all_to_all | solution.py:346
  26.0 4.7 %all-gather = bf16[32,24,256]{2,1,0:T(8,128)(2,1)S(1)} all-gather(bf16[16,24,256]{2,1,0:T(8,128)(2,1)S(1)} %all-to-all-done), channel_id=2, replica_groups=mesh['y'=8,'core'=2,'x1'=2,'x0'=2,'z2'=2,'z1'=2,'z0'=2] {'core'}, dimensions={0}, use_global_device_ids=true | all-gather | bytes 589824 | tf_op jit(solution)/shard_map/gather_tokens/all_gather | solution.py:347
  30.8 0.8 project.1
  31.7 34.1 %all_to_all.20.in_ref = bf16[32,112,128]{2,1,0:T(8,128)(2,1)S(1)} all-to-all(bf16[32,112,128]{2,1,0:T(8,128)(2,1)S(1)} %bitcast.21), channel_id=1, replica_groups=mesh['y'=8,'core'=2,'x1'=2,'x0'=2,'z2'=2,'z1'=2,'z0'=2] {'x1','x0','z2',..., dimensions={0} | all-to-all | bytes 1835008 | tf_op jit(solution)/shard_map/sum_req/all_to_all | solution.py:360
  65.8 0.7 sum_req.1
  66.6 6.2 %all-gather.3.pair_ref = f32[2,12,128]{2,1,0:T(8,128)S(1)} all-gather(f32[1,12,128]{2,1,0:T(8,128)S(1)} %bitcast.29), channel_id=3, replica_groups=mesh['y'=8,'core'=2,'x1'=2,'x0'=2,'z2'=2,'z1'=2,'z0'=2] {'core'}, dimensions={0}, use_global_device_ids=true | all-gather | bytes 18432 | tf_op jit(solution)/shard_map/scan/all_gather | solution.py:375
  72.8 2.6 %scan.1 = (f32[12,1024]{1,0:T(8,128)S(1)}, f32[12,128]{1,0:T(8,128)S(1)}, f32[3,1024,128]{2,1,0:T(8,128)}, bf16[3,3,1024]{2,1,0:T(4,128)(2,1)}) custom-call(f32[12,1024]{1,0:T(8,128)S(1)} %get-tuple-element.13.gate_ref, f32[12,1024]{1,0:T(8,128)S(1)} %get-tuple-element.14.inner_ref, f32[12,16]{1,0:T(8,128)S(1)} %get-tuple-element.15.step_ref, ...), custom_call_target="tpu_custom_call" | custom-call | tf_op jit(solution)/shard_map/scan/pallas_call | solution.py:376
  75.4 1.8 %all-gather.4.squares_ref = f32[2,12,128]{2,1,0:T(8,128)S(1)} all-gather(f32[1,12,128]{2,1,0:T(8,128)S(1)} %bitcast.28), channel_id=4, replica_groups=mesh['y'=8,'core'=2,'x1'=2,'x0'=2,'z2'=2,'z1'=2,'z0'=2] {'core'}, dimensions={0}, use_global_device_ids=true | all-gather | bytes 18432 | tf_op jit(solution)/shard_map/normalise/all_gather | solution.py:404
  77.2 0.1 normalise.1
  77.3 17.5 %all_to_all.21.in_ref = bf16[16,24,512]{2,1,0:T(8,128)(2,1)S(1)} all-to-all(bf16[16,24,512]{2,1,0:T(8,128)(2,1)S(1)} %normalise.1), channel_id=1, replica_groups=mesh['y'=8,'core'=2,'x1'=2,'x0'=2,'z2'=2,'z1'=2,'z0'=2] {'x1','x0','z2',..., dimensions={0} | all-to-all | bytes 786432 | tf_op jit(solution)/shard_map/gather_normed/all_to_all | solution.py:411
  94.8 0.7 project_out.1
  95.5 17.5 %all_to_all.22.in_ref = bf16[32,24,128]{2,1,0:T(8,128)(2,1)S(1)} all-to-all(bf16[32,24,128]{2,1,0:T(8,128)(2,1)S(1)} %bitcast.26), channel_id=1, replica_groups=mesh['y'=8,'core'=2,'x1'=2,'x0'=2,'z2'=2,'z1'=2,'z0'=2] {'y','core','z0'}, dimensions={0} | all-to-all | bytes 393216 | tf_op jit(solution)/shard_map/sum_head/all_to_all | solution.py:427
  113.0 0.6 sum_head.1
  (31 shorter events, 0.2 us)
Async XLA Ops:
  0.6 1.2 %copy-start = (bf16[256,2,1024]{2,1,0:T(2,128)(2,1)S(1)}, bf16[256,2,1024]{2,1,0:T(2,128)(2,1)}, u32[]{:S(2)}) copy-start(bf16[256,2,1024]{2,1,0:T(2,128)(2,1)} %param.17) | copy-start | bytes 3145732
  0.6 17.9 %copy-start.14 = (bf16[256,16]{0,1:T(8,128)(2,1)S(1)}, bf16[256,16]{0,1:T(8,128)(2,1)}, u32[]{:S(2)}) copy-start(bf16[256,16]{0,1:T(8,128)(2,1)} %param.18) | copy-start | bytes 24580
  2.2 28.5 %collective-permute-start = (bf16[256,2,512]{2,1,0:T(2,128)(2,1)S(1)}, bf16[256,2,512]{2,1,0:T(2,128)(2,1)S(1)}, u32[]{:S(2)}, u32[]{:S(2)}) collective-permute-start(bf16[256,2,512]{2,1,0:T(2,128)(2,1)S(1)} %constant_dynamic-slice_fusion), channel_id=1, source_target_pairs={{0,8},{8,0},{1,9},{9,1},{2,10},{10,2},{3,11},{11,3},{4,12},{12,4},... | collective-permute-start | bytes 1572872 | tf_op jit(solution)/shard_map/move_weights/ppermute | solution.py:330
  6.2 24.6 %collective-permute-start.1 = (bf16[1024,256]{1,0:T(8,128)(2,1)}, bf16[1024,256]{1,0:T(8,128)(2,1)S(1)}, u32[]{:S(2)}, u32[]{:S(2)}) collective-permute-start(bf16[1024,256]{1,0:T(8,128)(2,1)} %own_ref.1), channel_id=1, source_target_pairs={{0,1},{1,0},{2,3},{3,2},{4,5},{5,4},{6,7},{7,6},{8,9},{9,8},{10,11... | collective-permute-start | bytes 1572872 | tf_op jit(solution)/shard_map/move_out_weight/ppermute | solution.py:338
  10.2 0.7 copy-start.5
  11.6 14.4 %all-to-all-start = ((bf16[16,24,256]{2,1,0:T(8,128)(2,1)}), bf16[16,24,256]{2,1,0:T(8,128)(2,1)S(1)}, u32[]{:S(2)}, u32[]{:S(2)}) async-start(bf16[16,24,256]{2,1,0:T(8,128)(2,1)} %gather_tokens.1), calls=%async_computation | async-start | bytes 393216 | tf_op jit(solution)/shard_map/gather_tokens/all_to_all | solution.py:346
  31.5 34.3 %copy-start.8 = (bf16[3,3,128]{2,1,0:T(4,128)(2,1)S(1)}, bf16[3,3,128]{2,1,0:T(4,128)(2,1)}, u32[]{:S(2)}) copy-start(bf16[3,3,128]{2,1,0:T(4,128)(2,1)} %hist_ref.2) | copy-start | bytes 6916
  31.6 34.3 %copy-start.9 = (f32[4,128]{1,0:T(4,128)S(1)}, f32[4,128]{1,0:T(4,128)}, u32[]{:S(2)}) copy-start(f32[4,128]{1,0:T(4,128)} %taps_ref.2) | copy-start | bytes 6148
  31.6 34.3 %copy-start.10 = (f32[128]{0:T(128)S(1)}, f32[128]{0:T(128)}, u32[]{:S(2)}) copy-start(f32[128]{0:T(128)} %param.25) | copy-start | bytes 1540
  31.6 41.2 %copy-start.1 = (f32[3,16,64,128]{3,2,1,0:T(8,128)S(1)}, f32[3,16,64,128]{3,2,1,0:T(8,128)}, u32[]{:S(2)}) copy-start(f32[3,16,64,128]{3,2,1,0:T(8,128)} %param.31) | copy-start | bytes 4718596
  31.6 41.2 %copy-start.3 = (bf16[3,3,1024]{2,1,0:T(4,128)(2,1)S(1)}, bf16[3,3,1024]{2,1,0:T(4,128)(2,1)}, u32[]{:S(2)}) copy-start(bf16[3,3,1024]{2,1,0:T(4,128)(2,1)} %hist_ref.3) | copy-start | bytes 55300
  31.6 41.2 %copy-start.4 = (f32[4,1024]{1,0:T(4,128)S(1)}, f32[4,1024]{1,0:T(4,128)}, u32[]{:S(2)}) copy-start(f32[4,1024]{1,0:T(4,128)} %taps_ref.3) | copy-start | bytes 49156
  31.6 41.1 %copy-start.6 = (f32[1024]{0:T(1024)S(1)}, f32[1024]{0:T(1024)}, u32[]{:S(2)}) copy-start(f32[1024]{0:T(1024)} %param.23) | copy-start | bytes 12292
  31.6 41.1 %copy-start.11 = (f32[16]{0:T(128)S(1)}, f32[16]{0:T(128)}, u32[]{:S(2)}) copy-start(f32[16]{0:T(128)} %param.26) | copy-start | bytes 196
  31.6 41.1 %copy-start.12 = (f32[16]{0:T(128)S(1)}, f32[16]{0:T(128)}, u32[]{:S(2)}) copy-start(f32[16]{0:T(128)} %param.27) | copy-start | bytes 196
  31.6 41.1 %copy-start.13 = (f32[16]{0:T(128)S(1)}, f32[16]{0:T(128)}, u32[]{:S(2)}) copy-start(f32[16]{0:T(128)} %param.28) | copy-start | bytes 196
  65.8 11.4 %copy-start.7 = (f32[1024]{0:T(1024)S(1)}, f32[1024]{0:T(1024)}, u32[]{:S(2)}) copy-start(f32[1024]{0:T(1024)} %param.29) | copy-start | bytes 12292
  66.6 28.3 %copy-start.2 = (bf16[1024,256]{1,0:T(8,128)(2,1)S(1)}, bf16[1024,256]{1,0:T(8,128)(2,1)}, u32[]{:S(2)}) copy-start(bf16[1024,256]{1,0:T(8,128)(2,1)} %own_ref.1) | copy-start | bytes 1572868

commit v9 on v8

--- a/solution.py
+++ b/solution.py
@@ -317,6 +317,12 @@
 
     lanes = bc_weight.shape[1]
     chunk = width // SHARE
+    with jax.named_scope("gather_tokens"):
+        own = call(
+            copy_tokens,
+            sds((SHARE * Y_SIZE, rows_head * steps, features), BF16),
+            [pltpu.VMEM((rows_head * steps, features), F32)],
+        )(jnp.transpose(tokens, (1, 0, 2)))
     with jax.named_scope("move_weights"):
         here = lax.axis_index(SHARE_AXIS)
         own_part = lax.dynamic_slice(
@@ -324,8 +330,9 @@
             (0, 0, here * chunk),
             (features, 2, chunk),
         )
+        ahead, own = lax.optimization_barrier((gate_inner_weight, own))
         other_part = lax.dynamic_slice(
-            gate_inner_weight, (0, 0, (1 - here) * chunk), (features, 2, chunk)
+            ahead, (0, 0, (1 - here) * chunk), (features, 2, chunk)
         )
         other_part = lax.ppermute(other_part, SHARE_AXIS, [(0, 1), (1, 0)])
         chunks = [part.reshape(features, 2 * chunk) for part in (own_part, other_part)]
@@ -338,11 +345,6 @@
         other_weight = lax.ppermute(out_weight, PAIR_AXIS, [(0, 1), (1, 0)])
 
     with jax.named_scope("gather_tokens"):
-        own = call(
-            copy_tokens,
-            sds((SHARE * Y_SIZE, rows_head * steps, features), BF16),
-            [pltpu.VMEM((rows_head * steps, features), F32)],
-        )(jnp.transpose(tokens, (1, 0, 2)))
         gathered = lax.all_to_all(own, (SHARE_AXIS, "y"), 0, 0, tiled=True)
         gathered = lax.all_gather(gathered, "core", axis=0, tiled=False)
 

time: 114 us -> 113 us (level)
  transfers between devices with their start and end apart: 3 -> 3, of which waited for: 1 -> 1; matrix products, arithmetic and copies ran while one was open for 1% -> 1% of each run, Pallas kernels for 1% -> 0%
where the time goes in v9:
time: 113 us
  blocking collectives  81.8 us (72%)
  starting transfers between devices  14.9 us (13%)
  Pallas kernels  6.2 us (5%)
  waiting for transfers between devices  5.84 us (5%)
  local copies, waits for them, and re-layouts  2.91 us (3%)
    all_to_all x1, blocking collectives, shards(): lax.all_to_all(messages.reshape(req_count, lines, lanes), REQ_AXES, 0, 0,...  34.1 us
    all_to_all x1, blocking collectives, shards(): some_rows = lax.all_to_all(normed, REST_AXES, 0, 0, tiled=True)  17.5 us
    all_to_all x1, blocking collectives, shards(): blocks = lax.all_to_all(blocks, HEAD_AXES + (PAIR_AXIS,), 0, 0, tiled=True)  17.5 us
    all_to_all x1, starting transfers between devices, shards(): gathered = lax.all_to_all(own, (SHARE_AXIS, 'y'), 0, 0, tiled=True)  6.94 us
    all_gather x1, blocking collectives, shards(): pair = lax.all_gather(bc_conv, 'core', axis=0, tiled=False)  6.21 us
    all_to_all x1, waiting for transfers between devices, shards(): gathered = lax.all_to_all(own, (SHARE_AXIS, 'y'), 0, 0, tiled=True)  5.83 us
    all_gather x1, blocking collectives, shards(): gathered = lax.all_gather(gathered, 'core', axis=0, tiled=False)  4.66 us
    ppermute x1, starting transfers between devices, shards(): other_weight = lax.ppermute(out_weight, PAIR_AXIS, [(0, 1), (1, 0)])  4 us
  transfers between devices with their start and end apart: 3, of which 1 were waited for; matrix products, arithmetic and copies ran while one was open for 1% of the time, Pallas kernels for 0%

profile of v9, /device:TPU:1, one launch (start us, length us, event | category | flops | bytes accessed | tf_op | source)
XLA Modules:
  0.0 112.5 jit_solution(9721781500056686466)
XLA Ops:
  0.7 0.8 copy-done.5
  1.5 0.7 gather_tokens.1
  2.2 0.4 constant_dynamic-slice_fusion
  2.5 3.9 %collective-permute-start = (bf16[256,2,512]{2,1,0:T(2,128)(2,1)S(1)}, bf16[256,2,512]{2,1,0:T(2,128)(2,1)S(1)}, u32[]{:S(2)}, u32[]{:S(2)}) collective-permute-start(bf16[256,2,512]{2,1,0:T(2,128)(2,1)S(1)} %constant_dynamic-slice_fusion), channel_id=1, source_target_pairs={{0,8},{8,0},{1,9},{9,1},{2,10},{10,2},{3,11},{11,3},{4,12},{12,4},... | collective-permute-start | bytes 1572872 | tf_op jit(solution)/shard_map/move_weights/ppermute | solution.py:337
  6.5 4.0 %collective-permute-start.1 = (bf16[1024,256]{1,0:T(8,128)(2,1)}, bf16[1024,256]{1,0:T(8,128)(2,1)S(1)}, u32[]{:S(2)}, u32[]{:S(2)}) collective-permute-start(bf16[1024,256]{1,0:T(8,128)(2,1)} %own_ref.1), channel_id=1, source_target_pairs={{0,1},{1,0},{2,3},{3,2},{4,5},{5,4},{6,7},{7,6},{8,9},{9,8},{10,11... | collective-permute-start | bytes 1572872 | tf_op jit(solution)/shard_map/move_out_weight/ppermute | solution.py:345
  10.5 6.9 %all-to-all-start = ((bf16[16,24,256]{2,1,0:T(8,128)(2,1)}), bf16[16,24,256]{2,1,0:T(8,128)(2,1)S(1)}, u32[]{:S(2)}, u32[]{:S(2)}) async-start(bf16[16,24,256]{2,1,0:T(8,128)(2,1)} %gather_tokens.1), calls=%async_computation | async-start | bytes 393216 | tf_op jit(solution)/shard_map/gather_tokens/all_to_all | solution.py:348
  17.4 0.1 copy.28
  17.6 0.4 constant_dynamic-slice_fusion.1
  17.9 0.1 copy.36
  18.0 1.1 concatenate.3.extra_ref
  19.1 5.8 %all-to-all-done = bf16[16,24,256]{2,1,0:T(8,128)(2,1)S(1)} async-done(((bf16[16,24,256]{2,1,0:T(8,128)(2,1)}), bf16[16,24,256]{2,1,0:T(8,128)(2,1)S(1)}, u32[]{:S(2)}, u32[]{:S(2)}) %all-to-all-start) | async-done | bytes 196640 | tf_op jit(solution)/shard_map/gather_tokens/all_to_all | solution.py:348
  24.9 4.7 %all-gather = bf16[32,24,256]{2,1,0:T(8,128)(2,1)S(1)} all-gather(bf16[16,24,256]{2,1,0:T(8,128)(2,1)S(1)} %all-to-all-done), channel_id=2, replica_groups=mesh['y'=8,'core'=2,'x1'=2,'x0'=2,'z2'=2,'z1'=2,'z0'=2] {'core'}, dimensions={0}, use_global_device_ids=true | all-gather | bytes 589824 | tf_op jit(solution)/shard_map/gather_tokens/all_gather | solution.py:349
  29.6 0.1 copy.37
  29.7 0.8 project.1
  30.6 34.1 %all_to_all.20.in_ref = bf16[32,112,128]{2,1,0:T(8,128)(2,1)S(1)} all-to-all(bf16[32,112,128]{2,1,0:T(8,128)(2,1)S(1)} %bitcast.21), channel_id=1, replica_groups=mesh['y'=8,'core'=2,'x1'=2,'x0'=2,'z2'=2,'z1'=2,'z0'=2] {'x1','x0','z2',..., dimensions={0} | all-to-all | bytes 1835008 | tf_op jit(solution)/shard_map/sum_req/all_to_all | solution.py:362
  64.7 0.7 sum_req.1
  65.4 6.2 %all-gather.3.pair_ref = f32[2,12,128]{2,1,0:T(8,128)S(1)} all-gather(f32[1,12,128]{2,1,0:T(8,128)S(1)} %bitcast.29), channel_id=3, replica_groups=mesh['y'=8,'core'=2,'x1'=2,'x0'=2,'z2'=2,'z1'=2,'z0'=2] {'core'}, dimensions={0}, use_global_device_ids=true | all-gather | bytes 18432 | tf_op jit(solution)/shard_map/scan/all_gather | solution.py:377
  71.7 2.6 %scan.1 = (f32[12,1024]{1,0:T(8,128)S(1)}, f32[12,128]{1,0:T(8,128)S(1)}, f32[3,1024,128]{2,1,0:T(8,128)}, bf16[3,3,1024]{2,1,0:T(4,128)(2,1)}) custom-call(f32[12,1024]{1,0:T(8,128)S(1)} %get-tuple-element.17.gate_ref, f32[12,1024]{1,0:T(8,128)S(1)} %get-tuple-element.18.inner_ref, f32[12,16]{1,0:T(8,128)S(1)} %get-tuple-element.19.step_ref, ...), custom_call_target="tpu_custom_call" | custom-call | tf_op jit(solution)/shard_map/scan/pallas_call | solution.py:378
  74.3 1.8 %all-gather.4.squares_ref = f32[2,12,128]{2,1,0:T(8,128)S(1)} all-gather(f32[1,12,128]{2,1,0:T(8,128)S(1)} %bitcast.28), channel_id=4, replica_groups=mesh['y'=8,'core'=2,'x1'=2,'x0'=2,'z2'=2,'z1'=2,'z0'=2] {'core'}, dimensions={0}, use_global_device_ids=true | all-gather | bytes 18432 | tf_op jit(solution)/shard_map/normalise/all_gather | solution.py:406
  76.1 0.1 normalise.1
  76.2 17.5 %all_to_all.21.in_ref = bf16[16,24,512]{2,1,0:T(8,128)(2,1)S(1)} all-to-all(bf16[16,24,512]{2,1,0:T(8,128)(2,1)S(1)} %normalise.1), channel_id=1, replica_groups=mesh['y'=8,'core'=2,'x1'=2,'x0'=2,'z2'=2,'z1'=2,'z0'=2] {'x1','x0','z2',..., dimensions={0} | all-to-all | bytes 786432 | tf_op jit(solution)/shard_map/gather_normed/all_to_all | solution.py:413
  93.7 0.7 project_out.1
  94.4 17.5 %all_to_all.22.in_ref = bf16[32,24,128]{2,1,0:T(8,128)(2,1)S(1)} all-to-all(bf16[32,24,128]{2,1,0:T(8,128)(2,1)S(1)} %bitcast.26), channel_id=1, replica_groups=mesh['y'=8,'core'=2,'x1'=2,'x0'=2,'z2'=2,'z1'=2,'z0'=2] {'y','core','z0'}, dimensions={0} | all-to-all | bytes 393216 | tf_op jit(solution)/shard_map/sum_head/all_to_all | solution.py:429
  111.9 0.6 sum_head.1
  (31 shorter events, 0.1 us)
Async XLA Ops:
  0.6 1.5 %copy-start = (bf16[256,2,1024]{2,1,0:T(2,128)(2,1)S(1)}, bf16[256,2,1024]{2,1,0:T(2,128)(2,1)}, u32[]{:S(2)}) copy-start(bf16[256,2,1024]{2,1,0:T(2,128)(2,1)} %param.17) | copy-start | bytes 3145732
  0.6 16.8 %copy-start.14 = (bf16[256,16]{0,1:T(8,128)(2,1)S(1)}, bf16[256,16]{0,1:T(8,128)(2,1)}, u32[]{:S(2)}) copy-start(bf16[256,16]{0,1:T(8,128)(2,1)} %param.18) | copy-start | bytes 24580
  0.7 0.8 copy-start.5
  2.5 27.1 %collective-permute-start = (bf16[256,2,512]{2,1,0:T(2,128)(2,1)S(1)}, bf16[256,2,512]{2,1,0:T(2,128)(2,1)S(1)}, u32[]{:S(2)}, u32[]{:S(2)}) collective-permute-start(bf16[256,2,512]{2,1,0:T(2,128)(2,1)S(1)} %constant_dynamic-slice_fusion), channel_id=1, source_target_pairs={{0,8},{8,0},{1,9},{9,1},{2,10},{10,2},{3,11},{11,3},{4,12},{12,4},... | collective-permute-start | bytes 1572872 | tf_op jit(solution)/shard_map/move_weights/ppermute | solution.py:337
  6.5 23.2 %collective-permute-start.1 = (bf16[1024,256]{1,0:T(8,128)(2,1)}, bf16[1024,256]{1,0:T(8,128)(2,1)S(1)}, u32[]{:S(2)}, u32[]{:S(2)}) collective-permute-start(bf16[1024,256]{1,0:T(8,128)(2,1)} %own_ref.1), channel_id=1, source_target_pairs={{0,1},{1,0},{2,3},{3,2},{4,5},{5,4},{6,7},{7,6},{8,9},{9,8},{10,11... | collective-permute-start | bytes 1572872 | tf_op jit(solution)/shard_map/move_out_weight/ppermute | solution.py:345
  10.5 14.4 %all-to-all-start = ((bf16[16,24,256]{2,1,0:T(8,128)(2,1)}), bf16[16,24,256]{2,1,0:T(8,128)(2,1)S(1)}, u32[]{:S(2)}, u32[]{:S(2)}) async-start(bf16[16,24,256]{2,1,0:T(8,128)(2,1)} %gather_tokens.1), calls=%async_computation | async-start | bytes 393216 | tf_op jit(solution)/shard_map/gather_tokens/all_to_all | solution.py:348
  30.4 34.3 %copy-start.8 = (bf16[3,3,128]{2,1,0:T(4,128)(2,1)S(1)}, bf16[3,3,128]{2,1,0:T(4,128)(2,1)}, u32[]{:S(2)}) copy-start(bf16[3,3,128]{2,1,0:T(4,128)(2,1)} %hist_ref.2) | copy-start | bytes 6916
  30.5 34.2 %copy-start.9 = (f32[4,128]{1,0:T(4,128)S(1)}, f32[4,128]{1,0:T(4,128)}, u32[]{:S(2)}) copy-start(f32[4,128]{1,0:T(4,128)} %taps_ref.2) | copy-start | bytes 6148
  30.5 34.2 %copy-start.10 = (f32[128]{0:T(128)S(1)}, f32[128]{0:T(128)}, u32[]{:S(2)}) copy-start(f32[128]{0:T(128)} %param.25) | copy-start | bytes 1540
  30.5 41.2 %copy-start.1 = (f32[3,16,64,128]{3,2,1,0:T(8,128)S(1)}, f32[3,16,64,128]{3,2,1,0:T(8,128)}, u32[]{:S(2)}) copy-start(f32[3,16,64,128]{3,2,1,0:T(8,128)} %param.31) | copy-start | bytes 4718596
  30.5 41.2 %copy-start.3 = (bf16[3,3,1024]{2,1,0:T(4,128)(2,1)S(1)}, bf16[3,3,1024]{2,1,0:T(4,128)(2,1)}, u32[]{:S(2)}) copy-start(bf16[3,3,1024]{2,1,0:T(4,128)(2,1)} %hist_ref.3) | copy-start | bytes 55300
  30.5 41.2 %copy-start.4 = (f32[4,1024]{1,0:T(4,128)S(1)}, f32[4,1024]{1,0:T(4,128)}, u32[]{:S(2)}) copy-start(f32[4,1024]{1,0:T(4,128)} %taps_ref.3) | copy-start | bytes 49156
  30.5 41.1 %copy-start.6 = (f32[1024]{0:T(1024)S(1)}, f32[1024]{0:T(1024)}, u32[]{:S(2)}) copy-start(f32[1024]{0:T(1024)} %param.23) | copy-start | bytes 12292
  30.5 41.1 %copy-start.11 = (f32[16]{0:T(128)S(1)}, f32[16]{0:T(128)}, u32[]{:S(2)}) copy-start(f32[16]{0:T(128)} %param.26) | copy-start | bytes 196
  30.5 41.1 %copy-start.12 = (f32[16]{0:T(128)S(1)}, f32[16]{0:T(128)}, u32[]{:S(2)}) copy-start(f32[16]{0:T(128)} %param.27) | copy-start | bytes 196
  30.6 41.1 %copy-start.13 = (f32[16]{0:T(128)S(1)}, f32[16]{0:T(128)}, u32[]{:S(2)}) copy-start(f32[16]{0:T(128)} %param.28) | copy-start | bytes 196
  64.7 11.4 %copy-start.7 = (f32[1024]{0:T(1024)S(1)}, f32[1024]{0:T(1024)}, u32[]{:S(2)}) copy-start(f32[1024]{0:T(1024)} %param.29) | copy-start | bytes 12292
  65.4 28.3 %copy-start.2 = (bf16[1024,256]{1,0:T(8,128)(2,1)S(1)}, bf16[1024,256]{1,0:T(8,128)(2,1)}, u32[]{:S(2)}) copy-start(bf16[1024,256]{1,0:T(8,128)(2,1)} %own_ref.1) | copy-start | bytes 1572868
